TPU v7x, 256 devices: a whole 4x4x8 slice. The times are simulated.
256 devices in a mesh: seq: 64 (over y, z, core), head: 4 (over x).
Axes of the slice: x: 4, y: 4, z: 8, core: 2. Of those that a mesh axis runs over, the one named last changes fastest.
Arguments:
- queries: bfloat16 [16384, 4096], P('seq', 'head'), may hold values from -6 to 6
- keys: bfloat16 [16384, 4096], P('seq', 'head'), may hold values from -6 to 6
- values: bfloat16 [16384, 4096], P('seq', 'head'), may hold values from -6 to 6
- gating: int32 [512, 3], P('seq'), may hold values from 0 to 63, as said below
Outputs:
- attended: bfloat16 [16384, 4096], P('seq', 'head')
- gate_scores: float32 [16384, 64], P('seq')
Inputs may be any that keep to these rules, and one draw needn't show every extreme that they name: `gating`: an entry of a tile in block b is b itself (no further block) or an earlier block; among all tiles of one block no earlier block is named twice; every block b >= 1 names block 0 and block b - 1 in some of its tiles.
All inputs are finite; a program needn't handle non-finite values.
Results may differ from a plain program's by a relative error of at most 0.0048.
Values may be sent and summed in bfloat16 or wider, within the bound.
No kernel may reach another device: no remote copies, remote signals or barrier semaphores. Data moves between devices by JAX's collectives and lax.ppermute only.
A program may use at most 64 MiB of HBM per device.

v0:
```python
import math

import jax
import jax.numpy as jnp
from jax import lax
from jax.sharding import PartitionSpec as P

HEADS = 32
HD = 128
QT = 32
TOPK = 3


def attend(query, key_block, value_block, start):
    scores = jnp.einsum(
        "qhd,khd->hqk", query, key_block, preferred_element_type=jnp.float32
    ) * query.shape[2] ** (-0.5)
    if start is not None:
        places = start + jnp.arange(query.shape[0])
        scores = jnp.where(
            jnp.arange(key_block.shape[0])[None, None, :] <= places[None, :, None], scores, -jnp.inf
        )
    top = jnp.max(scores, axis=2, keepdims=True)
    weights = jnp.exp(scores - top)
    total = jnp.sum(weights, axis=2, keepdims=True)
    mixed = jnp.einsum(
        "hqk,khd->qhd",
        weights.astype(jnp.bfloat16),
        value_block,
        preferred_element_type=jnp.float32,
    )
    mixed = mixed / jnp.transpose(total, (1, 0, 2))
    spread = jnp.transpose(top + jnp.log(total), (1, 0, 2))[:, :, 0]
    return (mixed, spread)


def sweep(query_rows, key_block, value_block):
    rows = query_rows.shape[0]
    block = math.gcd(rows, 512)
    count = rows // block

    def step_rows(index):
        begin = index * block
        return attend(query_rows, key_block, value_block, begin)

    mixed, spread = lax.map(step_rows, jnp.arange(count))
    return (
        mixed.reshape(rows, query_rows.shape[1], query_rows.shape[2]),
        spread.reshape(rows, query_rows.shape[1]),
    )


def body(queries, keys, values, gating):
    rows, width = queries.shape
    heads = width // HD
    nblk = lax.axis_size("seq")
    owner = lax.axis_index("seq")
    tiles = rows // QT
    query_3d = queries.reshape(rows, heads, HD)
    key_3d = keys.reshape(rows, heads, HD)
    value_3d = values.reshape(rows, heads, HD)
    local_mean = jnp.sum(keys, axis=0, dtype=jnp.float32) / rows
    every_mean = lax.all_gather(local_mean.reshape(1, width), "seq", axis=0, tiled=True)
    share = jnp.einsum(
        "thd,jhd->tj",
        query_3d.astype(jnp.float32),
        every_mean.reshape(nblk, heads, HD),
        precision=lax.Precision.HIGHEST,
    )
    gate_total = lax.psum(share, "head")
    gate_scores = jnp.where(jnp.arange(nblk)[None, :] < owner, gate_total / HEADS, 0.0)
    slots = jnp.arange(nblk)
    hits = (gating[None, :, :] == slots[:, None, None]) & (gating[None, :, :] != owner)
    picked = jnp.any(hits, axis=2)
    tile_rows = queries.reshape(tiles, QT * width)
    outgoing = jnp.dot(picked.astype(jnp.bfloat16), tile_rows, preferred_element_type=jnp.float32)
    outgoing = outgoing.astype(jnp.bfloat16).reshape(nblk, QT, width)
    piece = lax.all_to_all(outgoing, "seq", split_axis=0, concat_axis=0, tiled=True)
    count = piece.shape[1]
    group = math.gcd(nblk, max(1, 512 // count))
    flat = piece.reshape(nblk // group, group * count, heads, HD)
    mixed, spread = lax.map(lambda block_q: attend(block_q, key_3d, value_3d, None), flat)
    mixed = mixed.reshape(nblk, count, width).astype(jnp.bfloat16)
    spread = spread.reshape(nblk, count, heads)
    mixed, spread = (mixed, spread)
    back_out = lax.all_to_all(mixed, "seq", split_axis=0, concat_axis=0, tiled=True)
    back_lse = lax.all_to_all(spread, "seq", split_axis=0, concat_axis=0, tiled=True)
    back_out, back_lse = (back_out, back_lse)
    back_flat = back_out.reshape(nblk, QT * width)
    lse_flat = back_lse.reshape(nblk, QT * heads)
    own_out, own_lse = sweep(query_3d, key_3d, value_3d)
    outs = [own_out]
    lses = [own_lse]
    for slot in range(TOPK):
        selected = jnp.transpose(hits[:, :, slot])
        part_out = jnp.dot(
            selected.astype(jnp.bfloat16), back_flat, preferred_element_type=jnp.float32
        ).reshape(rows, heads, HD)
        part_lse = jnp.dot(
            selected.astype(jnp.float32), lse_flat, precision=lax.Precision.HIGHEST
        ).reshape(rows, heads)
        live = jnp.repeat(jnp.any(selected, axis=1), QT)
        part_lse = jnp.where(live[:, None], part_lse, -jnp.inf)
        outs.append(part_out)
        lses.append(part_lse)
    lse_all = jnp.stack(lses)
    out_all = jnp.stack(outs)
    peak = jnp.max(lse_all, axis=0)
    scale = jnp.exp(lse_all - peak[None])
    final = jnp.sum(scale[..., None] * out_all, axis=0) / jnp.sum(scale, axis=0)[..., None]
    return (final.reshape(rows, width).astype(jnp.bfloat16), gate_scores)


def solution(mesh):
    return jax.shard_map(
        body,
        mesh=mesh,
        in_specs=(P("seq", "head"), P("seq", "head"), P("seq", "head"), P("seq", None)),
        out_specs=(P("seq", "head"), P("seq", None)),
        check_vma=False,
    )
```

profile of v0, /device:TPU:8, one launch (start us, length us, event | category | flops | bytes accessed | tf_op | source)
XLA Modules:
  0.0 402.4 jit_solution(3500703471987267630)
XLA Ops:
  9.9 1.3 convolution_convert_fusion
  11.2 4.4 %copy.103 = bf16[8,8,32,1024]{3,2,1,0:T(8,128)(2,1)} copy(bf16[8,8,32,1024]{3,1,2,0:T(8,128)(2,1)S(1)} %bitcast.155) | data formatting | bytes 8388608
  15.6 12.4 %all-to-all-start = ((bf16[64,32,1024]{2,1,0:T(8,128)(2,1)}), bf16[64,32,1024]{2,1,0:T(8,128)(2,1)}, u32[]{:S(2)}, u32[]{:S(2)}) async-start(bf16[64,32,1024]{2,1,0:T(8,128)(2,1)} %bitcast.156), calls=%async_computation | async-start | bytes 8388608 | tf_op jit(solution)/shard_map/all_to_all | solution.py:78
  29.0 93.9 %all-to-all-done = bf16[64,32,1024]{2,1,0:T(8,128)(2,1)} async-done(((bf16[64,32,1024]{2,1,0:T(8,128)(2,1)}), bf16[64,32,1024]{2,1,0:T(8,128)(2,1)}, u32[]{:S(2)}, u32[]{:S(2)}) %all-to-all-start) | async-done | bytes 4194336 | tf_op jit(solution)/shard_map/all_to_all | solution.py:78
  122.9 5.2 %copy.104 = bf16[256,8,8,128]{3,2,1,0:T(8,128)(2,1)} copy(bf16[256,8,8,128]{3,1,2,0:T(8,128)(2,1)} %bitcast.41) | data formatting | bytes 8388608
  128.1 38.0 %while.2 = (s32[]{:T(128)}, bf16[4,512,8,128]{3,1,2,0:T(8,128)(2,1)}, f32[4,512,8]{1,0,2:T(4,128)S(1)}, bf16[4,512,8,128]{3,2,1,0:T(8,128)(2,1)}, bf16[256,8,128...) while((s32[]{:T(128)}, bf16[4,512,8,128]{3,1,2,0:T(8,128)(2,1)}, ...), condition=%wide.region_7.8_spmd, body=%wide.region_4.7_spmd.sunk | while | flops 545779712 | bytes 35848824 | solution.py:82
  128.1 1.3 constant_dynamic-slice_fusion.2
  130.1 2.0 copy-done
  133.0 4.6 %bitcast_dynamic-update-slice_fusion.2 = bf16[4,512,8,128]{3,1,2,0:T(8,128)(2,1)} fusion(bf16[4,512,8,128]{3,1,2,0:T(8,128)(2,1)} %get-tuple-element.148, s32[]{:T(128)} %get-tuple-element.147, bf16[256,8,128]{2,0,1:T(8,128)(2,1)S(1)} %get-tuple-element.160, f32[8,512,256]{1,2,0:T(8,128)} %copy-done, f32[8,512]{1,0:T(8,128)S(1)} %get-tuple-element.138, ...), kind=kOutput, calls=%fused_computation.5.clone.1 | convolution fusion | flops 272105472 | bytes 6849024 | tf_op jit(solution)/shard_map/while/body/eval_jaxpr/hqk,khd->qhd/dot_general | solution.py:26
  137.6 1.3 constant_dynamic-slice_fusion.2
  139.6 2.0 copy-done
  142.4 4.6 %bitcast_dynamic-update-slice_fusion.2 = bf16[4,512,8,128]{3,1,2,0:T(8,128)(2,1)} fusion(bf16[4,512,8,128]{3,1,2,0:T(8,128)(2,1)} %get-tuple-element.148, s32[]{:T(128)} %get-tuple-element.147, bf16[256,8,128]{2,0,1:T(8,128)(2,1)S(1)} %get-tuple-element.160, f32[8,512,256]{1,2,0:T(8,128)} %copy-done, f32[8,512]{1,0:T(8,128)S(1)} %get-tuple-element.138, ...), kind=kOutput, calls=%fused_computation.5.clone.1 | convolution fusion | flops 272105472 | bytes 6849024 | tf_op jit(solution)/shard_map/while/body/eval_jaxpr/hqk,khd->qhd/dot_general | solution.py:26
  147.1 1.3 constant_dynamic-slice_fusion.2
  149.1 2.0 copy-done
  152.0 4.6 %bitcast_dynamic-update-slice_fusion.2 = bf16[4,512,8,128]{3,1,2,0:T(8,128)(2,1)} fusion(bf16[4,512,8,128]{3,1,2,0:T(8,128)(2,1)} %get-tuple-element.148, s32[]{:T(128)} %get-tuple-element.147, bf16[256,8,128]{2,0,1:T(8,128)(2,1)S(1)} %get-tuple-element.160, f32[8,512,256]{1,2,0:T(8,128)} %copy-done, f32[8,512]{1,0:T(8,128)S(1)} %get-tuple-element.138, ...), kind=kOutput, calls=%fused_computation.5.clone.1 | convolution fusion | flops 272105472 | bytes 6849024 | tf_op jit(solution)/shard_map/while/body/eval_jaxpr/hqk,khd->qhd/dot_general | solution.py:26
  156.6 1.3 constant_dynamic-slice_fusion.2
  158.6 2.0 copy-done
  161.5 4.6 %bitcast_dynamic-update-slice_fusion.2 = bf16[4,512,8,128]{3,1,2,0:T(8,128)(2,1)} fusion(bf16[4,512,8,128]{3,1,2,0:T(8,128)(2,1)} %get-tuple-element.148, s32[]{:T(128)} %get-tuple-element.147, bf16[256,8,128]{2,0,1:T(8,128)(2,1)S(1)} %get-tuple-element.160, f32[8,512,256]{1,2,0:T(8,128)} %copy-done, f32[8,512]{1,0:T(8,128)S(1)} %get-tuple-element.138, ...), kind=kOutput, calls=%fused_computation.5.clone.1 | convolution fusion | flops 272105472 | bytes 6849024 | tf_op jit(solution)/shard_map/while/body/eval_jaxpr/hqk,khd->qhd/dot_general | solution.py:26
  167.2 6.8 %all-to-all-start.1 = ((f32[64,1,256]{2,1,0:T(1,128)}), f32[64,1,256]{2,1,0:T(1,128)S(1)}, u32[]{:S(2)}, u32[]{:S(2)}) async-start(f32[64,1,256]{2,1,0:T(1,128)} %reshape.359), calls=%async_computation.1 | async-start | bytes 131072 | tf_op jit(solution)/shard_map/all_to_all | solution.py:87
  174.0 6.9 %copy.83 = bf16[4,512,8,128]{3,2,1,0:T(8,128)(2,1)} copy(bf16[4,512,8,128]{3,1,2,0:T(8,128)(2,1)} %get-tuple-element.54) | data formatting | bytes 8388608 | tf_op jit(solution)/shard_map/convert_element_type | solution.py:83
  180.8 7.3 %convert_element_type.36 = bf16[64,32,1024]{2,1,0:T(8,128)(2,1)} reshape(bf16[4,512,8,128]{3,2,1,0:T(8,128)(2,1)} %copy.83) | data formatting | bytes 8388608 | tf_op jit(solution)/shard_map/convert_element_type | solution.py:83
  188.1 10.6 %all-to-all-start.2 = ((bf16[64,32,1024]{2,1,0:T(8,128)(2,1)}), bf16[64,32,1024]{2,1,0:T(8,128)(2,1)}, u32[]{:S(2)}, u32[]{:S(2)}) async-start(bf16[64,32,1024]{2,1,0:T(8,128)(2,1)} %convert_element_type.36), calls=%async_computation.2 | async-start | bytes 8388608 | tf_op jit(solution)/shard_map/all_to_all | solution.py:86
  198.9 128.0 %all-gather = f32[65536]{0:T(1024)S(1)} all-gather(f32[1024]{0:T(1024)S(1)} %broadcast_multiply_fusion), channel_id=2, replica_groups=mesh['seq'=64,'head'=4] {'seq'}, dimensions={0}, use_global_device_ids=true | all-gather | bytes 266240 | tf_op jit(solution)/shard_map/all_gather | solution.py:63
  329.9 2.0 fusion.16
  331.9 41.6 %all-reduce.2.cloned.1.call-done = f32[256,64]{0,1:T(8,128)} async-done(((f32[256,64]{0,1:T(8,128)}), f32[256,64]{0,1:T(8,128)}) %all-reduce.2.cloned.1.call-update) | async-done | bytes 65552 | tf_op jit(solution)/shard_map/psum | solution.py:70
  373.5 1.5 multiply_select_fusion.1
  378.7 4.7 %copy.105 = bf16[8,8,32,1024]{3,1,2,0:T(8,128)(2,1)S(1)} copy(bf16[8,8,32,1024]{3,2,1,0:T(8,128)(2,1)} %bitcast.46) | data formatting | bytes 8388608
  384.0 1.7 fusion.42
  385.7 1.6 fusion.39
  387.7 1.4 stack_reshape.10
  389.3 1.4 stack_reshape.11
  390.9 3.1 fusion.11
  (93 shorter events, 20.6 us)
Async XLA Ops:
  15.6 12.5 %copy-start.2 = (bf16[256,1024]{1,0:T(8,128)(2,1)S(1)}, bf16[256,1024]{1,0:T(8,128)(2,1)}, u32[]{:S(2)}) copy-start(bf16[256,1024]{1,0:T(8,128)(2,1)} %param.7) | copy-start | bytes 1572868
  15.6 13.0 %copy-start.3 = (bf16[256,1024]{1,0:T(8,128)(2,1)S(1)}, bf16[256,1024]{1,0:T(8,128)(2,1)}, u32[]{:S(2)}) copy-start(bf16[256,1024]{1,0:T(8,128)(2,1)} %param.8) | copy-start | bytes 1572868
  15.6 107.3 %all-to-all-start = ((bf16[64,32,1024]{2,1,0:T(8,128)(2,1)}), bf16[64,32,1024]{2,1,0:T(8,128)(2,1)}, u32[]{:S(2)}, u32[]{:S(2)}) async-start(bf16[64,32,1024]{2,1,0:T(8,128)(2,1)} %bitcast.156), calls=%async_computation | async-start | bytes 8388608 | tf_op jit(solution)/shard_map/all_to_all | solution.py:78
  130.1 2.0 copy-start
  139.6 2.0 copy-start
  149.1 2.0 copy-start
  158.6 2.0 copy-start
  167.2 21.0 %all-to-all-start.1 = ((f32[64,1,256]{2,1,0:T(1,128)}), f32[64,1,256]{2,1,0:T(1,128)S(1)}, u32[]{:S(2)}, u32[]{:S(2)}) async-start(f32[64,1,256]{2,1,0:T(1,128)} %reshape.359), calls=%async_computation.1 | async-start | bytes 131072 | tf_op jit(solution)/shard_map/all_to_all | solution.py:87
  188.1 138.8 %copy-start.1 = (bf16[256,1024]{1,0:T(8,128)(2,1)S(1)}, bf16[256,1024]{1,0:T(8,128)(2,1)}, u32[]{:S(2)}) copy-start(bf16[256,1024]{1,0:T(8,128)(2,1)} %param.6) | copy-start | bytes 1572868
  188.1 190.5 %all-to-all-start.2 = ((bf16[64,32,1024]{2,1,0:T(8,128)(2,1)}), bf16[64,32,1024]{2,1,0:T(8,128)(2,1)}, u32[]{:S(2)}, u32[]{:S(2)}) async-start(bf16[64,32,1024]{2,1,0:T(8,128)(2,1)} %convert_element_type.36), calls=%async_computation.2 | async-start | bytes 8388608 | tf_op jit(solution)/shard_map/all_to_all | solution.py:86
  198.8 174.7 %all-reduce.2.cloned.1.call-start = ((), (), s32[]{:S(2)}) async-start(), calls=%async_computation.3 | async-start | bytes 131072 | tf_op jit(solution)/shard_map/psum | solution.py:70
Sparse Core Ops, SparseCore 0:
  328.3 45.1 all-reduce.1
where the time goes:
time: 404 us; the launch traced here: 402 us
  waiting for transfers between devices  135 us (33%)
  blocking collectives  128 us (32%)
  local copies, waits for them, and re-layouts  52.3 us (13%)
  matrix products  30.9 us (8%)
  starting transfers between devices  29.9 us (7%)
  between operations  14.4 us (4%)
  other arithmetic  11.2 us (3%)
    all_gather x1, blocking collectives, body(): lax.all_gather(local_mean.reshape(1, width), 'seq', axis=0, tiled=True)  128 us
    all_to_all x1, waiting for transfers between devices, body(): lax.all_to_all(outgoing, 'seq', split_axis=0, concat_axis=0, tiled=True)  93.9 us
    psum x1, waiting for transfers between devices, body(): gate_total = lax.psum(share, 'head')  41.6 us
    dot_general x5, matrix products, attend(): jnp.einsum('hqk,khd->qhd', weights.astype(jnp.bfloat16), value_block, pre...  20.5 us
    unnamed x14, local copies, waits for them, and re-layouts  16.6 us
    convert_element_type x2, local copies, waits for them, and re-layouts, body(): mixed = mixed.reshape(nblk, count, width).astype(jnp.bfloat16)  14.2 us
    all_to_all x1, starting transfers between devices, body(): lax.all_to_all(outgoing, 'seq', split_axis=0, concat_axis=0, tiled=True)  12.4 us
    all_to_all x1, starting transfers between devices, body(): lax.all_to_all(mixed, 'seq', split_axis=0, concat_axis=0, tiled=True)  10.6 us
  transfers between devices with their start and end apart: 4, of which 2 were waited for; matrix products, arithmetic and copies ran while one was open for 6% of the time, Pallas kernels for 0%

commit v1 on v0

v1 whole, which is shorter than its diff:
```python
import functools

import jax
import jax.numpy as jnp
from jax import lax
from jax.experimental import pallas as pl
from jax.experimental.pallas import tpu as pltpu
from jax.sharding import PartitionSpec as P

HEADS = 32
HD = 128
QT = 32
TOPK = 3
NY, NZ, NC = 4, 8, 2
NBLK = NY * NZ * NC
ROWS = 256
WIDTH = 1024
LOCAL = WIDTH // HD
TILES = ROWS // QT
MEANS = 32
EXT = WIDTH + 128
SCALE = HD ** -0.5
PLACES = [(0, 0, 0), (0, 0, 1)]
for hop in (1, 2, 3):
    PLACES += [(hop, 0, 0), (hop, 0, 1), (hop, 1, 1), (hop, 1, 0)]
PLACES += [(4, 0, 0), (4, 1, 1)]
SPANS = ((0, 6), (6, 10), (10, 14), (14, 16))


def at(y, z, c):
    return (y * NZ + z) * NC + c


COLUMNS = [[(y * NZ + z) * NC + c for y in range(NY)] for z in range(NZ) for c in range(NC)]


def send(x, to):
    pairs = []
    for y in range(NY):
        for z in range(NZ):
            for c in range(NC):
                there = to(y, z, c)
                if there is not None and 0 <= there[0] < NY:
                    pairs.append((at(y, z, c), at(there[0], there[1] % NZ, there[2])))
    return lax.ppermute(x, "seq", pairs)


def ring(x):
    return send(x, lambda y, z, c: (y, z + 1 - 2 * c, c))


def swap(x):
    return send(x, lambda y, z, c: (y, z, 1 - c))


def climb(x, steps):
    return send(x, lambda y, z, c: (y + steps, z, c))


def attend(q, k, v, ones, mask=None):
    scores = lax.dot_general(q, k, (((1,), (1,)), ((), ())), preferred_element_type=jnp.float32)
    if mask is not None:
        scores = jnp.where(mask, scores, -jnp.inf)
    top = jnp.max(scores, axis=1, keepdims=True)
    weights = jnp.exp((scores - top) * SCALE).astype(jnp.bfloat16)
    both = jnp.dot(weights, jnp.concatenate([v, ones], axis=1), preferred_element_type=jnp.float32)
    total = both[:, HD:]
    return both[:, :HD] / total, top * SCALE + jnp.log(total)


def own_kernel(q_ref, k_ref, v_ref, out_ref, lse_ref):
    row = lax.broadcasted_iota(jnp.int32, (ROWS, ROWS), 0)
    col = lax.broadcasted_iota(jnp.int32, (ROWS, ROWS), 1)
    lane = lax.broadcasted_iota(jnp.int32, (ROWS, 128), 1)
    ones = jnp.ones((ROWS, HD), jnp.bfloat16)
    lse_ref[...] = jnp.zeros_like(lse_ref)

    @pl.loop(0, LOCAL // 2)
    def _(half):
        for u in range(2):
            h = half * 2 + u
            cols = pl.ds(pl.multiple_of(h * HD, HD), HD)
            mixed, lse = attend(q_ref[:, cols], k_ref[:, cols], v_ref[:, cols], ones, col <= row)
            out_ref[:, cols] = mixed
            lse_ref[...] = jnp.where(lane == h, lse, lse_ref[...])


def chosen_kernel(span, keys_at, values_at, order_ref, idx_ref, q_ref, *refs):
    arrays = max(a for a, _ in values_at) + 1
    blocks, outs = refs[:arrays], refs[arrays:]
    outs = [outs[0].at[s] for s in range(NY)] if len(outs) == 1 else outs
    sides = [order_ref[s] for s in range(NY)]
    rows = NY * QT
    lane = lax.broadcasted_iota(jnp.int32, (rows, 128), 1)
    ones = jnp.ones((ROWS, HD), jnp.bfloat16)
    for i in range(span[1] - span[0]):
        tiles = [
            pl.ds(pl.multiple_of(idx_ref[side, span[0] + i] * QT, QT), QT) for side in sides
        ]
        (ka, kr), (va, vr) = keys_at[i], values_at[i]
        spread = jnp.zeros((rows, 128), jnp.float32)
        for h in range(LOCAL):
            cols = slice(h * HD, (h + 1) * HD)
            q = jnp.concatenate([q_ref[sides[s], tiles[s], cols] for s in range(NY)], axis=0)
            mixed, lse = attend(q, blocks[ka][kr:kr + ROWS, cols], blocks[va][vr:vr + ROWS, cols], ones)
            mixed = mixed.astype(jnp.bfloat16)
            for s in range(NY):
                outs[s][i * QT:(i + 1) * QT, cols] = mixed[s * QT:(s + 1) * QT]
            spread = jnp.where(lane % 8 == h, lse, spread)
        high = spread.astype(jnp.bfloat16).astype(jnp.float32)
        rest = spread - high
        middle = rest.astype(jnp.bfloat16).astype(jnp.float32)
        parts = jnp.where(lane < 8, high, jnp.where(lane < 16, middle, rest - middle))
        parts = jnp.where(lane < 24, parts, 0.0).astype(jnp.bfloat16)
        for s in range(NY):
            outs[s][i * QT:(i + 1) * QT, WIDTH:] = parts[s * QT:(s + 1) * QT]


def combine_kernel(kinds, last, sel_ref, before_ref, lse_ref, *refs):
    count = len(kinds)
    pieces, outs, held, sems = refs[:count], refs[count:-2], refs[-2], refs[-1]

    def fetch(p, n):
        rows = pl.ds(pl.multiple_of(sel_ref[n, 2] * QT, QT), QT)
        piece = pieces[p].at[sel_ref[n, 1], rows, :] if kinds[p] else pieces[p].at[rows, :]
        return pltpu.make_async_copy(piece, held.at[n], sems.at[n])

    def present(n):
        return (sel_ref[n, 0] >= 0) & (sel_ref[n, 0] < count)

    @pl.loop(0, TILES * TOPK)
    def _(n):
        for p in range(count):
            @pl.when(sel_ref[n, 0] == p)
            def _():
                fetch(p, n).start()

        @pl.when(jnp.logical_not(present(n)))
        def _():
            held[n] = jnp.zeros((QT, EXT), jnp.bfloat16)

    @pl.loop(0, TILES * TOPK)
    def _(n):
        for p in range(count):
            @pl.when(sel_ref[n, 0] == p)
            def _():
                fetch(p, n).wait()

    @pl.loop(0, TILES)
    def _(t):
        rows = pl.ds(pl.multiple_of(t * QT, QT), QT)
        here = [present(t * TOPK + c) for c in range(TOPK)]
        some = functools.reduce(jnp.logical_or, here)

        @pl.when(jnp.logical_not(some))
        def _():
            outs[0][rows, :] = before_ref[rows, :].astype(outs[0].dtype)
            if not last:
                outs[1][rows, :] = lse_ref[rows, :]

        @pl.when(some)
        def _():
            spreads = [lse_ref[rows, :]]
            for c in range(TOPK):
                parts = held[t * TOPK + c, :, WIDTH:].astype(jnp.float32)
                spread = parts + pltpu.roll(parts, 120, 1) + pltpu.roll(parts, 112, 1)
                spreads.append(jnp.where(here[c], spread, -jnp.inf))
            peak = functools.reduce(jnp.maximum, spreads)
            scales = [jnp.exp(spread - peak) for spread in spreads]
            total = functools.reduce(jnp.add, scales)
            scales = [scale / total for scale in scales]
            if not last:
                outs[1][rows, :] = peak + jnp.log(total)
            for h in range(LOCAL):
                cols = slice(h * HD, (h + 1) * HD)
                mixed = scales[0][:, h:h + 1] * before_ref[rows, cols]
                for c in range(TOPK):
                    mixed += scales[c + 1][:, h:h + 1] * held[t * TOPK + c, :, cols].astype(jnp.float32)
                outs[0][rows, cols] = mixed.astype(outs[0].dtype)


def gate_kernel(order_ref, q_ref, *refs):
    means, so_far, out_ref = refs[:order_ref.shape[0] // MEANS], refs[order_ref.shape[0] // MEANS:-1], refs[-1]
    share = jnp.concatenate([
        lax.dot_general(q_ref[...], ref[...], (((1,), (1,)), ((), ())), preferred_element_type=jnp.float32)
        for ref in means
    ], axis=1)
    total = jnp.dot(
        share, order_ref[...], precision=lax.Precision.HIGHEST, preferred_element_type=jnp.float32
    ) * (1.0 / HEADS)
    for ref in so_far:
        total += ref[...]
    out_ref[...] = total


VMEM = pl.BlockSpec(memory_space=pltpu.VMEM)
SMEM = pl.BlockSpec(memory_space=pltpu.SMEM)
HBM = pl.BlockSpec(memory_space=pltpu.HBM)
WIDE = pltpu.CompilerParams(vmem_limit_bytes=60 * 1024 * 1024)
PARAMS = pltpu.CompilerParams(vmem_limit_bytes=16 * 1024 * 1024)


COST = pl.CostEstimate(flops=1, bytes_accessed=1, transcendentals=0)


def own_attention(q, k, v):
    return pl.pallas_call(
        own_kernel,
        out_shape=(
            jax.ShapeDtypeStruct((ROWS, WIDTH), jnp.float32),
            jax.ShapeDtypeStruct((ROWS, 128), jnp.float32),
        ),
        in_specs=[VMEM] * 3,
        out_specs=(VMEM, VMEM),
        compiler_params=PARAMS,
        cost_estimate=COST,
        name="own_attention",
    )(q, k, v)


def chosen_attention(order, idx, sources, blocks, span, keys_at, values_at, apart):
    rows = (span[1] - span[0]) * QT
    shapes = [jax.ShapeDtypeStruct((rows, EXT), jnp.bfloat16)] * NY
    return pl.pallas_call(
        functools.partial(chosen_kernel, span, keys_at, values_at),
        out_shape=shapes if apart else jax.ShapeDtypeStruct((NY, rows, EXT), jnp.bfloat16),
        in_specs=[SMEM] * 2 + [VMEM] * (1 + len(blocks)),
        out_specs=[VMEM] * NY if apart else VMEM,
        compiler_params=PARAMS,
        cost_estimate=COST,
        name="chosen_attention",
    )(order, idx, sources, *blocks)


def combine(sel, state, pieces, last):
    small = jax.ShapeDtypeStruct((ROWS, 128), jnp.float32)
    whole = jax.ShapeDtypeStruct((ROWS, WIDTH), jnp.bfloat16 if last else jnp.float32)
    return pl.pallas_call(
        functools.partial(combine_kernel, tuple(x.ndim == 3 for x in pieces), last),
        out_shape=whole if last else (whole, small),
        in_specs=[SMEM, VMEM, VMEM] + [HBM] * len(pieces),
        out_specs=VMEM if last else (VMEM,) * 2,
        scratch_shapes=[
            pltpu.VMEM((TILES * TOPK, QT, EXT), jnp.bfloat16),
            pltpu.SemaphoreType.DMA((TILES * TOPK,)),
        ],
        compiler_params=WIDE,
        cost_estimate=COST,
        name="combine",
    )(sel, *state, *pieces)


def after(x, *others):
    return lax.optimization_barrier((x,) + others)[0] if others else x


def split(x):
    high = lax.reduce_precision(x, 8, 7)
    middle = lax.reduce_precision(x - high, 8, 7)
    return [high, middle, x - high - middle]


def gates(order, queries, carriers, *so_far):
    return pl.pallas_call(
        gate_kernel,
        out_shape=jax.ShapeDtypeStruct((ROWS, NBLK), jnp.float32),
        in_specs=[VMEM] * (2 + len(carriers) + len(so_far)),
        out_specs=VMEM,
        compiler_params=PARAMS,
        cost_estimate=COST,
        name="gate_share",
    )(order, queries, *carriers, *so_far)


def over_heads(share):
    for bits in (1, 2):
        share = share + lax.ppermute(share, "head", [(i, i ^ bits) for i in range(4)])
    return share


def body(queries, keys, values, gating):
    me = lax.axis_index("seq")
    y, z, c = me // (NZ * NC), (me // NC) % NZ, me % NC
    sign = 2 * c - 1

    k_swapped = swap(keys)
    own_k = jnp.concatenate([keys, k_swapped], axis=0)
    own_v = jnp.concatenate([values, swap(values)], axis=0)
    k_hops, v_hops = [own_k, ring(own_k)], [own_v, ring(own_v)]
    own_out, own_lse = own_attention(queries, keys, values)
    mean = after(jnp.sum(own_k.reshape(NC, ROWS, WIDTH), axis=1, dtype=jnp.float32) / ROWS, own_lse)
    means = jnp.concatenate([mean] + [climb(mean, d) for d in (1, 2, 3)], axis=0)
    means = jnp.concatenate(split(means) + [jnp.zeros((8, WIDTH), jnp.float32)], axis=0).astype(jnp.bfloat16)
    m_hops = [means]
    for _ in range(4):
        m_hops.append(ring(m_hops[-1]))

    choices = jnp.zeros((16, WIDTH), jnp.bfloat16).at[:TILES, :TOPK].set(gating.astype(jnp.bfloat16))
    sources = lax.all_gather(
        jnp.concatenate([queries, choices], axis=0), "seq", axis_index_groups=COLUMNS
    )
    chosen = sources[:, ROWS:ROWS + TILES, :TOPK].astype(jnp.int32)
    blocks = jnp.stack([
        (y * NZ + (z + (sign if chain == 0 else -sign) * hop) % NZ) * NC + (c ^ core)
        for hop, chain, core in PLACES
    ])
    hits = jnp.any(chosen[:, :, :, None] == blocks, axis=2)
    idx = jnp.max(jnp.where(hits, jnp.arange(TILES)[None, :, None], 0), axis=1).astype(jnp.int32)

    block_y, block_z, block_c = gating // (NZ * NC), (gating // NC) % NZ, gating % NC
    ahead = (block_z - z) * sign % NZ
    hop = jnp.minimum(ahead, NZ - ahead)
    core = c ^ block_c
    group = jnp.maximum(hop - 1, 0)
    chain = (ahead > 4) | ((ahead == 4) & (core == 1))
    within = jnp.where(hop == 4, core, jnp.where(chain, 3 - core, core) + jnp.where(hop == 1, 2, 0))
    up = jnp.clip(y - block_y, 0, NY - 1)
    kind = jnp.where(group < 2, group, jnp.where(group == 2, 2 + up, 2 + NY))
    sel = jnp.stack([jnp.where(gating != me, kind, -1), jnp.clip(block_y, 0, NY - 1), within], axis=2)
    sel = sel.reshape(TILES * TOPK, 3).astype(jnp.int32)
    late = jnp.concatenate([jnp.where(sel[:, :1] == 2 + NY, 0, -1), sel[:, 1:]], axis=1)

    r = jnp.arange(8 * MEANS)
    down, part, array = (r % 8) // 2, (r % MEANS) // 8, r // MEANS
    far = jnp.where(array > 4, 4 - array, array)
    column = ((y - down) * NZ + (z + sign * far) % NZ) * NC + (c ^ (array > 4) ^ (r % 2))
    column = jnp.where((part < 3) & (down <= y) & (column < me), column, -1)
    order = (column[:, None] == jnp.arange(NBLK)[None, :]).astype(jnp.float32)
    idx = after(idx, sel, late, order)

    k_other, v_other = [None], [None]
    rows_here = jnp.arange(NY, dtype=jnp.int32)
    rows_up = (rows_here + y) % NY

    def swap_hop(hop, *ties):
        k_other.append(swap(after(k_hops[hop], *ties)))
        v_other.append(swap(after(v_hops[hop], *ties)))

    def attend_hop(hop, idx):
        arrays = [k_hops[hop], v_hops[hop], k_other[hop], v_other[hop]]
        if hop == 1:
            arrays = [own_k, own_v] + arrays
        cuts = (0,) if hop == 4 else (0, ROWS)
        keys_at = [(a, cut) for a in range(0, len(arrays), 2) for cut in cuts]
        values_at = [(a + 1, cut) for a, cut in keys_at]
        apart = hop == 3
        return chosen_attention(rows_up if apart else rows_here, idx, sources, arrays, SPANS[hop - 1], keys_at, values_at, apart)

    def back(out):
        return lax.all_to_all(
            out, "seq", split_axis=0, concat_axis=0, tiled=True, axis_index_groups=COLUMNS
        )

    def back_up(outs):
        return [outs[0]] + [climb(outs[d], d) for d in (1, 2, 3)]

    for _ in range(2):
        k_hops.append(ring(k_hops[-1]))
        v_hops.append(ring(after(v_hops[-1], means) if len(v_hops) == 2 else v_hops[-1]))
    k_hops.append(ring(k_hops[3][:ROWS]))
    v_hops.append(ring(v_hops[3][:ROWS]))
    swap_hop(1)
    out1 = attend_hop(1, idx)
    back1 = back(out1)
    swap_hop(2, out1)
    out2 = attend_hop(2, idx)
    back2 = back(out2)
    swap_hop(3, out2, back1, m_hops[1])
    out3 = attend_hop(3, idx)
    back3 = back_up(out3)
    swap_hop(4, m_hops[2], *out3)
    out4 = attend_hop(4, idx)
    back4 = back(out4)
    m_other = swap(jnp.concatenate(m_hops[1:4], axis=0))

    share = gates(order, queries, m_hops + [m_other[i * MEANS:(i + 1) * MEANS] for i in range(3)])
    gate_scores = over_heads(after(share, out4))
    state = combine(sel, (own_out, own_lse), [back1, back2] + back3, False)
    return combine(late, state, [back4], True), gate_scores


def solution(mesh):
    return jax.shard_map(
        body,
        mesh=mesh,
        in_specs=(P("seq", "head"), P("seq", "head"), P("seq", "head"), P("seq", None)),
        out_specs=(P("seq", "head"), P("seq", None)),
        check_vma=False,
    )
```

time: 404 us -> 176 us (0.44)
  blocking collectives: 128 us -> 0 us
  waiting for transfers between devices: 135 us -> 55.6 us
  local copies, waits for them, and re-layouts: 52.3 us -> 17.6 us
  Pallas kernels: 0 us -> 32.2 us
  matrix products: 30.9 us -> 0 us
  starting transfers between devices: 29.9 us -> 47.6 us
  other arithmetic: 11.2 us -> 4.73 us
    all_gather x1 -> x0, blocking collectives: 128 us -> none  [body(): lax.all_gather(local_mean.reshape(1, width), 'seq', axis=0, tiled=True)]
    all_to_all x3, waiting for transfers between devices: 93.9 us -> 0.01 us  [back(): lax.all_to_all(out, 'seq', split_axis=0, concat_axis=0, tiled=True, axis_...]
    ppermute x0 -> x31, waiting for transfers between devices: none -> 51.5 us  [the longest x29 48 us: send(): return lax.ppermute(x, 'seq', pairs)]
    psum x1 -> x0, waiting for transfers between devices: 41.6 us -> none  [body(): gate_total = lax.psum(share, 'head')]
    pallas_call x0 -> x8, Pallas kernels: none -> 32.2 us  [the longest x4 16.1 us: chosen_attention(): pl.pallas_call(functools.partial(chosen_kernel, span, keys_at, values_at)...]
    ppermute x0 -> x31, starting transfers between devices: none -> 31.7 us  [the longest x29 27 us: send(): return lax.ppermute(x, 'seq', pairs)]
    dot_general x18 -> x0, matrix products: 30.9 us -> none  [the longest x5 20.5 us: attend(): jnp.einsum('hqk,khd->qhd', weights.astype(jnp.bfloat16), value_block, pre...]
    convert_element_type x3 -> x1, local copies, waits for them, and re-layouts: 14.4 us -> 0.1 us  [body(): chosen = sources[:, ROWS:ROWS + TILES, :TOPK].astype(jnp.int32)]
  transfers between devices with their start and end apart: 4 -> 35, of which waited for: 2 -> 10; matrix products, arithmetic and copies ran while one was open for 6% -> 6% of each run, Pallas kernels for 0% -> 16%
where the time goes in v1:
time: 176 us; the launch traced here: 172 us
  waiting for transfers between devices  55.6 us (32%)
  starting transfers between devices  47.6 us (27%)
  Pallas kernels  32.2 us (18%)
  local copies, waits for them, and re-layouts  17.6 us (10%)
  between operations  14.8 us (8%)
  other arithmetic  4.73 us (3%)
    ppermute x29, waiting for transfers between devices, send(): return lax.ppermute(x, 'seq', pairs)  48 us
    ppermute x29, starting transfers between devices, send(): return lax.ppermute(x, 'seq', pairs)  27 us
    pallas_call x4, Pallas kernels, chosen_attention(): pl.pallas_call(functools.partial(chosen_kernel, span, keys_at, values_at)...  16.1 us
    all_to_all x3, starting transfers between devices, back(): lax.all_to_all(out, 'seq', split_axis=0, concat_axis=0, tiled=True, axis_...  15.9 us
    pallas_call x2, Pallas kernels, combine(): pl.pallas_call(functools.partial(combine_kernel, tuple((x.ndim == 3 for x...  11 us
    unnamed x52, local copies, waits for them, and re-layouts  10.8 us
    ppermute x2, starting transfers between devices, over_heads(): lax.ppermute(share, 'head', [(i, i ^ bits) for i in range(4)])  4.68 us
    all_gather x1, waiting for transfers between devices, body(): lax.all_gather(jnp.concatenate([queries, choices], axis=0), 'seq', axis_i...  4.07 us
  transfers between devices with their start and end apart: 35, of which 10 were waited for; matrix products, arithmetic and copies ran while one was open for 6% of the time, Pallas kernels for 16%

profile of v1, /device:TPU:8, one launch (start us, length us, event | category | flops | bytes accessed | tf_op | source)
XLA Modules:
  0.0 172.4 jit_solution(3567481791460034489)
XLA Ops:
  8.2 1.9 %fusion.1 = bf16[272,1024]{1,0:T(8,128)(2,1)} fusion(bf16[8,3]{1,0:T(8,128)(2,1)S(1)} %copy.51, bf16[256,1024]{1,0:T(8,128)(2,1)} %q_ref.3), kind=kLoop, calls=%fused_computation.3 | loop fusion | flops 1671168 | bytes 1081392 | tf_op jit(solution)/shard_map/concatenate | solution.py:300
  12.2 2.0 %collective-permute-start.2 = (bf16[512,1024]{1,0:T(8,128)(2,1)S(1)}, bf16[512,1024]{1,0:T(8,128)(2,1)}, u32[]{:S(2)}, u32[]{:S(2)}) collective-permute-start(bf16[512,1024]{1,0:T(8,128)(2,1)S(1)} %constant_dynamic-update-slice_fusion.refs_0_), channel_id=1, source_target_pairs={{0,8},{4,60},{8,16},{12,4},{16,24},{20,12},{24,32},{28,20},{32,40}... | collective-permute-start | bytes 3145736 | tf_op jit(solution)/shard_map/ppermute | solution.py:45
  14.2 2.0 %collective-permute-start.3 = (bf16[512,1024]{1,0:T(8,128)(2,1)S(1)}, bf16[512,1024]{1,0:T(8,128)(2,1)}, u32[]{:S(2)}, u32[]{:S(2)}) collective-permute-start(bf16[512,1024]{1,0:T(8,128)(2,1)S(1)} %constant_dynamic-update-slice_fusion.2.refs_1_), channel_id=1, source_target_pairs={{0,8},{4,60},{8,16},{12,4},{16,24},{20,12},{24,32},{28,20},{32,40}... | collective-permute-start | bytes 3145736 | tf_op jit(solution)/shard_map/ppermute | solution.py:45
  16.2 3.1 %own_attention.1 = (f32[256,1024]{1,0:T(8,128)S(1)}, f32[256,128]{1,0:T(8,128)S(1)}) custom-call(bf16[256,1024]{1,0:T(8,128)(2,1)S(1)} %copy-done.3, bf16[256,1024]{1,0:T(8,128)(2,1)S(1)} %copy-done.5, bf16[256,1024]{1,0:T(8,128)(2,1)} %v_ref.1), custom_call_target="tpu_custom_call" | custom-call | flops 1 | bytes 1 | tf_op jit(solution)/shard_map/own_attention/pallas_call | solution.py:207
  21.1 3.5 %collective-permute-start.7 = (f32[2,1024]{1,0:T(2,128)S(1)}, f32[2,1024]{1,0:T(2,128)S(1)}, u32[]{:S(2)}, u32[]{:S(2)}) collective-permute-start(f32[2,1024]{1,0:T(2,128)S(1)} %broadcast_multiply_fusion), channel_id=1, source_target_pairs={{0,64},{4,68},{8,72},{12,76},{16,80},{20,84},{24,88},{28,92},{32,9... | collective-permute-start | bytes 24584 | tf_op jit(solution)/shard_map/ppermute | solution.py:45
  24.6 2.0 %collective-permute-start.8 = (f32[2,1024]{1,0:T(2,128)S(1)}, f32[2,1024]{1,0:T(2,128)S(1)}, u32[]{:S(2)}, u32[]{:S(2)}) collective-permute-start(f32[2,1024]{1,0:T(2,128)S(1)} %broadcast_multiply_fusion), channel_id=1, source_target_pairs={{0,128},{4,132},{8,136},{12,140},{16,144},{20,148},{24,152},{28,15... | collective-permute-start | bytes 24584 | tf_op jit(solution)/shard_map/ppermute | solution.py:45
  27.6 3.4 %collective-permute-done.2.refs_2_ = bf16[512,1024]{1,0:T(8,128)(2,1)} collective-permute-done((bf16[512,1024]{1,0:T(8,128)(2,1)S(1)}, bf16[512,1024]{1,0:T(8,128)(2,1)}, u32[]{:S(2)}, u32[]{:S(2)}) %collective-permute-start.2) | collective-permute-done | bytes 1048608 | tf_op jit(solution)/shard_map/ppermute | solution.py:45
  31.0 11.2 %collective-permute-done.3.refs_3_ = bf16[512,1024]{1,0:T(8,128)(2,1)} collective-permute-done((bf16[512,1024]{1,0:T(8,128)(2,1)S(1)}, bf16[512,1024]{1,0:T(8,128)(2,1)}, u32[]{:S(2)}, u32[]{:S(2)}) %collective-permute-start.3) | collective-permute-done | bytes 1048608 | tf_op jit(solution)/shard_map/ppermute | solution.py:45
  42.6 4.1 %all-gather.3.cloned.1.call-done = bf16[1088,1024]{1,0:T(8,128)(2,1)} async-done(((bf16[272,1024]{1,0:T(8,128)(2,1)}), bf16[1088,1024]{1,0:T(8,128)(2,1)}) %all-gather.3.cloned.1.call-update) | async-done | bytes 2228240 | tf_op jit(solution)/shard_map/all_gather | solution.py:299
  47.7 1.6 copy-done
  49.3 5.2 %chosen_attention.4 = bf16[4,192,1152]{2,1,0:T(8,128)(2,1)S(1)} custom-call(s32[4]{0:T(128)S(1)} %iota.32.order_ref, s32[4,16]{1,0:T(4,128)S(1)} %select_reduce_fusion.idx_ref, bf16[4,272,1024]{2,1,0:T(8,128)(2,1)S(1)} %bitcast.21, bf16[512,1024]{1,0:T(8,128)(2,1)S(1)} %constant_dynamic-update-slice_fusion.refs_0_, ...), custom_call_target="tpu_custom_call" | custom-call | flops 1 | bytes 1 | tf_op jit(solution)/shard_map/chosen_attention/pallas_call | solution.py:224
  55.7 5.9 %all-to-all-start = ((bf16[4,192,1152]{2,1,0:T(8,128)(2,1)}), bf16[4,192,1152]{2,1,0:T(8,128)(2,1)}, u32[]{:S(2)}, u32[]{:S(2)}) async-start(bf16[4,192,1152]{2,1,0:T(8,128)(2,1)} %copy-done.2), calls=%async_computation | async-start | bytes 3538944 | tf_op jit(solution)/shard_map/all_to_all | solution.py:350
  61.7 8.3 %collective-permute-done.6.refs_0_ = bf16[512,1024]{1,0:T(8,128)(2,1)} collective-permute-done((bf16[512,1024]{1,0:T(8,128)(2,1)}, bf16[512,1024]{1,0:T(8,128)(2,1)}, u32[]{:S(2)}, u32[]{:S(2)}) %collective-permute-start.6) | collective-permute-done | bytes 1048608 | tf_op jit(solution)/shard_map/ppermute | solution.py:45
  70.0 2.6 %collective-permute-start.15 = (bf16[32,1024]{1,0:T(8,128)(2,1)S(1)}, bf16[32,1024]{1,0:T(8,128)(2,1)S(1)}, u32[]{:S(2)}, u32[]{:S(2)}) collective-permute-start(bf16[32,1024]{1,0:T(8,128)(2,1)S(1)} %maximum_maximum_fusion.refs_0_), channel_id=1, source_target_pairs={{0,8},{4,60},{8,16},{12,4},{16,24},{20,12},{24,32},{28,20},{32,40}... | collective-permute-start | bytes 196616 | tf_op jit(solution)/shard_map/ppermute | solution.py:45
  72.8 3.7 %chosen_attention.5 = bf16[4,128,1152]{2,1,0:T(8,128)(2,1)S(1)} custom-call(s32[4]{0:T(128)S(1)} %iota.37.order_ref, s32[4,16]{1,0:T(4,128)S(1)} %select_reduce_fusion.idx_ref, bf16[4,272,1024]{2,1,0:T(8,128)(2,1)S(1)} %bitcast.22, bf16[512,1024]{1,0:T(8,128)(2,1)} %collective-permute-done.6.refs_0_, bf16[512,1024]{1,0:T(8,128)(2,1)} %collective-permute-done.10.refs_1_, ...), custom_call_target="tpu_custom_call" | custom-call | flops 1 | bytes 1 | tf_op jit(solution)/shard_map/chosen_attention/pallas_call | solution.py:224
  77.5 20.6 %collective-permute-done.15.refs_1_ = bf16[32,1024]{1,0:T(8,128)(2,1)S(1)} collective-permute-done((bf16[32,1024]{1,0:T(8,128)(2,1)S(1)}, bf16[32,1024]{1,0:T(8,128)(2,1)S(1)}, u32[]{:S(2)}, u32[]{:S(2)}) %collective-permute-start.15) | collective-permute-done | bytes 65568 | tf_op jit(solution)/shard_map/ppermute | solution.py:45
  98.6 1.9 %slice.49 = bf16[256,1024]{1,0:T(8,128)(2,1)} slice(bf16[512,1024]{1,0:T(8,128)(2,1)} %collective-permute-done.14.refs_1_), slice={[0:256], [0:1024]} | slice | bytes 1048576 | tf_op jit(solution)/shard_map/slice | solution.py:361
  100.5 1.9 %slice.48 = bf16[256,1024]{1,0:T(8,128)(2,1)} slice(bf16[512,1024]{1,0:T(8,128)(2,1)} %collective-permute-done.13.refs_0_), slice={[0:256], [0:1024]} | slice | bytes 1048576 | tf_op jit(solution)/shard_map/slice | solution.py:360
  102.4 4.9 %all-to-all-start.1 = ((bf16[4,128,1152]{2,1,0:T(8,128)(2,1)}), bf16[4,128,1152]{2,1,0:T(8,128)(2,1)}, u32[]{:S(2)}, u32[]{:S(2)}) async-start(bf16[4,128,1152]{2,1,0:T(8,128)(2,1)} %copy-done.4), calls=%async_computation.1 | async-start | bytes 2359296 | tf_op jit(solution)/shard_map/all_to_all | solution.py:350
  107.3 2.6 %collective-permute-start.23 = (bf16[32,1024]{1,0:T(8,128)(2,1)S(1)}, bf16[32,1024]{1,0:T(8,128)(2,1)S(1)}, u32[]{:S(2)}, u32[]{:S(2)}) collective-permute-start(bf16[32,1024]{1,0:T(8,128)(2,1)S(1)} %collective-permute-done.15.refs_1_), channel_id=1, source_target_pairs={{0,8},{4,60},{8,16},{12,4},{16,24},{20,12},{24,32},{28,20},{32,40}... | collective-permute-start | bytes 196616 | tf_op jit(solution)/shard_map/ppermute | solution.py:45
  109.8 4.3 %chosen_attention.6 = (bf16[128,1152]{1,0:T(8,128)(2,1)S(1)}, bf16[128,1152]{1,0:T(8,128)(2,1)S(1)}, bf16[128,1152]{1,0:T(8,128)(2,1)S(1)}, bf16[128,1152]{1,0:T(8,128)(2,1)S(1)}) custom-call(s32[4]{0:T(128)S(1)} %and_select_fusion.order_ref, s32[4,16]{1,0:T(4,128)S(1)} %select_reduce_fusion.idx_ref, bf16[4,272,1024]{2,1,0:T(8,128)(2,1)S(1)} %bitcast.23, ...), custom_call_target="tpu_custom_call" | custom-call | flops 1 | bytes 1 | tf_op jit(solution)/shard_map/chosen_attention/pallas_call | solution.py:224
  117.9 2.6 %collective-permute-start.26 = (bf16[32,1024]{1,0:T(8,128)(2,1)S(1)}, bf16[32,1024]{1,0:T(8,128)(2,1)S(1)}, u32[]{:S(2)}, u32[]{:S(2)}) collective-permute-start(bf16[32,1024]{1,0:T(8,128)(2,1)S(1)} %collective-permute-done.23.refs_2_), channel_id=1, source_target_pairs={{0,8},{4,60},{8,16},{12,4},{16,24},{20,12},{24,32},{28,20},{32,40}... | collective-permute-start | bytes 196616 | tf_op jit(solution)/shard_map/ppermute | solution.py:45
  120.6 2.8 %collective-permute-done.26.refs_3_ = bf16[32,1024]{1,0:T(8,128)(2,1)S(1)} collective-permute-done((bf16[32,1024]{1,0:T(8,128)(2,1)S(1)}, bf16[32,1024]{1,0:T(8,128)(2,1)S(1)}, u32[]{:S(2)}, u32[]{:S(2)}) %collective-permute-start.26) | collective-permute-done | bytes 65568 | tf_op jit(solution)/shard_map/ppermute | solution.py:45
  124.2 3.0 %chosen_attention.7 = bf16[4,64,1152]{2,1,0:T(8,128)(2,1)} custom-call(s32[4]{0:T(128)S(1)} %iota.39.order_ref, s32[4,16]{1,0:T(4,128)S(1)} %select_reduce_fusion.idx_ref, bf16[4,272,1024]{2,1,0:T(8,128)(2,1)S(1)} %bitcast.24, bf16[256,1024]{1,0:T(8,128)(2,1)} %collective-permute-done.21.refs_0_, bf16[256,1024]{1,0:T(8,128)(2,1)S(1)} %collective-permute-done.22.refs_1_, ...), custom_call_target="tpu_custom_call" | custom-call | flops 1 | bytes 1 | tf_op jit(solution)/shard_map/chosen_attention/pallas_call | solution.py:224
  127.2 5.1 %all-to-all-start.2 = ((bf16[4,64,1152]{2,1,0:T(8,128)(2,1)}), bf16[4,64,1152]{2,1,0:T(8,128)(2,1)S(1)}, u32[]{:S(2)}, u32[]{:S(2)}) async-start(bf16[4,64,1152]{2,1,0:T(8,128)(2,1)} %chosen_attention.7), calls=%async_computation.2 | async-start | bytes 1179648 | tf_op jit(solution)/shard_map/all_to_all | solution.py:350
  133.6 3.4 %collective-permute-start.18 = (bf16[128,1152]{1,0:T(8,128)(2,1)S(1)}, bf16[128,1152]{1,0:T(8,128)(2,1)S(1)}, u32[]{:S(2)}, u32[]{:S(2)}) collective-permute-start(bf16[128,1152]{1,0:T(8,128)(2,1)S(1)} %copy-done.18), channel_id=1, source_target_pairs={{0,64},{4,68},{8,72},{12,76},{16,80},{20,84},{24,88},{28,92},{32,9... | collective-permute-start | bytes 884744 | tf_op jit(solution)/shard_map/ppermute | solution.py:45
  137.0 1.9 %collective-permute-start.19 = (bf16[128,1152]{1,0:T(8,128)(2,1)S(1)}, bf16[128,1152]{1,0:T(8,128)(2,1)S(1)}, u32[]{:S(2)}, u32[]{:S(2)}) collective-permute-start(bf16[128,1152]{1,0:T(8,128)(2,1)S(1)} %copy-done.16), channel_id=1, source_target_pairs={{0,128},{4,132},{8,136},{12,140},{16,144},{20,148},{24,152},{28,15... | collective-permute-start | bytes 884744 | tf_op jit(solution)/shard_map/ppermute | solution.py:45
  140.5 2.0 %gate_share.1 = f32[256,64]{1,0:T(8,128)S(1)} custom-call(f32[256,64]{1,0:T(8,128)S(1)} %fusion.2.order_ref, bf16[256,1024]{1,0:T(8,128)(2,1)S(1)} %copy-done.3, bf16[32,1024]{1,0:T(8,128)(2,1)S(1)} %maximum_maximum_fusion.refs_0_, bf16[32,1024]{1,0:T(8,128)(2,1)S(1)} %collective-permute-done.15.refs_1_, bf16[32,1024]{1,0:T(8,128)(2,1)S(1)} %copy-done.9, ...), custom_call_target="tpu_custom_call" | custom-call | flops 1 | bytes 1 | tf_op jit(solution)/shard_map/gate_share/pallas_call | solution.py:264
  144.1 3.5 %collective-permute-done.29 = f32[256,64]{1,0:T(8,128)S(1)} collective-permute-done((f32[256,64]{1,0:T(8,128)S(1)}, f32[256,64]{1,0:T(8,128)S(1)}, u32[]{:S(2)}, u32[]{:S(2)}) %collective-permute-start.29) | collective-permute-done | bytes 65568 | tf_op jit(solution)/shard_map/ppermute | solution.py:277
  147.6 3.1 %collective-permute-start.30 = (f32[256,64]{1,0:T(8,128)S(1)}, f32[256,64]{1,0:T(8,128)S(1)}, u32[]{:S(2)}, u32[]{:S(2)}) collective-permute-start(f32[256,64]{1,0:T(8,128)S(1)} %add.336), channel_id=1, source_target_pairs={{0,2},{1,3},{2,0},{3,1},{4,6},{5,7},{6,4},{7,5},{8,10},{9,11},{10,... | collective-permute-start | bytes 196616 | tf_op jit(solution)/shard_map/ppermute | solution.py:277
  153.0 6.7 %combine.2 = (f32[256,1024]{1,0:T(8,128)}, f32[256,128]{1,0:T(8,128)}) custom-call(s32[24,3]{1,0:T(8,128)} %copy.48.sel_ref, f32[256,1024]{1,0:T(8,128)} %copy-done.6, f32[256,128]{1,0:T(8,128)} %copy-done.12, bf16[4,192,1152]{2,1,0:T(8,128)(2,1)} %all-to-all-done.refs_0_, bf16[4,128,1152]{2,1,0:T(8,128)(2,1)} %all-to-all-done.1.refs_1_, ...), custom_call_target="tpu_custom_call" | custom-call | flops 1 | bytes 1 | tf_op jit(solution)/shard_map/combine/pallas_call | solution.py:238
  161.3 4.3 %combine.3 = bf16[256,1024]{1,0:T(8,128)(2,1)} custom-call(s32[24,3]{1,0:T(8,128)} %copy.49.sel_ref, f32[256,1024]{1,0:T(8,128)} %get-tuple-element.45.before_ref, f32[256,128]{1,0:T(8,128)} %get-tuple-element.46.lse_ref, bf16[4,64,1152]{2,1,0:T(8,128)(2,1)} %copy-done.19), custom_call_target="tpu_custom_call" | custom-call | flops 1 | bytes 1 | tf_op jit(solution)/shard_map/combine/pallas_call | solution.py:238
  (137 shorter events, 22.8 us)
Async XLA Ops:
  7.2 39.5 %all-gather.3.cloned.1.call-start = ((), (), s32[]{:S(2)}) async-start(), calls=%async_computation.3 | async-start | bytes 2785280 | tf_op jit(solution)/shard_map/all_gather | solution.py:299
  12.2 18.8 %collective-permute-start.2 = (bf16[512,1024]{1,0:T(8,128)(2,1)S(1)}, bf16[512,1024]{1,0:T(8,128)(2,1)}, u32[]{:S(2)}, u32[]{:S(2)}) collective-permute-start(bf16[512,1024]{1,0:T(8,128)(2,1)S(1)} %constant_dynamic-update-slice_fusion.refs_0_), channel_id=1, source_target_pairs={{0,8},{4,60},{8,16},{12,4},{16,24},{20,12},{24,32},{28,20},{32,40}... | collective-permute-start | bytes 3145736 | tf_op jit(solution)/shard_map/ppermute | solution.py:45
  14.2 28.0 %collective-permute-start.3 = (bf16[512,1024]{1,0:T(8,128)(2,1)S(1)}, bf16[512,1024]{1,0:T(8,128)(2,1)}, u32[]{:S(2)}, u32[]{:S(2)}) collective-permute-start(bf16[512,1024]{1,0:T(8,128)(2,1)S(1)} %constant_dynamic-update-slice_fusion.2.refs_1_), channel_id=1, source_target_pairs={{0,8},{4,60},{8,16},{12,4},{16,24},{20,12},{24,32},{28,20},{32,40}... | collective-permute-start | bytes 3145736 | tf_op jit(solution)/shard_map/ppermute | solution.py:45
  21.1 21.1 %collective-permute-start.7 = (f32[2,1024]{1,0:T(2,128)S(1)}, f32[2,1024]{1,0:T(2,128)S(1)}, u32[]{:S(2)}, u32[]{:S(2)}) collective-permute-start(f32[2,1024]{1,0:T(2,128)S(1)} %broadcast_multiply_fusion), channel_id=1, source_target_pairs={{0,64},{4,68},{8,72},{12,76},{16,80},{20,84},{24,88},{28,92},{32,9... | collective-permute-start | bytes 24584 | tf_op jit(solution)/shard_map/ppermute | solution.py:45
  24.6 17.6 %collective-permute-start.8 = (f32[2,1024]{1,0:T(2,128)S(1)}, f32[2,1024]{1,0:T(2,128)S(1)}, u32[]{:S(2)}, u32[]{:S(2)}) collective-permute-start(f32[2,1024]{1,0:T(2,128)S(1)} %broadcast_multiply_fusion), channel_id=1, source_target_pairs={{0,128},{4,132},{8,136},{12,140},{16,144},{20,148},{24,152},{28,15... | collective-permute-start | bytes 24584 | tf_op jit(solution)/shard_map/ppermute | solution.py:45
  26.6 15.6 %collective-permute-start.9 = (f32[2,1024]{1,0:T(2,128)S(1)}, f32[2,1024]{1,0:T(2,128)S(1)}, u32[]{:S(2)}, u32[]{:S(2)}) collective-permute-start(f32[2,1024]{1,0:T(2,128)S(1)} %broadcast_multiply_fusion), channel_id=1, source_target_pairs={{0,192},{4,196},{8,200},{12,204},{16,208},{20,212},{24,216},{28,22... | collective-permute-start | bytes 24584 | tf_op jit(solution)/shard_map/ppermute | solution.py:45
  31.0 16.6 %collective-permute-start.4 = (bf16[512,1024]{1,0:T(8,128)(2,1)}, bf16[512,1024]{1,0:T(8,128)(2,1)}, u32[]{:S(2)}, u32[]{:S(2)}) collective-permute-start(bf16[512,1024]{1,0:T(8,128)(2,1)} %collective-permute-done.2.refs_2_), channel_id=1, source_target_pairs={{0,4},{4,0},{8,12},{12,8},{16,20},{20,16},{24,28},{28,24},{32,36},... | collective-permute-start | bytes 3145736 | tf_op jit(solution)/shard_map/ppermute | solution.py:45
  42.2 5.4 %collective-permute-start.5 = (bf16[512,1024]{1,0:T(8,128)(2,1)}, bf16[512,1024]{1,0:T(8,128)(2,1)}, u32[]{:S(2)}, u32[]{:S(2)}) collective-permute-start(bf16[512,1024]{1,0:T(8,128)(2,1)} %collective-permute-done.3.refs_3_), channel_id=1, source_target_pairs={{0,4},{4,0},{8,12},{12,8},{16,20},{20,16},{24,28},{28,24},{32,36},... | collective-permute-start | bytes 3145736 | tf_op jit(solution)/shard_map/ppermute | solution.py:45
  42.3 19.3 %collective-permute-start.10 = (bf16[512,1024]{1,0:T(8,128)(2,1)}, bf16[512,1024]{1,0:T(8,128)(2,1)}, u32[]{:S(2)}, u32[]{:S(2)}) collective-permute-start(bf16[512,1024]{1,0:T(8,128)(2,1)} %collective-permute-done.3.refs_3_), channel_id=1, source_target_pairs={{0,8},{4,60},{8,16},{12,4},{16,24},{20,12},{24,32},{28,20},{32,40}... | collective-permute-start | bytes 3145736 | tf_op jit(solution)/shard_map/ppermute | solution.py:45
  42.4 27.5 %collective-permute-start.6 = (bf16[512,1024]{1,0:T(8,128)(2,1)}, bf16[512,1024]{1,0:T(8,128)(2,1)}, u32[]{:S(2)}, u32[]{:S(2)}) collective-permute-start(bf16[512,1024]{1,0:T(8,128)(2,1)} %collective-permute-done.2.refs_2_), channel_id=1, source_target_pairs={{0,8},{4,60},{8,16},{12,4},{16,24},{20,12},{24,32},{28,20},{32,40}... | collective-permute-start | bytes 3145736 | tf_op jit(solution)/shard_map/ppermute | solution.py:45
  55.7 42.4 %all-to-all-start = ((bf16[4,192,1152]{2,1,0:T(8,128)(2,1)}), bf16[4,192,1152]{2,1,0:T(8,128)(2,1)}, u32[]{:S(2)}, u32[]{:S(2)}) async-start(bf16[4,192,1152]{2,1,0:T(8,128)(2,1)} %copy-done.2), calls=%async_computation | async-start | bytes 3538944 | tf_op jit(solution)/shard_map/all_to_all | solution.py:350
  61.7 10.9 %collective-permute-start.12 = (bf16[512,1024]{1,0:T(8,128)(2,1)}, bf16[512,1024]{1,0:T(8,128)(2,1)S(1)}, u32[]{:S(2)}, u32[]{:S(2)}) collective-permute-start(bf16[512,1024]{1,0:T(8,128)(2,1)} %collective-permute-done.10.refs_1_), channel_id=1, source_target_pairs={{0,4},{4,0},{8,12},{12,8},{16,20},{20,16},{24,28},{28,24},{32,36},... | collective-permute-start | bytes 3145736 | tf_op jit(solution)/shard_map/ppermute | solution.py:45
  69.9 28.2 %collective-permute-start.14 = (bf16[512,1024]{1,0:T(8,128)(2,1)}, bf16[512,1024]{1,0:T(8,128)(2,1)}, u32[]{:S(2)}, u32[]{:S(2)}) collective-permute-start(bf16[512,1024]{1,0:T(8,128)(2,1)} %collective-permute-done.10.refs_1_), channel_id=1, source_target_pairs={{0,8},{4,60},{8,16},{12,4},{16,24},{20,12},{24,32},{28,20},{32,40}... | collective-permute-start | bytes 3145736 | tf_op jit(solution)/shard_map/ppermute | solution.py:45
  69.9 28.2 %collective-permute-start.13 = (bf16[512,1024]{1,0:T(8,128)(2,1)}, bf16[512,1024]{1,0:T(8,128)(2,1)}, u32[]{:S(2)}, u32[]{:S(2)}) collective-permute-start(bf16[512,1024]{1,0:T(8,128)(2,1)} %collective-permute-done.6.refs_0_), channel_id=1, source_target_pairs={{0,8},{4,60},{8,16},{12,4},{16,24},{20,12},{24,32},{28,20},{32,40}... | collective-permute-start | bytes 3145736 | tf_op jit(solution)/shard_map/ppermute | solution.py:45
  70.0 28.1 %collective-permute-start.15 = (bf16[32,1024]{1,0:T(8,128)(2,1)S(1)}, bf16[32,1024]{1,0:T(8,128)(2,1)S(1)}, u32[]{:S(2)}, u32[]{:S(2)}) collective-permute-start(bf16[32,1024]{1,0:T(8,128)(2,1)S(1)} %maximum_maximum_fusion.refs_0_), channel_id=1, source_target_pairs={{0,8},{4,60},{8,16},{12,4},{16,24},{20,12},{24,32},{28,20},{32,40}... | collective-permute-start | bytes 196616 | tf_op jit(solution)/shard_map/ppermute | solution.py:45
  98.1 11.7 %collective-permute-start.17 = (bf16[512,1024]{1,0:T(8,128)(2,1)}, bf16[512,1024]{1,0:T(8,128)(2,1)}, u32[]{:S(2)}, u32[]{:S(2)}) collective-permute-start(bf16[512,1024]{1,0:T(8,128)(2,1)} %collective-permute-done.14.refs_1_), channel_id=1, source_target_pairs={{0,4},{4,0},{8,12},{12,8},{16,20},{20,16},{24,28},{28,24},{32,36},... | collective-permute-start | bytes 3145736 | tf_op jit(solution)/shard_map/ppermute | solution.py:45
  98.1 11.7 %collective-permute-start.16 = (bf16[512,1024]{1,0:T(8,128)(2,1)}, bf16[512,1024]{1,0:T(8,128)(2,1)}, u32[]{:S(2)}, u32[]{:S(2)}) collective-permute-start(bf16[512,1024]{1,0:T(8,128)(2,1)} %collective-permute-done.13.refs_0_), channel_id=1, source_target_pairs={{0,4},{4,0},{8,12},{12,8},{16,20},{20,16},{24,28},{28,24},{32,36},... | collective-permute-start | bytes 3145736 | tf_op jit(solution)/shard_map/ppermute | solution.py:45
  100.5 16.9 %collective-permute-start.22 = (bf16[256,1024]{1,0:T(8,128)(2,1)}, bf16[256,1024]{1,0:T(8,128)(2,1)S(1)}, u32[]{:S(2)}, u32[]{:S(2)}) collective-permute-start(bf16[256,1024]{1,0:T(8,128)(2,1)} %slice.49), channel_id=1, source_target_pairs={{0,8},{4,60},{8,16},{12,4},{16,24},{20,12},{24,32},{28,20},{32,40}... | collective-permute-start | bytes 1572872 | tf_op jit(solution)/shard_map/ppermute | solution.py:45
  102.4 15.1 %collective-permute-start.21 = (bf16[256,1024]{1,0:T(8,128)(2,1)}, bf16[256,1024]{1,0:T(8,128)(2,1)}, u32[]{:S(2)}, u32[]{:S(2)}) collective-permute-start(bf16[256,1024]{1,0:T(8,128)(2,1)} %slice.48), channel_id=1, source_target_pairs={{0,8},{4,60},{8,16},{12,4},{16,24},{20,12},{24,32},{28,20},{32,40}... | collective-permute-start | bytes 1572872 | tf_op jit(solution)/shard_map/ppermute | solution.py:45
  102.4 24.8 %all-to-all-start.1 = ((bf16[4,128,1152]{2,1,0:T(8,128)(2,1)}), bf16[4,128,1152]{2,1,0:T(8,128)(2,1)}, u32[]{:S(2)}, u32[]{:S(2)}) async-start(bf16[4,128,1152]{2,1,0:T(8,128)(2,1)} %copy-done.4), calls=%async_computation.1 | async-start | bytes 2359296 | tf_op jit(solution)/shard_map/all_to_all | solution.py:350
  107.3 10.1 %collective-permute-start.23 = (bf16[32,1024]{1,0:T(8,128)(2,1)S(1)}, bf16[32,1024]{1,0:T(8,128)(2,1)S(1)}, u32[]{:S(2)}, u32[]{:S(2)}) collective-permute-start(bf16[32,1024]{1,0:T(8,128)(2,1)S(1)} %collective-permute-done.15.refs_1_), channel_id=1, source_target_pairs={{0,8},{4,60},{8,16},{12,4},{16,24},{20,12},{24,32},{28,20},{32,40}... | collective-permute-start | bytes 196616 | tf_op jit(solution)/shard_map/ppermute | solution.py:45
  117.4 6.7 %collective-permute-start.25 = (bf16[256,1024]{1,0:T(8,128)(2,1)S(1)}, bf16[256,1024]{1,0:T(8,128)(2,1)S(1)}, u32[]{:S(2)}, u32[]{:S(2)}) collective-permute-start(bf16[256,1024]{1,0:T(8,128)(2,1)S(1)} %collective-permute-done.22.refs_1_), channel_id=1, source_target_pairs={{0,4},{4,0},{8,12},{12,8},{16,20},{20,16},{24,28},{28,24},{32,36},... | collective-permute-start | bytes 1572872 | tf_op jit(solution)/shard_map/ppermute | solution.py:45
  117.4 6.7 %collective-permute-start.24 = (bf16[256,1024]{1,0:T(8,128)(2,1)}, bf16[256,1024]{1,0:T(8,128)(2,1)S(1)}, u32[]{:S(2)}, u32[]{:S(2)}) collective-permute-start(bf16[256,1024]{1,0:T(8,128)(2,1)} %collective-permute-done.21.refs_0_), channel_id=1, source_target_pairs={{0,4},{4,0},{8,12},{12,8},{16,20},{20,16},{24,28},{28,24},{32,36},... | collective-permute-start | bytes 1572872 | tf_op jit(solution)/shard_map/ppermute | solution.py:45
  117.9 5.5 %collective-permute-start.26 = (bf16[32,1024]{1,0:T(8,128)(2,1)S(1)}, bf16[32,1024]{1,0:T(8,128)(2,1)S(1)}, u32[]{:S(2)}, u32[]{:S(2)}) collective-permute-start(bf16[32,1024]{1,0:T(8,128)(2,1)S(1)} %collective-permute-done.23.refs_2_), channel_id=1, source_target_pairs={{0,8},{4,60},{8,16},{12,4},{16,24},{20,12},{24,32},{28,20},{32,40}... | collective-permute-start | bytes 196616 | tf_op jit(solution)/shard_map/ppermute | solution.py:45
  124.1 15.5 %collective-permute-start.28 = (bf16[96,1024]{1,0:T(8,128)(2,1)}, bf16[96,1024]{1,0:T(8,128)(2,1)}, u32[]{:S(2)}, u32[]{:S(2)}) collective-permute-start(bf16[96,1024]{1,0:T(8,128)(2,1)} %pad_maximum_fusion), channel_id=1, source_target_pairs={{0,4},{4,0},{8,12},{12,8},{16,20},{20,16},{24,28},{28,24},{32,36},... | collective-permute-start | bytes 589832 | tf_op jit(solution)/shard_map/ppermute | solution.py:45
  127.2 33.2 %all-to-all-start.2 = ((bf16[4,64,1152]{2,1,0:T(8,128)(2,1)}), bf16[4,64,1152]{2,1,0:T(8,128)(2,1)S(1)}, u32[]{:S(2)}, u32[]{:S(2)}) async-start(bf16[4,64,1152]{2,1,0:T(8,128)(2,1)} %chosen_attention.7), calls=%async_computation.2 | async-start | bytes 1179648 | tf_op jit(solution)/shard_map/all_to_all | solution.py:350
  132.3 8.3 %collective-permute-start.27 = (bf16[32,1024]{1,0:T(8,128)(2,1)S(1)}, bf16[32,1024]{1,0:T(8,128)(2,1)S(1)}, u32[]{:S(2)}, u32[]{:S(2)}) collective-permute-start(bf16[32,1024]{1,0:T(8,128)(2,1)S(1)} %copy-done.11), channel_id=1, source_target_pairs={{0,8},{4,60},{8,16},{12,4},{16,24},{20,12},{24,32},{28,20},{32,40}... | collective-permute-start | bytes 196616 | tf_op jit(solution)/shard_map/ppermute | solution.py:45
  133.6 18.5 %collective-permute-start.18 = (bf16[128,1152]{1,0:T(8,128)(2,1)S(1)}, bf16[128,1152]{1,0:T(8,128)(2,1)S(1)}, u32[]{:S(2)}, u32[]{:S(2)}) collective-permute-start(bf16[128,1152]{1,0:T(8,128)(2,1)S(1)} %copy-done.18), channel_id=1, source_target_pairs={{0,64},{4,68},{8,72},{12,76},{16,80},{20,84},{24,88},{28,92},{32,9... | collective-permute-start | bytes 884744 | tf_op jit(solution)/shard_map/ppermute | solution.py:45
  137.0 15.1 %collective-permute-start.19 = (bf16[128,1152]{1,0:T(8,128)(2,1)S(1)}, bf16[128,1152]{1,0:T(8,128)(2,1)S(1)}, u32[]{:S(2)}, u32[]{:S(2)}) collective-permute-start(bf16[128,1152]{1,0:T(8,128)(2,1)S(1)} %copy-done.16), channel_id=1, source_target_pairs={{0,128},{4,132},{8,136},{12,140},{16,144},{20,148},{24,152},{28,15... | collective-permute-start | bytes 884744 | tf_op jit(solution)/shard_map/ppermute | solution.py:45
  138.9 13.2 %collective-permute-start.20 = (bf16[128,1152]{1,0:T(8,128)(2,1)S(1)}, bf16[128,1152]{1,0:T(8,128)(2,1)S(1)}, u32[]{:S(2)}, u32[]{:S(2)}) collective-permute-start(bf16[128,1152]{1,0:T(8,128)(2,1)S(1)} %copy-done.14), channel_id=1, source_target_pairs={{0,192},{4,196},{8,200},{12,204},{16,208},{20,212},{24,216},{28,22... | collective-permute-start | bytes 884744 | tf_op jit(solution)/shard_map/ppermute | solution.py:45
  142.5 5.1 %collective-permute-start.29 = (f32[256,64]{1,0:T(8,128)S(1)}, f32[256,64]{1,0:T(8,128)S(1)}, u32[]{:S(2)}, u32[]{:S(2)}) collective-permute-start(f32[256,64]{1,0:T(8,128)S(1)} %gate_share.1), channel_id=1, source_target_pairs={{0,1},{1,0},{2,3},{3,2},{4,5},{5,4},{6,7},{7,6},{8,9},{9,8},{10,11... | collective-permute-start | bytes 196616 | tf_op jit(solution)/shard_map/ppermute | solution.py:277
  147.6 12.1 %collective-permute-start.30 = (f32[256,64]{1,0:T(8,128)S(1)}, f32[256,64]{1,0:T(8,128)S(1)}, u32[]{:S(2)}, u32[]{:S(2)}) collective-permute-start(f32[256,64]{1,0:T(8,128)S(1)} %add.336), channel_id=1, source_target_pairs={{0,2},{1,3},{2,0},{3,1},{4,6},{5,7},{6,4},{7,5},{8,10},{9,11},{10,... | collective-permute-start | bytes 196616 | tf_op jit(solution)/shard_map/ppermute | solution.py:277
  (27 other events, 140.7 us)
Sparse Core Ops, SparseCore 0:
  10.2 36.4 all-gather.2

commit v2 on v0

v2 whole, which is shorter than its diff:
```python
import functools

import jax
import jax.numpy as jnp
from jax import lax
from jax.experimental import pallas as pl
from jax.experimental.pallas import tpu as pltpu
from jax.sharding import PartitionSpec as P

HEADS = 32
HD = 128
QT = 32
TOPK = 3
NY, NZ, NC = 4, 8, 2
NBLK = NY * NZ * NC
ROWS = 256
WIDTH = 1024
LOCAL = WIDTH // HD
TILES = ROWS // QT
HALF = LOCAL // 2
LANES = HALF * HD
EXT = LANES + 128
MEANS = 32
SCALE = HD ** -0.5
LOG2E = 1.4426950408889634
ABSENT = -1e30
PLACES = [(0, 0, 0), (0, 0, 1)]
for hop in (1, 2, 3):
    PLACES += [(hop, 0, 0), (hop, 0, 1), (hop, 1, 1), (hop, 1, 0)]
PLACES += [(4, 0, 0), (4, 1, 1)]
COLUMNS = [[(y * NZ + z) * NC + c for y in range(NY)] for z in range(NZ) for c in range(NC)]
PLANES = [[(y * NZ + z) * NC + c for z in range(NZ) for c in range(NC)] for y in range(NY)]


def at(y, z, c):
    return (y * NZ + z) * NC + c


def send(x, to):
    pairs = []
    for y in range(NY):
        for z in range(NZ):
            for c in range(NC):
                there = to(y, z, c)
                if 0 <= there[0] < NY:
                    pairs.append((at(y, z, c), at(there[0], there[1] % NZ, there[2])))
    return lax.ppermute(x, "seq", pairs)


def ring(x):
    return send(x, lambda y, z, c: (y, z + 1 - 2 * c, c))


def swap(x):
    return send(x, lambda y, z, c: (y, z, 1 - c))


def climb(x, steps):
    return send(x, lambda y, z, c: (y + steps, z, c))


def attend(q, k, v, ones, mask=None):
    scores = lax.dot_general(q, k, (((1,), (1,)), ((), ())), preferred_element_type=jnp.float32)
    if mask is not None:
        scores = jnp.where(mask, scores, -jnp.inf)
    top = jnp.max(scores, axis=1, keepdims=True)
    weights = jnp.exp2((scores - top) * (SCALE * LOG2E)).astype(jnp.bfloat16)
    both = jnp.dot(weights, jnp.concatenate([v, ones], axis=1), preferred_element_type=jnp.float32)
    return top * SCALE, both[:, :HD], both[:, HD:]


def own_kernel(q_ref, k_ref, v_ref, first_ref, second_ref, lse_ref):
    row = lax.broadcasted_iota(jnp.int32, (ROWS, ROWS), 0)
    col = lax.broadcasted_iota(jnp.int32, (ROWS, ROWS), 1)
    lane = lax.broadcasted_iota(jnp.int32, (ROWS, 128), 1)
    ones = jnp.ones((ROWS, HD), jnp.bfloat16)
    lse_ref[...] = jnp.zeros_like(lse_ref)

    @pl.loop(0, HALF)
    def _(h):
        for half, out_ref in enumerate((first_ref, second_ref)):
            wide = pl.ds(pl.multiple_of((half * HALF + h) * HD, HD), HD)
            top, mixed, total = attend(q_ref[:, wide], k_ref[:, wide], v_ref[:, wide], ones, col <= row)
            out_ref[:, pl.ds(pl.multiple_of(h * HD, HD), HD)] = mixed / total
            lse_ref[...] = jnp.where(lane == half * HALF + h, top + jnp.log(total), lse_ref[...])


def chosen_kernel(half, blocks, y_ref, idx_ref, *refs):
    arrays = max(a for a, _, _ in blocks) + 1
    queries, held, out_ref = refs[:NY], refs[NY:NY + arrays], refs[NY + arrays]
    kv, acc, tops, totals, sems = refs[NY + arrays + 1:]
    copies = []
    for n, (a, index, row) in enumerate(blocks):
        ref = held[a] if index is None else held[a].at[index]
        copies.append(pltpu.make_async_copy(ref.at[pl.ds(row, 2 * ROWS), :], kv.at[n], sems.at[n]))
    for copy in copies:
        copy.start()
    acc[...] = jnp.zeros_like(acc)
    tops[...] = jnp.full_like(tops, ABSENT)
    totals[...] = jnp.zeros_like(totals)
    ones = jnp.ones((ROWS, HD), jnp.bfloat16)

    @pl.loop(0, len(blocks) // 4)
    def _(some):
        for u in range(4):
            n = some * 4 + u
            pltpu.make_async_copy(kv.at[0], kv.at[n], sems.at[n]).wait()
        for u in range(4):
            n = some * 4 + u
            tiles, present = [], []
            for d in range(NY):
                choice = idx_ref[d, n]
                tiles.append(pl.ds(pl.multiple_of(jnp.maximum(choice, 0) * QT, QT), QT))
                present.append(choice >= 0)
            for h in range(HALF):
                cols = slice(h * HD, (h + 1) * HD)
                wide = slice(half * LANES + h * HD, half * LANES + (h + 1) * HD)
                q = jnp.concatenate([queries[d][tiles[d], wide] for d in range(NY)], axis=0)
                top, mixed, total = attend(q, kv[n, :ROWS, cols], kv[n, ROWS:, cols], ones)
                for d in range(NY):
                    mine = slice(d * QT, (d + 1) * QT)
                    before = tops[d, h, tiles[d], :]
                    now = jnp.where(present[d], top[mine], ABSENT)
                    peak = jnp.maximum(before, now)
                    old = jnp.exp(before - peak)
                    new = jnp.where(present[d], jnp.exp(now - peak), 0.0)
                    tops[d, h, tiles[d], :] = peak
                    totals[d, h, tiles[d], :] = old * totals[d, h, tiles[d], :] + new * total[mine]
                    acc[d, tiles[d], cols] = old * acc[d, tiles[d], cols] + new * mixed[mine]

    lane = lax.broadcasted_iota(jnp.int32, (ROWS, 128), 1)
    for d in range(NY):
        to = lax.rem(y_ref[0] + d, NY)
        spread = jnp.zeros((ROWS, 128), jnp.float32)
        for h in range(HALF):
            cols = slice(h * HD, (h + 1) * HD)
            total = totals[d, h]
            any_here = total > 0
            safe = jnp.where(any_here, total, 1.0)
            out_ref[to, :, cols] = (acc[d, :, cols] / safe).astype(jnp.bfloat16)
            lse = jnp.where(any_here, tops[d, h] + jnp.log(safe), ABSENT)
            spread = jnp.where(lane % HALF == h, lse, spread)
        high = spread.astype(jnp.bfloat16).astype(jnp.float32)
        rest = spread - high
        middle = rest.astype(jnp.bfloat16).astype(jnp.float32)
        parts = jnp.where(lane < HALF, high, jnp.where(lane < 2 * HALF, middle, rest - middle))
        parts = jnp.where(lane < 3 * HALF, parts, 0.0).astype(jnp.bfloat16)
        out_ref[to, :, LANES:] = parts


def combine_kernel(half, y_ref, own_ref, lse_ref, pieces_ref, *refs):
    out_ref = refs[-1]
    if half:
        out_ref[:, :LANES] = refs[0][...]

    @pl.loop(0, TILES)
    def _(t):
        rows = pl.ds(pl.multiple_of(t * QT, QT), QT)
        mine = lse_ref[rows, :]
        spreads = [pltpu.roll(mine, 128 - HALF, 1) if half else mine]
        for r in range(NY):
            parts = pieces_ref[r, rows, LANES:].astype(jnp.float32)
            spread = parts + pltpu.roll(parts, 128 - HALF, 1) + pltpu.roll(parts, 128 - 2 * HALF, 1)
            spreads.append(jnp.where(y_ref[0] >= r, spread, ABSENT))
        peak = functools.reduce(jnp.maximum, spreads)
        scales = [jnp.exp(spread - peak) for spread in spreads]
        total = functools.reduce(jnp.add, scales)
        scales = [scale / total for scale in scales]
        for h in range(HALF):
            cols = slice(h * HD, (h + 1) * HD)
            wide = slice(half * LANES + h * HD, half * LANES + (h + 1) * HD)
            mixed = scales[0][:, h:h + 1] * own_ref[rows, cols]
            for r in range(NY):
                mixed += scales[r + 1][:, h:h + 1] * pieces_ref[r, rows, cols].astype(jnp.float32)
            out_ref[rows, wide if half else cols] = mixed.astype(jnp.bfloat16)


def gate_kernel(order_ref, q_ref, means_ref, out_ref):
    share = lax.dot_general(
        q_ref[...], means_ref[...], (((1,), (1,)), ((), ())), preferred_element_type=jnp.float32
    )
    out_ref[...] = jnp.dot(
        share, order_ref[...], precision=lax.Precision.HIGHEST, preferred_element_type=jnp.float32
    ) * (1.0 / HEADS)


VMEM = pl.BlockSpec(memory_space=pltpu.VMEM)
SMEM = pl.BlockSpec(memory_space=pltpu.SMEM)
HBM = pl.BlockSpec(memory_space=pltpu.HBM)
PARAMS = pltpu.CompilerParams(vmem_limit_bytes=24 * 1024 * 1024)
WIDE = pltpu.CompilerParams(vmem_limit_bytes=60 * 1024 * 1024)
COST = pl.CostEstimate(flops=1, bytes_accessed=1, transcendentals=0)


def call(kernel, name, outs, in_specs, scratch=(), params=PARAMS):
    many = isinstance(outs, tuple)
    return pl.pallas_call(
        kernel,
        out_shape=outs,
        in_specs=in_specs,
        out_specs=(VMEM,) * len(outs) if many else VMEM,
        scratch_shapes=scratch,
        compiler_params=params,
        cost_estimate=COST,
        name=name,
    )


def own_attention(q, k, v):
    half = jax.ShapeDtypeStruct((ROWS, LANES), jnp.float32)
    outs = (half, half, jax.ShapeDtypeStruct((ROWS, 128), jnp.float32))
    return call(own_kernel, "own_attention", outs, [VMEM] * 3)(q, k, v)


def chosen_attention(half, here, idx, queries, arrays, blocks):
    return call(
        functools.partial(chosen_kernel, half, blocks),
        "chosen_attention",
        jax.ShapeDtypeStruct((NY, ROWS, EXT), jnp.bfloat16),
        [SMEM] * 2 + [VMEM] * NY + [HBM] * len(arrays),
        [
            pltpu.VMEM((len(blocks), 2 * ROWS, LANES), jnp.bfloat16),
            pltpu.VMEM((NY, ROWS, LANES), jnp.float32),
            pltpu.VMEM((NY, HALF, ROWS, 128), jnp.float32),
            pltpu.VMEM((NY, HALF, ROWS, 128), jnp.float32),
            pltpu.SemaphoreType.DMA((len(blocks),)),
        ],
        WIDE,
    )(here, idx, *queries, *arrays)


def combine(half, here, own_out, own_lse, pieces, *first):
    width = WIDTH if half else LANES
    return call(
        functools.partial(combine_kernel, half),
        "combine",
        jax.ShapeDtypeStruct((ROWS, width), jnp.bfloat16),
        [SMEM] + [VMEM] * (3 + len(first)),
    )(here, own_out, own_lse, pieces, *first)


def after(x, *others):
    return lax.optimization_barrier((x,) + others)[0] if others else x


def split(x):
    high = lax.reduce_precision(x, 8, 7)
    middle = lax.reduce_precision(x - high, 8, 7)
    return [high, middle, x - high - middle]


def over_heads(share):
    for bits in (1, 2):
        share = share + lax.ppermute(share, "head", [(i, i ^ bits) for i in range(4)])
    return share


def back(out):
    return lax.all_to_all(
        out, "seq", split_axis=0, concat_axis=0, tiled=True, axis_index_groups=COLUMNS
    )


def body(queries, keys, values, gating):
    me = lax.axis_index("seq")
    y, z, c = me // (NZ * NC), (me // NC) % NZ, me % NC
    here = y.reshape(1).astype(jnp.int32)
    sign = 2 * c - 1

    second = jnp.concatenate([keys[:, LANES:], values[:, LANES:]], axis=0)
    hops = [jnp.concatenate([second, swap(second)], axis=0)]
    hops += [ring(hops[0])]
    hops += [ring(hops[1])]
    first = jnp.concatenate([keys[:, :LANES], values[:, :LANES]], axis=0)
    gathered = lax.all_gather(first, "seq", axis_index_groups=PLANES)

    choices = jnp.zeros((16, WIDTH), jnp.bfloat16).at[:TILES, :TOPK].set(gating.astype(jnp.bfloat16))
    sent = jnp.concatenate([queries, choices], axis=0)
    sources = [sent] + [climb(sent, -d) for d in (1, 2, 3)]
    chosen = jnp.stack([x[ROWS:ROWS + TILES, :TOPK] for x in sources]).astype(jnp.int32)

    def tiles_of(blocks):
        hits = jnp.any(chosen[:, :, :, None] == blocks, axis=2)
        tile = jnp.max(jnp.where(hits, jnp.arange(TILES)[None, :, None], -1), axis=1)
        owner = me + jnp.arange(NY)[:, None] * (NZ * NC)
        return jnp.where(blocks[None, :] != owner, tile, -1).astype(jnp.int32)

    in_row = y * (NZ * NC) + jnp.arange(NZ * NC)
    in_ring = jnp.stack([
        (y * NZ + (z + (sign if chain == 0 else -sign) * hop) % NZ) * NC + (c ^ core)
        for hop, chain, core in PLACES
    ])
    idx_first, idx_second = tiles_of(in_row), tiles_of(in_ring)

    own_first, own_second, own_lse = own_attention(queries, keys, values)

    hops.append(ring(after(hops[2], own_lse, *sources)))
    mean = jnp.sum(keys, axis=0, dtype=jnp.float32).reshape(1, WIDTH) / ROWS
    means = jnp.concatenate([mean] + [climb(mean, d) for d in (1, 2, 3)], axis=0)
    means = jnp.concatenate(split(means) + [jnp.zeros((MEANS - 3 * NY, WIDTH), jnp.float32)], axis=0).astype(jnp.bfloat16)
    means = lax.all_gather(after(means, gathered), "seq", axis_index_groups=PLANES)
    r = jnp.arange(NZ * NC * MEANS)
    part, down = (r % MEANS) // NY, r % NY
    column = (y - down) * (NZ * NC) + r // MEANS
    column = jnp.where((part < 3) & (down <= y) & (column < me), column, -1)
    order = (column[:, None] == jnp.arange(NBLK)[None, :]).astype(jnp.float32)
    share = call(
        gate_kernel, "gate_share", jax.ShapeDtypeStruct((ROWS, NBLK), jnp.float32), [VMEM] * 3
    )(order, queries, means.reshape(NZ * NC * MEANS, WIDTH))
    gate_scores = over_heads(share)

    out_first = chosen_attention(
        0, here, idx_first, sources, [gathered], [(0, n, 0) for n in range(NZ * NC)]
    )
    back_first = back(out_first)
    hops[3] = after(hops[3], out_first)
    hops.append(ring(hops[3][:2 * ROWS]))
    others = [None] + [swap(x) for x in hops[1:]]
    arrays = [hops[0]] + [x for n in (1, 2, 3, 4) for x in (hops[n], others[n])]
    blocks = [(a, None, row) for a in range(7) for row in (0, 2 * ROWS)] + [(7, None, 0), (8, None, 0)]
    out_second = chosen_attention(1, here, after(idx_second, out_first), sources, arrays, blocks)
    back_second = back(out_second)
    attended = combine(0, here, own_first, own_lse, back_first)
    return combine(1, here, own_second, own_lse, back_second, attended), gate_scores


def solution(mesh):
    return jax.shard_map(
        body,
        mesh=mesh,
        in_specs=(P("seq", "head"), P("seq", "head"), P("seq", "head"), P("seq", None)),
        out_specs=(P("seq", "head"), P("seq", None)),
        check_vma=False,
    )
```

time: 404 us -> 159 us (0.39)
  blocking collectives: 128 us -> 0 us
  waiting for transfers between devices: 135 us -> 48.9 us
  local copies, waits for them, and re-layouts: 52.3 us -> 9.4 us
  matrix products: 30.9 us -> 0 us
  Pallas kernels: 0 us -> 29.1 us
  starting transfers between devices: 29.9 us -> 49.5 us
  other arithmetic: 11.2 us -> 5.3 us
    all_gather x1 -> x0, blocking collectives: 128 us -> none  [body(): lax.all_gather(local_mean.reshape(1, width), 'seq', axis=0, tiled=True)]
    all_to_all x3 -> x2, waiting for transfers between devices: 93.9 us -> 3.11 us  [back(): lax.all_to_all(out, 'seq', split_axis=0, concat_axis=0, tiled=True, axis_...]
    psum x1 -> x0, waiting for transfers between devices: 41.6 us -> none  [body(): gate_total = lax.psum(share, 'head')]
    ppermute x0 -> x17, waiting for transfers between devices: none -> 40.4 us  [the longest x15 37 us: send(): return lax.ppermute(x, 'seq', pairs)]
    ppermute x0 -> x17, starting transfers between devices: none -> 39.3 us  [the longest x15 34.5 us: send(): return lax.ppermute(x, 'seq', pairs)]
    dot_general x18 -> x0, matrix products: 30.9 us -> none  [the longest x5 20.5 us: attend(): jnp.einsum('hqk,khd->qhd', weights.astype(jnp.bfloat16), value_block, pre...]
    pallas_call x0 -> x6, Pallas kernels: none -> 29.1 us  [the longest x2 20.7 us: chosen_attention(): call(functools.partial(chosen_kernel, half, blocks), 'chosen_attention',...]
    all_to_all x3 -> x2, starting transfers between devices: 29.9 us -> 10.1 us  [back(): lax.all_to_all(out, 'seq', split_axis=0, concat_axis=0, tiled=True, axis_...]
  transfers between devices with their start and end apart: 4 -> 21, of which waited for: 2 -> 9; matrix products, arithmetic and copies ran while one was open for 6% -> 5% of each run, Pallas kernels for 0% -> 19%
where the time goes in v2:
time: 159 us; the launch traced here: 157 us
  starting transfers between devices  49.5 us (31%)
  waiting for transfers between devices  48.9 us (31%)
  Pallas kernels  29.1 us (18%)
  between operations  14.5 us (9%)
  local copies, waits for them, and re-layouts  9.4 us (6%)
  other arithmetic  5.3 us (3%)
    ppermute x15, waiting for transfers between devices, send(): return lax.ppermute(x, 'seq', pairs)  37 us
    ppermute x15, starting transfers between devices, send(): return lax.ppermute(x, 'seq', pairs)  34.5 us
    pallas_call x2, Pallas kernels, chosen_attention(): call(functools.partial(chosen_kernel, half, blocks), 'chosen_attention',...  20.7 us
    all_to_all x2, starting transfers between devices, back(): lax.all_to_all(out, 'seq', split_axis=0, concat_axis=0, tiled=True, axis_...  10.1 us
    all_gather x1, waiting for transfers between devices, body(): gathered = lax.all_gather(first, 'seq', axis_index_groups=PLANES)  5.4 us
    pallas_call x2, Pallas kernels, combine(): call(functools.partial(combine_kernel, half), 'combine', jax.ShapeDtypeSt...  5.18 us
    ppermute x2, starting transfers between devices, over_heads(): lax.ppermute(share, 'head', [(i, i ^ bits) for i in range(4)])  4.78 us
    unnamed x25, local copies, waits for them, and re-layouts  3.79 us
  transfers between devices with their start and end apart: 21, of which 9 were waited for; matrix products, arithmetic and copies ran while one was open for 5% of the time, Pallas kernels for 19%

profile of v2, /device:TPU:8, one launch (start us, length us, event | category | flops | bytes accessed | tf_op | source)
XLA Modules:
  0.0 156.8 jit_solution(5663851591785791455)
XLA Ops:
  7.2 1.1 fusion.22
  8.4 0.9 pad_maximum_fusion.1
  9.6 1.9 %collective-permute-done.3 = bf16[512,512]{1,0:T(8,128)(2,1)S(1)} collective-permute-done((bf16[512,512]{1,0:T(8,128)(2,1)S(1)}, bf16[512,512]{1,0:T(8,128)(2,1)S(1)}, u32[]{:S(2)}, u32[]{:S(2)}) %collective-permute-start.3) | collective-permute-done | bytes 524320 | tf_op jit(solution)/shard_map/ppermute | solution.py:47
  11.5 2.0 %collective-permute-start.4 = (bf16[1024,512]{1,0:T(8,128)(2,1)S(1)}, bf16[1024,512]{1,0:T(8,128)(2,1)}, u32[]{:S(2)}, u32[]{:S(2)}) collective-permute-start(bf16[1024,512]{1,0:T(8,128)(2,1)S(1)} %pad_maximum_fusion.refs_4_), channel_id=1, source_target_pairs={{0,8},{4,60},{8,16},{12,4},{16,24},{20,12},{24,32},{28,20},{32,40}... | collective-permute-start | bytes 3145736 | tf_op jit(solution)/shard_map/ppermute | solution.py:47
  13.5 22.0 %collective-permute-done.4.refs_5_ = bf16[1024,512]{1,0:T(8,128)(2,1)} collective-permute-done((bf16[1024,512]{1,0:T(8,128)(2,1)S(1)}, bf16[1024,512]{1,0:T(8,128)(2,1)}, u32[]{:S(2)}, u32[]{:S(2)}) %collective-permute-start.4) | collective-permute-done | bytes 1048608 | tf_op jit(solution)/shard_map/ppermute | solution.py:47
  35.6 0.9 fusion.1.refs_0_
  36.5 1.5 collective-permute-start.2
  38.0 1.3 collective-permute-start.1
  39.2 2.0 %collective-permute-start = (bf16[272,1024]{1,0:T(8,128)(2,1)}, bf16[272,1024]{1,0:T(8,128)(2,1)}, u32[]{:S(2)}, u32[]{:S(2)}) collective-permute-start(bf16[272,1024]{1,0:T(8,128)(2,1)} %fusion.1.refs_0_), channel_id=1, source_target_pairs={{64,0},{68,4},{72,8},{76,12},{80,16},{84,20},{88,24},{92,28},{96,3... | collective-permute-start | bytes 1671176 | tf_op jit(solution)/shard_map/ppermute | solution.py:47
  42.0 2.0 %own_attention.1 = (f32[256,512]{1,0:T(8,128)S(1)}, f32[256,512]{1,0:T(8,128)S(1)}, f32[256,128]{1,0:T(8,128)S(1)}) custom-call(bf16[256,1024]{1,0:T(8,128)(2,1)S(1)} %copy-done.1, bf16[256,1024]{1,0:T(8,128)(2,1)S(1)} %copy-done, bf16[256,1024]{1,0:T(8,128)(2,1)S(1)} %copy-done.2), custom_call_target="tpu_custom_call" | custom-call | flops 1 | bytes 1 | tf_op jit(solution)/shard_map/own_attention/pallas_call | solution.py:212
  44.1 22.0 %collective-permute-start.13 = (f32[1,1024]{1,0:T(1,128)S(1)}, f32[1,1024]{1,0:T(1,128)S(1)}, u32[]{:S(2)}, u32[]{:S(2)}) collective-permute-start(f32[1,1024]{1,0:T(1,128)S(1)} %bitcast.26), channel_id=1, source_target_pairs={{0,128},{4,132},{8,136},{12,140},{16,144},{20,148},{24,152},{28,15... | collective-permute-start | bytes 12296 | tf_op jit(solution)/shard_map/ppermute | solution.py:47
  66.1 1.9 %collective-permute-start.12 = (f32[1,1024]{1,0:T(1,128)S(1)}, f32[1,1024]{1,0:T(1,128)S(1)}, u32[]{:S(2)}, u32[]{:S(2)}) collective-permute-start(f32[1,1024]{1,0:T(1,128)S(1)} %bitcast.27), channel_id=1, source_target_pairs={{0,64},{4,68},{8,72},{12,76},{16,80},{20,84},{24,88},{28,92},{32,9... | collective-permute-start | bytes 12296 | tf_op jit(solution)/shard_map/ppermute | solution.py:47
  68.3 6.0 %collective-permute-done.6.refs_7_ = bf16[1024,512]{1,0:T(8,128)(2,1)} collective-permute-done((bf16[1024,512]{1,0:T(8,128)(2,1)}, bf16[1024,512]{1,0:T(8,128)(2,1)}, u32[]{:S(2)}, u32[]{:S(2)}) %collective-permute-start.6) | collective-permute-done | bytes 1048608 | tf_op jit(solution)/shard_map/ppermute | solution.py:47
  77.9 5.4 %all-gather.5.cloned.1.call-done = bf16[8192,512]{1,0:T(8,128)(2,1)} async-done(((bf16[512,512]{1,0:T(8,128)(2,1)}), bf16[8192,512]{1,0:T(8,128)(2,1)}) %all-gather.5.cloned.1.call-update) | async-done | bytes 8388624 | tf_op jit(solution)/shard_map/all_gather | solution.py:275
  84.7 10.4 %chosen_attention.2 = bf16[4,256,640]{2,1,0:T(8,128)(2,1)} custom-call(s32[1]{0:T(128)} %bitcast.y_ref, s32[4,16]{1,0:T(4,128)} %get-tuple-element.43.idx_ref, bf16[272,1024]{1,0:T(8,128)(2,1)} %fusion.1.refs_0_, bf16[272,1024]{1,0:T(8,128)(2,1)} %collective-permute-done.refs_1_, bf16[272,1024]{1,0:T(8,128)(2,1)} %collective-permute-done.1.refs_2_, ...), custom_call_target="tpu_custom_call" | custom-call | flops 1 | bytes 1 | tf_op jit(solution)/shard_map/chosen_attention/pallas_call | solution.py:216
  95.1 1.9 %slice.52 = bf16[512,512]{1,0:T(8,128)(2,1)} slice(bf16[1024,512]{1,0:T(8,128)(2,1)} %collective-permute-done.8.refs_9_), slice={[0:512], [0:512]} | slice | bytes 1048576 | tf_op jit(solution)/shard_map/slice | solution.py:317
  97.0 2.4 %collective-permute-start.9 = (bf16[1024,512]{1,0:T(8,128)(2,1)}, bf16[1024,512]{1,0:T(8,128)(2,1)S(1)}, u32[]{:S(2)}, u32[]{:S(2)}) collective-permute-start(bf16[1024,512]{1,0:T(8,128)(2,1)} %collective-permute-done.8.refs_9_), channel_id=1, source_target_pairs={{0,4},{4,0},{8,12},{12,8},{16,20},{20,16},{24,28},{28,24},{32,36},... | collective-permute-start | bytes 3145736 | tf_op jit(solution)/shard_map/ppermute | solution.py:47
  99.4 4.8 %all-to-all-start.1 = ((bf16[4,256,640]{2,1,0:T(8,128)(2,1)}), bf16[4,256,640]{2,1,0:T(8,128)(2,1)S(1)}, u32[]{:S(2)}, u32[]{:S(2)}) async-start(bf16[4,256,640]{2,1,0:T(8,128)(2,1)} %chosen_attention.2), calls=%async_computation.1 | async-start | bytes 2621440 | tf_op jit(solution)/shard_map/all_to_all | solution.py:259
  104.2 4.7 %collective-permute-done.10.refs_11_ = bf16[512,512]{1,0:T(8,128)(2,1)} collective-permute-done((bf16[512,512]{1,0:T(8,128)(2,1)}, bf16[512,512]{1,0:T(8,128)(2,1)}, u32[]{:S(2)}, u32[]{:S(2)}) %collective-permute-start.10) | collective-permute-done | bytes 524320 | tf_op jit(solution)/shard_map/ppermute | solution.py:47
  108.9 2.1 %collective-permute-done.11.refs_12_ = bf16[512,512]{1,0:T(8,128)(2,1)S(1)} collective-permute-done((bf16[512,512]{1,0:T(8,128)(2,1)}, bf16[512,512]{1,0:T(8,128)(2,1)S(1)}, u32[]{:S(2)}, u32[]{:S(2)}) %collective-permute-start.11) | collective-permute-done | bytes 524320 | tf_op jit(solution)/shard_map/ppermute | solution.py:47
  111.8 1.0 copy-done.9
  112.8 10.4 %chosen_attention.3 = bf16[4,256,640]{2,1,0:T(8,128)(2,1)} custom-call(s32[1]{0:T(128)} %bitcast.y_ref, s32[4,16]{1,0:T(4,128)} %get-tuple-element.23.idx_ref, bf16[272,1024]{1,0:T(8,128)(2,1)} %fusion.1.refs_0_, bf16[272,1024]{1,0:T(8,128)(2,1)} %collective-permute-done.refs_1_, bf16[272,1024]{1,0:T(8,128)(2,1)} %collective-permute-done.1.refs_2_, ...), custom_call_target="tpu_custom_call" | custom-call | flops 1 | bytes 1 | tf_op jit(solution)/shard_map/chosen_attention/pallas_call | solution.py:216
  123.1 5.3 %all-to-all-start = ((bf16[4,256,640]{2,1,0:T(8,128)(2,1)}), bf16[4,256,640]{2,1,0:T(8,128)(2,1)S(1)}, u32[]{:S(2)}, u32[]{:S(2)}) async-start(bf16[4,256,640]{2,1,0:T(8,128)(2,1)} %chosen_attention.3), calls=%async_computation | async-start | bytes 2621440 | tf_op jit(solution)/shard_map/all_to_all | solution.py:259
  128.7 1.2 copy-done.3
  129.9 1.2 gate_share.1
  131.1 1.7 %collective-permute-start.15 = (f32[256,64]{1,0:T(8,128)S(1)}, f32[256,64]{1,0:T(8,128)S(1)}, u32[]{:S(2)}, u32[]{:S(2)}) collective-permute-start(f32[256,64]{1,0:T(8,128)S(1)} %gate_share.1), channel_id=1, source_target_pairs={{0,1},{1,0},{2,3},{3,2},{4,5},{5,4},{6,7},{7,6},{8,9},{9,8},{10,11... | collective-permute-start | bytes 196616 | tf_op jit(solution)/shard_map/ppermute | solution.py:254
  132.8 3.4 %collective-permute-done.15 = f32[256,64]{1,0:T(8,128)S(1)} collective-permute-done((f32[256,64]{1,0:T(8,128)S(1)}, f32[256,64]{1,0:T(8,128)S(1)}, u32[]{:S(2)}, u32[]{:S(2)}) %collective-permute-start.15) | collective-permute-done | bytes 65568 | tf_op jit(solution)/shard_map/ppermute | solution.py:254
  136.8 3.1 %collective-permute-start.16 = (f32[256,64]{1,0:T(8,128)}, f32[256,64]{1,0:T(8,128)}, u32[]{:S(2)}, u32[]{:S(2)}) collective-permute-start(f32[256,64]{1,0:T(8,128)} %add.281), channel_id=1, source_target_pairs={{0,2},{1,3},{2,0},{3,1},{4,6},{5,7},{6,4},{7,5},{8,10},{9,11},{10,... | collective-permute-start | bytes 196616 | tf_op jit(solution)/shard_map/ppermute | solution.py:254
  139.9 2.2 %combine.2.refs_0_ = bf16[256,512]{1,0:T(8,128)(2,1)S(1)} custom-call(s32[1]{0:T(128)} %bitcast.y_ref, f32[256,512]{1,0:T(8,128)S(1)} %copy-done.5, f32[256,128]{1,0:T(8,128)S(1)} %get-tuple-element.22.lse_ref, bf16[4,256,640]{2,1,0:T(8,128)(2,1)S(1)} %all-to-all-done.1.pieces_ref), custom_call_target="tpu_custom_call" | custom-call | flops 1 | bytes 1 | tf_op jit(solution)/shard_map/combine/pallas_call | solution.py:234
  142.1 3.1 %all-to-all-done.pieces_ref = bf16[4,256,640]{2,1,0:T(8,128)(2,1)S(1)} async-done(((bf16[4,256,640]{2,1,0:T(8,128)(2,1)}), bf16[4,256,640]{2,1,0:T(8,128)(2,1)S(1)}, u32[]{:S(2)}, u32[]{:S(2)}) %all-to-all-start) | async-done | bytes 1310752 | tf_op jit(solution)/shard_map/all_to_all | solution.py:259
  145.2 3.0 %combine.3 = bf16[256,1024]{1,0:T(8,128)(2,1)} custom-call(s32[1]{0:T(128)} %bitcast.y_ref, f32[256,512]{1,0:T(8,128)S(1)} %copy-done.7, f32[256,128]{1,0:T(8,128)S(1)} %get-tuple-element.22.lse_ref, bf16[4,256,640]{2,1,0:T(8,128)(2,1)S(1)} %all-to-all-done.pieces_ref, bf16[256,512]{1,0:T(8,128)(2,1)S(1)} %combine.2.refs_0_), custom_call_target="tpu_custom_call" | custom-call | flops 1 | bytes 1 | tf_op jit(solution)/shard_map/combine/pallas_call | solution.py:234
  148.2 1.0 add.282
  (76 shorter events, 8.7 us)
Async XLA Ops:
  7.2 1.2 copy-start
  7.2 76.1 %all-gather.5.cloned.1.call-start = ((), (), s32[]{:S(2)}) async-start(), calls=%async_computation.2 | async-start | bytes 8912896 | tf_op jit(solution)/shard_map/all_gather | solution.py:275
  9.3 119.3 %all-gather.7.cloned.1.call-start = ((), (), s32[]{:S(2)}) async-start(), calls=%async_computation.3 | async-start | bytes 1114112 | tf_op jit(solution)/shard_map/all_gather | solution.py:301
  9.4 26.1 %copy-start.11 = (s32[8,3]{0,1:T(4,128)S(1)}, s32[8,3]{0,1:T(4,128)}, u32[]{:S(2)}) copy-start(s32[8,3]{0,1:T(4,128)} %param.9) | copy-start | bytes 292
  9.4 26.2 %copy-start.1 = (bf16[256,1024]{1,0:T(8,128)(2,1)S(1)}, bf16[256,1024]{1,0:T(8,128)(2,1)}, u32[]{:S(2)}) copy-start(bf16[256,1024]{1,0:T(8,128)(2,1)} %q_ref.3) | copy-start | bytes 1572868
  9.5 2.0 %collective-permute-start.3 = (bf16[512,512]{1,0:T(8,128)(2,1)S(1)}, bf16[512,512]{1,0:T(8,128)(2,1)S(1)}, u32[]{:S(2)}, u32[]{:S(2)}) collective-permute-start(bf16[512,512]{1,0:T(8,128)(2,1)S(1)} %pad_maximum_fusion.2), channel_id=1, source_target_pairs={{0,4},{4,0},{8,12},{12,8},{16,20},{20,16},{24,28},{28,24},{32,36},... | collective-permute-start | bytes 1572872 | tf_op jit(solution)/shard_map/ppermute | solution.py:47
  11.5 29.8 %copy-start.8 = (bf16[1024,512]{1,0:T(8,128)(2,1)}, bf16[1024,512]{1,0:T(8,128)(2,1)S(1)}, u32[]{:S(2)}) copy-start(bf16[1024,512]{1,0:T(8,128)(2,1)S(1)} %pad_maximum_fusion.refs_4_) | copy-start | bytes 3145732
  11.5 30.5 %copy-start.2 = (bf16[256,1024]{1,0:T(8,128)(2,1)S(1)}, bf16[256,1024]{1,0:T(8,128)(2,1)}, u32[]{:S(2)}) copy-start(bf16[256,1024]{1,0:T(8,128)(2,1)} %v_ref.1) | copy-start | bytes 1572868
  11.5 24.0 %collective-permute-start.4 = (bf16[1024,512]{1,0:T(8,128)(2,1)S(1)}, bf16[1024,512]{1,0:T(8,128)(2,1)}, u32[]{:S(2)}, u32[]{:S(2)}) collective-permute-start(bf16[1024,512]{1,0:T(8,128)(2,1)S(1)} %pad_maximum_fusion.refs_4_), channel_id=1, source_target_pairs={{0,8},{4,60},{8,16},{12,4},{16,24},{20,12},{24,32},{28,20},{32,40}... | collective-permute-start | bytes 3145736 | tf_op jit(solution)/shard_map/ppermute | solution.py:47
  35.5 38.9 %collective-permute-start.6 = (bf16[1024,512]{1,0:T(8,128)(2,1)}, bf16[1024,512]{1,0:T(8,128)(2,1)}, u32[]{:S(2)}, u32[]{:S(2)}) collective-permute-start(bf16[1024,512]{1,0:T(8,128)(2,1)} %collective-permute-done.4.refs_5_), channel_id=1, source_target_pairs={{0,8},{4,60},{8,16},{12,4},{16,24},{20,12},{24,32},{28,20},{32,40}... | collective-permute-start | bytes 3145736 | tf_op jit(solution)/shard_map/ppermute | solution.py:47
  36.5 7.6 %collective-permute-start.2 = (bf16[272,1024]{1,0:T(8,128)(2,1)}, bf16[272,1024]{1,0:T(8,128)(2,1)}, u32[]{:S(2)}, u32[]{:S(2)}) collective-permute-start(bf16[272,1024]{1,0:T(8,128)(2,1)} %fusion.1.refs_0_), channel_id=1, source_target_pairs={{192,0},{196,4},{200,8},{204,12},{208,16},{212,20},{216,24},{220,2... | collective-permute-start | bytes 1671176 | tf_op jit(solution)/shard_map/ppermute | solution.py:47
  38.0 28.1 %collective-permute-start.1 = (bf16[272,1024]{1,0:T(8,128)(2,1)}, bf16[272,1024]{1,0:T(8,128)(2,1)}, u32[]{:S(2)}, u32[]{:S(2)}) collective-permute-start(bf16[272,1024]{1,0:T(8,128)(2,1)} %fusion.1.refs_0_), channel_id=1, source_target_pairs={{128,0},{132,4},{136,8},{140,12},{144,16},{148,20},{152,24},{156,2... | collective-permute-start | bytes 1671176 | tf_op jit(solution)/shard_map/ppermute | solution.py:47
  39.2 29.1 %collective-permute-start = (bf16[272,1024]{1,0:T(8,128)(2,1)}, bf16[272,1024]{1,0:T(8,128)(2,1)}, u32[]{:S(2)}, u32[]{:S(2)}) collective-permute-start(bf16[272,1024]{1,0:T(8,128)(2,1)} %fusion.1.refs_0_), channel_id=1, source_target_pairs={{64,0},{68,4},{72,8},{76,12},{80,16},{84,20},{88,24},{92,28},{96,3... | collective-permute-start | bytes 1671176 | tf_op jit(solution)/shard_map/ppermute | solution.py:47
  41.4 33.3 %collective-permute-start.14 = (f32[1,1024]{1,0:T(1,128)S(1)}, f32[1,1024]{1,0:T(1,128)S(1)}, u32[]{:S(2)}, u32[]{:S(2)}) collective-permute-start(f32[1,1024]{1,0:T(1,128)S(1)} %bitcast.25), channel_id=1, source_target_pairs={{0,192},{4,196},{8,200},{12,204},{16,208},{20,212},{24,216},{28,22... | collective-permute-start | bytes 12296 | tf_op jit(solution)/shard_map/ppermute | solution.py:47
  44.1 51.0 %copy-start.4 = (f32[256,512]{1,0:T(8,128)}, f32[256,512]{1,0:T(8,128)S(1)}, u32[]{:S(2)}) copy-start(f32[256,512]{1,0:T(8,128)S(1)} %get-tuple-element.26.own_ref) | copy-start | bytes 1572868
  44.1 51.0 %copy-start.6 = (f32[256,512]{1,0:T(8,128)}, f32[256,512]{1,0:T(8,128)S(1)}, u32[]{:S(2)}) copy-start(f32[256,512]{1,0:T(8,128)S(1)} %get-tuple-element.21.own_ref) | copy-start | bytes 1572868
  44.1 30.5 %collective-permute-start.13 = (f32[1,1024]{1,0:T(1,128)S(1)}, f32[1,1024]{1,0:T(1,128)S(1)}, u32[]{:S(2)}, u32[]{:S(2)}) collective-permute-start(f32[1,1024]{1,0:T(1,128)S(1)} %bitcast.26), channel_id=1, source_target_pairs={{0,128},{4,132},{8,136},{12,140},{16,144},{20,148},{24,152},{28,15... | collective-permute-start | bytes 12296 | tf_op jit(solution)/shard_map/ppermute | solution.py:47
  66.1 8.6 %collective-permute-start.12 = (f32[1,1024]{1,0:T(1,128)S(1)}, f32[1,1024]{1,0:T(1,128)S(1)}, u32[]{:S(2)}, u32[]{:S(2)}) collective-permute-start(f32[1,1024]{1,0:T(1,128)S(1)} %bitcast.27), channel_id=1, source_target_pairs={{0,64},{4,68},{8,72},{12,76},{16,80},{20,84},{24,88},{28,92},{32,9... | collective-permute-start | bytes 12296 | tf_op jit(solution)/shard_map/ppermute | solution.py:47
  74.3 20.7 %collective-permute-start.8 = (bf16[1024,512]{1,0:T(8,128)(2,1)}, bf16[1024,512]{1,0:T(8,128)(2,1)}, u32[]{:S(2)}, u32[]{:S(2)}) collective-permute-start(bf16[1024,512]{1,0:T(8,128)(2,1)} %collective-permute-done.6.refs_7_), channel_id=1, source_target_pairs={{0,8},{4,60},{8,16},{12,4},{16,24},{20,12},{24,32},{28,20},{32,40}... | collective-permute-start | bytes 3145736 | tf_op jit(solution)/shard_map/ppermute | solution.py:47
  84.0 24.9 %collective-permute-start.5 = (bf16[1024,512]{1,0:T(8,128)(2,1)}, bf16[1024,512]{1,0:T(8,128)(2,1)}, u32[]{:S(2)}, u32[]{:S(2)}) collective-permute-start(bf16[1024,512]{1,0:T(8,128)(2,1)} %collective-permute-done.4.refs_5_), channel_id=1, source_target_pairs={{0,4},{4,0},{8,12},{12,8},{16,20},{20,16},{24,28},{28,24},{32,36},... | collective-permute-start | bytes 3145736 | tf_op jit(solution)/shard_map/ppermute | solution.py:47
  84.7 24.1 %collective-permute-start.7 = (bf16[1024,512]{1,0:T(8,128)(2,1)}, bf16[1024,512]{1,0:T(8,128)(2,1)}, u32[]{:S(2)}, u32[]{:S(2)}) collective-permute-start(bf16[1024,512]{1,0:T(8,128)(2,1)} %collective-permute-done.6.refs_7_), channel_id=1, source_target_pairs={{0,4},{4,0},{8,12},{12,8},{16,20},{20,16},{24,28},{28,24},{32,36},... | collective-permute-start | bytes 3145736 | tf_op jit(solution)/shard_map/ppermute | solution.py:47
  97.0 11.8 %collective-permute-start.10 = (bf16[512,512]{1,0:T(8,128)(2,1)}, bf16[512,512]{1,0:T(8,128)(2,1)}, u32[]{:S(2)}, u32[]{:S(2)}) collective-permute-start(bf16[512,512]{1,0:T(8,128)(2,1)} %slice.52), channel_id=1, source_target_pairs={{0,8},{4,60},{8,16},{12,4},{16,24},{20,12},{24,32},{28,20},{32,40}... | collective-permute-start | bytes 1572872 | tf_op jit(solution)/shard_map/ppermute | solution.py:47
  97.0 14.0 %collective-permute-start.9 = (bf16[1024,512]{1,0:T(8,128)(2,1)}, bf16[1024,512]{1,0:T(8,128)(2,1)S(1)}, u32[]{:S(2)}, u32[]{:S(2)}) collective-permute-start(bf16[1024,512]{1,0:T(8,128)(2,1)} %collective-permute-done.8.refs_9_), channel_id=1, source_target_pairs={{0,4},{4,0},{8,12},{12,8},{16,20},{20,16},{24,28},{28,24},{32,36},... | collective-permute-start | bytes 3145736 | tf_op jit(solution)/shard_map/ppermute | solution.py:47
  99.4 23.8 %all-to-all-start.1 = ((bf16[4,256,640]{2,1,0:T(8,128)(2,1)}), bf16[4,256,640]{2,1,0:T(8,128)(2,1)S(1)}, u32[]{:S(2)}, u32[]{:S(2)}) async-start(bf16[4,256,640]{2,1,0:T(8,128)(2,1)} %chosen_attention.2), calls=%async_computation.1 | async-start | bytes 2621440 | tf_op jit(solution)/shard_map/all_to_all | solution.py:259
  108.8 2.1 %collective-permute-start.11 = (bf16[512,512]{1,0:T(8,128)(2,1)}, bf16[512,512]{1,0:T(8,128)(2,1)S(1)}, u32[]{:S(2)}, u32[]{:S(2)}) collective-permute-start(bf16[512,512]{1,0:T(8,128)(2,1)} %collective-permute-done.10.refs_11_), channel_id=1, source_target_pairs={{0,4},{4,0},{8,12},{12,8},{16,20},{20,16},{24,28},{28,24},{32,36},... | collective-permute-start | bytes 1572872 | tf_op jit(solution)/shard_map/ppermute | solution.py:47
  111.8 1.0 copy-start.9
  123.1 22.1 %all-to-all-start = ((bf16[4,256,640]{2,1,0:T(8,128)(2,1)}), bf16[4,256,640]{2,1,0:T(8,128)(2,1)S(1)}, u32[]{:S(2)}, u32[]{:S(2)}) async-start(bf16[4,256,640]{2,1,0:T(8,128)(2,1)} %chosen_attention.3), calls=%async_computation | async-start | bytes 2621440 | tf_op jit(solution)/shard_map/all_to_all | solution.py:259
  128.7 1.2 copy-start.3
  129.9 10.1 %copy-start.5 = (f32[256,512]{1,0:T(8,128)S(1)}, f32[256,512]{1,0:T(8,128)}, u32[]{:S(2)}) copy-start(f32[256,512]{1,0:T(8,128)} %copy-done.4) | copy-start | bytes 1572868
  131.1 14.2 %copy-start.7 = (f32[256,512]{1,0:T(8,128)S(1)}, f32[256,512]{1,0:T(8,128)}, u32[]{:S(2)}) copy-start(f32[256,512]{1,0:T(8,128)} %copy-done.6) | copy-start | bytes 1572868
  131.1 5.1 %collective-permute-start.15 = (f32[256,64]{1,0:T(8,128)S(1)}, f32[256,64]{1,0:T(8,128)S(1)}, u32[]{:S(2)}, u32[]{:S(2)}) collective-permute-start(f32[256,64]{1,0:T(8,128)S(1)} %gate_share.1), channel_id=1, source_target_pairs={{0,1},{1,0},{2,3},{3,2},{4,5},{5,4},{6,7},{7,6},{8,9},{9,8},{10,11... | collective-permute-start | bytes 196616 | tf_op jit(solution)/shard_map/ppermute | solution.py:254
  136.8 11.4 %collective-permute-start.16 = (f32[256,64]{1,0:T(8,128)}, f32[256,64]{1,0:T(8,128)}, u32[]{:S(2)}, u32[]{:S(2)}) collective-permute-start(f32[256,64]{1,0:T(8,128)} %add.281), channel_id=1, source_target_pairs={{0,2},{1,3},{2,0},{3,1},{4,6},{5,7},{6,4},{7,5},{8,10},{9,11},{10,... | collective-permute-start | bytes 196616 | tf_op jit(solution)/shard_map/ppermute | solution.py:254
  (1 other events, 0.8 us)
Sparse Core Ops, SparseCore 0:
  9.8 73.4 all-gather.4
  85.7 39.4 all-gather.6

commit v3 on v2

--- a/solution.py
+++ b/solution.py
@@ -294,10 +294,12 @@
 
     own_first, own_second, own_lse = own_attention(queries, keys, values)
 
-    hops.append(ring(after(hops[2], own_lse, *sources)))
     mean = jnp.sum(keys, axis=0, dtype=jnp.float32).reshape(1, WIDTH) / ROWS
     means = jnp.concatenate([mean] + [climb(mean, d) for d in (1, 2, 3)], axis=0)
     means = jnp.concatenate(split(means) + [jnp.zeros((MEANS - 3 * NY, WIDTH), jnp.float32)], axis=0).astype(jnp.bfloat16)
+    ready = after(hops[2], own_lse, means, *sources)
+    same, cross = ring(ready[:2 * ROWS]), ring(ready[2 * ROWS:])
+
     means = lax.all_gather(after(means, gathered), "seq", axis_index_groups=PLANES)
     r = jnp.arange(NZ * NC * MEANS)
     part, down = (r % MEANS) // NY, r % NY
@@ -313,15 +315,16 @@
         0, here, idx_first, sources, [gathered], [(0, n, 0) for n in range(NZ * NC)]
     )
     back_first = back(out_first)
-    hops[3] = after(hops[3], out_first)
-    hops.append(ring(hops[3][:2 * ROWS]))
-    others = [None] + [swap(x) for x in hops[1:]]
-    arrays = [hops[0]] + [x for n in (1, 2, 3, 4) for x in (hops[n], others[n])]
-    blocks = [(a, None, row) for a in range(7) for row in (0, 2 * ROWS)] + [(7, None, 0), (8, None, 0)]
+    same, cross = after(same, out_first), after(cross, out_first)
+    last = ring(same)
+    before = [swap(after(hops[n], out_first)) for n in (1, 2)]
+    arrays = [hops[0], hops[1], before[0], hops[2], before[1]]
+    arrays += [same, cross, swap(same), swap(cross), last, swap(last)]
+    blocks = [(a, None, row) for a in range(5) for row in (0, 2 * ROWS)] + [(a, None, 0) for a in range(5, 11)]
     out_second = chosen_attention(1, here, after(idx_second, out_first), sources, arrays, blocks)
     back_second = back(out_second)
     attended = combine(0, here, own_first, own_lse, back_first)
-    return combine(1, here, own_second, own_lse, back_second, attended), gate_scores
+    return combine(1, after(here, gate_scores), own_second, own_lse, back_second, attended), gate_scores
 
 
 def solution(mesh):

time: 159 us -> 154 us (0.969)
  starting transfers between devices: 49.5 us -> 37.6 us
  waiting for transfers between devices: 48.9 us -> 58.6 us
  other arithmetic: 5.3 us -> 3.64 us
    ppermute x15 -> x17, starting transfers between devices: 34.5 us -> 23.3 us  [send(): return lax.ppermute(x, 'seq', pairs)]
    ppermute x15 -> x17, waiting for transfers between devices: 37 us -> 45.8 us  [send(): return lax.ppermute(x, 'seq', pairs)]
    add x2, other arithmetic: 1.64 us -> 0.04 us  [over_heads(): share + lax.ppermute(share, 'head', [(i, i ^ bits) for i in range(4)])]
    unnamed x25 -> x27, local copies, waits for them, and re-layouts: 3.79 us -> 2.79 us
  transfers between devices with their start and end apart: 21 -> 23, of which waited for: 9 -> 11; matrix products, arithmetic and copies ran while one was open for 5% -> 5% of each run, Pallas kernels for 19% -> 17%
where the time goes in v3:
time: 154 us; the launch traced here: 152 us
  waiting for transfers between devices  58.6 us (38%)
  starting transfers between devices  37.6 us (24%)
  Pallas kernels  29.1 us (19%)
  between operations  14.7 us (10%)
  local copies, waits for them, and re-layouts  8.53 us (6%)
  other arithmetic  3.64 us (2%)
    ppermute x17, waiting for transfers between devices, send(): return lax.ppermute(x, 'seq', pairs)  45.8 us
    ppermute x17, starting transfers between devices, send(): return lax.ppermute(x, 'seq', pairs)  23.3 us
    pallas_call x2, Pallas kernels, chosen_attention(): call(functools.partial(chosen_kernel, half, blocks), 'chosen_attention',...  20.7 us
    all_to_all x2, starting transfers between devices, back(): lax.all_to_all(out, 'seq', split_axis=0, concat_axis=0, tiled=True, axis_...  9.65 us
    all_gather x1, waiting for transfers between devices, body(): gathered = lax.all_gather(first, 'seq', axis_index_groups=PLANES)  6.08 us
    pallas_call x2, Pallas kernels, combine(): call(functools.partial(combine_kernel, half), 'combine', jax.ShapeDtypeSt...  5.18 us
    ppermute x2, waiting for transfers between devices, over_heads(): lax.ppermute(share, 'head', [(i, i ^ bits) for i in range(4)])  4.82 us
    ppermute x2, starting transfers between devices, over_heads(): lax.ppermute(share, 'head', [(i, i ^ bits) for i in range(4)])  4.62 us
  transfers between devices with their start and end apart: 23, of which 11 were waited for; matrix products, arithmetic and copies ran while one was open for 5% of the time, Pallas kernels for 17%

profile of v3, /device:TPU:8, one launch (start us, length us, event | category | flops | bytes accessed | tf_op | source)
XLA Modules:
  0.0 152.1 jit_solution(5643751461185535511)
XLA Ops:
  7.2 1.1 fusion.23
  9.5 1.9 %collective-permute-done.8 = bf16[512,512]{1,0:T(8,128)(2,1)S(1)} collective-permute-done((bf16[512,512]{1,0:T(8,128)(2,1)S(1)}, bf16[512,512]{1,0:T(8,128)(2,1)S(1)}, u32[]{:S(2)}, u32[]{:S(2)}) %collective-permute-start.8) | collective-permute-done | bytes 524320 | tf_op jit(solution)/shard_map/ppermute | solution.py:47
  11.5 2.0 %collective-permute-start.9 = (bf16[1024,512]{1,0:T(8,128)(2,1)S(1)}, bf16[1024,512]{1,0:T(8,128)(2,1)}, u32[]{:S(2)}, u32[]{:S(2)}) collective-permute-start(bf16[1024,512]{1,0:T(8,128)(2,1)S(1)} %pad_maximum_fusion.refs_4_), channel_id=1, source_target_pairs={{0,8},{4,60},{8,16},{12,4},{16,24},{20,12},{24,32},{28,20},{32,40}... | collective-permute-start | bytes 3145736 | tf_op jit(solution)/shard_map/ppermute | solution.py:47
  13.6 0.9 fusion.1.refs_0_
  14.4 1.5 collective-permute-start.7
  15.9 1.3 collective-permute-start.6
  17.2 2.2 %collective-permute-start.5 = (bf16[272,1024]{1,0:T(8,128)(2,1)}, bf16[272,1024]{1,0:T(8,128)(2,1)}, u32[]{:S(2)}, u32[]{:S(2)}) collective-permute-start(bf16[272,1024]{1,0:T(8,128)(2,1)} %fusion.1.refs_0_), channel_id=1, source_target_pairs={{64,0},{68,4},{72,8},{76,12},{80,16},{84,20},{88,24},{92,28},{96,3... | collective-permute-start | bytes 1671176 | tf_op jit(solution)/shard_map/ppermute | solution.py:47
  19.4 15.9 %collective-permute-done.9.refs_5_ = bf16[1024,512]{1,0:T(8,128)(2,1)} collective-permute-done((bf16[1024,512]{1,0:T(8,128)(2,1)S(1)}, bf16[1024,512]{1,0:T(8,128)(2,1)}, u32[]{:S(2)}, u32[]{:S(2)}) %collective-permute-start.9) | collective-permute-done | bytes 1048608 | tf_op jit(solution)/shard_map/ppermute | solution.py:47
  36.2 10.5 %collective-permute-start.1 = (f32[1,1024]{1,0:T(1,128)S(1)}, f32[1,1024]{1,0:T(1,128)S(1)}, u32[]{:S(2)}, u32[]{:S(2)}) collective-permute-start(f32[1,1024]{1,0:T(1,128)S(1)} %bitcast.26), channel_id=1, source_target_pairs={{0,128},{4,132},{8,136},{12,140},{16,144},{20,148},{24,152},{28,15... | collective-permute-start | bytes 12296 | tf_op jit(solution)/shard_map/ppermute | solution.py:47
  46.8 1.2 collective-permute-done.1
  48.0 1.9 %collective-permute-start = (f32[1,1024]{1,0:T(1,128)S(1)}, f32[1,1024]{1,0:T(1,128)S(1)}, u32[]{:S(2)}, u32[]{:S(2)}) collective-permute-start(f32[1,1024]{1,0:T(1,128)S(1)} %bitcast.27), channel_id=1, source_target_pairs={{0,64},{4,68},{8,72},{12,76},{16,80},{20,84},{24,88},{28,92},{32,9... | collective-permute-start | bytes 12296 | tf_op jit(solution)/shard_map/ppermute | solution.py:47
  49.9 2.0 %own_attention.1 = (f32[256,512]{1,0:T(8,128)S(1)}, f32[256,512]{1,0:T(8,128)S(1)}, f32[256,128]{1,0:T(8,128)S(1)}) custom-call(bf16[256,1024]{1,0:T(8,128)(2,1)S(1)} %copy-done.1, bf16[256,1024]{1,0:T(8,128)(2,1)S(1)} %copy-done, bf16[256,1024]{1,0:T(8,128)(2,1)S(1)} %copy-done.2), custom_call_target="tpu_custom_call" | custom-call | flops 1 | bytes 1 | tf_op jit(solution)/shard_map/own_attention/pallas_call | solution.py:212
  52.3 1.2 collective-permute-done
  56.5 17.7 %collective-permute-done.11.refs_7_ = bf16[1024,512]{1,0:T(8,128)(2,1)} collective-permute-done((bf16[1024,512]{1,0:T(8,128)(2,1)}, bf16[1024,512]{1,0:T(8,128)(2,1)}, u32[]{:S(2)}, u32[]{:S(2)}) %collective-permute-start.11) | collective-permute-done | bytes 1048608 | tf_op jit(solution)/shard_map/ppermute | solution.py:47
  74.2 2.1 %fusion.21 = (bf16[512,512]{1,0:T(8,128)(2,1)}, bf16[512,512]{1,0:T(8,128)(2,1)S(1)}) fusion(bf16[1024,512]{1,0:T(8,128)(2,1)} %collective-permute-done.11.refs_7_), kind=kLoop, calls=%fused_computation.55 | loop fusion | bytes 2097152 | tf_op jit(solution)/shard_map/slice | solution.py:301
  76.4 6.1 %all-gather.5.cloned.1.call-done = bf16[8192,512]{1,0:T(8,128)(2,1)} async-done(((bf16[512,512]{1,0:T(8,128)(2,1)}), bf16[8192,512]{1,0:T(8,128)(2,1)}) %all-gather.5.cloned.1.call-update) | async-done | bytes 8388624 | tf_op jit(solution)/shard_map/all_gather | solution.py:275
  83.2 10.4 %chosen_attention.2 = bf16[4,256,640]{2,1,0:T(8,128)(2,1)} custom-call(s32[1]{0:T(128)} %bitcast.y_ref, s32[4,16]{1,0:T(4,128)} %get-tuple-element.53.idx_ref, bf16[272,1024]{1,0:T(8,128)(2,1)} %fusion.1.refs_0_, bf16[272,1024]{1,0:T(8,128)(2,1)} %collective-permute-done.5.refs_1_, bf16[272,1024]{1,0:T(8,128)(2,1)} %collective-permute-done.6.refs_2_, ...), custom_call_target="tpu_custom_call" | custom-call | flops 1 | bytes 1 | tf_op jit(solution)/shard_map/chosen_attention/pallas_call | solution.py:216
  93.5 2.6 %collective-permute-start.10 = (bf16[1024,512]{1,0:T(8,128)(2,1)}, bf16[1024,512]{1,0:T(8,128)(2,1)}, u32[]{:S(2)}, u32[]{:S(2)}) collective-permute-start(bf16[1024,512]{1,0:T(8,128)(2,1)} %collective-permute-done.9.refs_5_), channel_id=1, source_target_pairs={{0,4},{4,0},{8,12},{12,8},{16,20},{20,16},{24,28},{28,24},{32,36},... | collective-permute-start | bytes 3145736 | tf_op jit(solution)/shard_map/ppermute | solution.py:47
  96.2 4.8 %all-to-all-start.1 = ((bf16[4,256,640]{2,1,0:T(8,128)(2,1)}), bf16[4,256,640]{2,1,0:T(8,128)(2,1)S(1)}, u32[]{:S(2)}, u32[]{:S(2)}) async-start(bf16[4,256,640]{2,1,0:T(8,128)(2,1)} %chosen_attention.2), calls=%async_computation.1 | async-start | bytes 2621440 | tf_op jit(solution)/shard_map/all_to_all | solution.py:259
  101.6 6.5 %collective-permute-done.17.refs_13_ = bf16[512,512]{1,0:T(8,128)(2,1)} collective-permute-done((bf16[512,512]{1,0:T(8,128)(2,1)}, bf16[512,512]{1,0:T(8,128)(2,1)}, u32[]{:S(2)}, u32[]{:S(2)}) %collective-permute-start.17) | collective-permute-done | bytes 524320 | tf_op jit(solution)/shard_map/ppermute | solution.py:47
  108.9 1.4 collective-permute-done.18.refs_14_
  110.3 10.3 %chosen_attention.3 = bf16[4,256,640]{2,1,0:T(8,128)(2,1)} custom-call(s32[1]{0:T(128)} %bitcast.y_ref, s32[4,16]{1,0:T(4,128)} %get-tuple-element.29.idx_ref, bf16[272,1024]{1,0:T(8,128)(2,1)} %fusion.1.refs_0_, bf16[272,1024]{1,0:T(8,128)(2,1)} %collective-permute-done.5.refs_1_, bf16[272,1024]{1,0:T(8,128)(2,1)} %collective-permute-done.6.refs_2_, ...), custom_call_target="tpu_custom_call" | custom-call | flops 1 | bytes 1 | tf_op jit(solution)/shard_map/chosen_attention/pallas_call | solution.py:216
  120.7 4.8 %all-to-all-start = ((bf16[4,256,640]{2,1,0:T(8,128)(2,1)}), bf16[4,256,640]{2,1,0:T(8,128)(2,1)S(1)}, u32[]{:S(2)}, u32[]{:S(2)}) async-start(bf16[4,256,640]{2,1,0:T(8,128)(2,1)} %chosen_attention.3), calls=%async_computation | async-start | bytes 2621440 | tf_op jit(solution)/shard_map/all_to_all | solution.py:259
  125.7 1.2 copy-done.3
  126.9 1.2 gate_share.1
  128.1 1.6 %collective-permute-start.3 = (f32[256,64]{1,0:T(8,128)S(1)}, f32[256,64]{1,0:T(8,128)S(1)}, u32[]{:S(2)}, u32[]{:S(2)}) collective-permute-start(f32[256,64]{1,0:T(8,128)S(1)} %gate_share.1), channel_id=1, source_target_pairs={{0,1},{1,0},{2,3},{3,2},{4,5},{5,4},{6,7},{7,6},{8,9},{9,8},{10,11... | collective-permute-start | bytes 196616 | tf_op jit(solution)/shard_map/ppermute | solution.py:254
  129.7 3.5 %collective-permute-done.3 = f32[256,64]{1,0:T(8,128)S(1)} collective-permute-done((f32[256,64]{1,0:T(8,128)S(1)}, f32[256,64]{1,0:T(8,128)S(1)}, u32[]{:S(2)}, u32[]{:S(2)}) %collective-permute-start.3) | collective-permute-done | bytes 65568 | tf_op jit(solution)/shard_map/ppermute | solution.py:254
  133.2 3.1 %collective-permute-start.4 = (f32[256,64]{1,0:T(8,128)S(1)}, f32[256,64]{1,0:T(8,128)S(1)}, u32[]{:S(2)}, u32[]{:S(2)}) collective-permute-start(f32[256,64]{1,0:T(8,128)S(1)} %add.233), channel_id=1, source_target_pairs={{0,2},{1,3},{2,0},{3,1},{4,6},{5,7},{6,4},{7,5},{8,10},{9,11},{10,... | collective-permute-start | bytes 196616 | tf_op jit(solution)/shard_map/ppermute | solution.py:254
  136.3 2.2 %combine.2.refs_0_ = bf16[256,512]{1,0:T(8,128)(2,1)S(1)} custom-call(s32[1]{0:T(128)} %bitcast.y_ref, f32[256,512]{1,0:T(8,128)S(1)} %copy-done.5, f32[256,128]{1,0:T(8,128)S(1)} %get-tuple-element.28.lse_ref, bf16[4,256,640]{2,1,0:T(8,128)(2,1)S(1)} %all-to-all-done.1.pieces_ref), custom_call_target="tpu_custom_call" | custom-call | flops 1 | bytes 1 | tf_op jit(solution)/shard_map/combine/pallas_call | solution.py:234
  138.5 1.3 collective-permute-done.4
  140.5 1.8 %all-to-all-done.pieces_ref = bf16[4,256,640]{2,1,0:T(8,128)(2,1)S(1)} async-done(((bf16[4,256,640]{2,1,0:T(8,128)(2,1)}), bf16[4,256,640]{2,1,0:T(8,128)(2,1)S(1)}, u32[]{:S(2)}, u32[]{:S(2)}) %all-to-all-start) | async-done | bytes 1310752 | tf_op jit(solution)/shard_map/all_to_all | solution.py:259
  142.3 3.0 %combine.3 = bf16[256,1024]{1,0:T(8,128)(2,1)} custom-call(s32[1]{0:T(128)} %bitcast.y_ref, f32[256,512]{1,0:T(8,128)S(1)} %copy-done.7, f32[256,128]{1,0:T(8,128)S(1)} %get-tuple-element.28.lse_ref, bf16[4,256,640]{2,1,0:T(8,128)(2,1)S(1)} %all-to-all-done.pieces_ref, bf16[256,512]{1,0:T(8,128)(2,1)S(1)} %combine.2.refs_0_), custom_call_target="tpu_custom_call" | custom-call | flops 1 | bytes 1 | tf_op jit(solution)/shard_map/combine/pallas_call | solution.py:234
  (82 shorter events, 8.4 us)
Async XLA Ops:
  7.2 75.3 %all-gather.5.cloned.1.call-start = ((), (), s32[]{:S(2)}) async-start(), calls=%async_computation.2 | async-start | bytes 8912896 | tf_op jit(solution)/shard_map/all_gather | solution.py:275
  9.3 116.4 %all-gather.7.cloned.1.call-start = ((), (), s32[]{:S(2)}) async-start(), calls=%async_computation.3 | async-start | bytes 1114112 | tf_op jit(solution)/shard_map/all_gather | solution.py:303
  9.3 4.2 %copy-start.12 = (s32[8,3]{0,1:T(4,128)S(1)}, s32[8,3]{0,1:T(4,128)}, u32[]{:S(2)}) copy-start(s32[8,3]{0,1:T(4,128)} %param.9) | copy-start | bytes 292
  9.4 4.2 %copy-start.1 = (bf16[256,1024]{1,0:T(8,128)(2,1)S(1)}, bf16[256,1024]{1,0:T(8,128)(2,1)}, u32[]{:S(2)}) copy-start(bf16[256,1024]{1,0:T(8,128)(2,1)} %q_ref.3) | copy-start | bytes 1572868
  9.4 2.0 %collective-permute-start.8 = (bf16[512,512]{1,0:T(8,128)(2,1)S(1)}, bf16[512,512]{1,0:T(8,128)(2,1)S(1)}, u32[]{:S(2)}, u32[]{:S(2)}) collective-permute-start(bf16[512,512]{1,0:T(8,128)(2,1)S(1)} %pad_maximum_fusion.2), channel_id=1, source_target_pairs={{0,4},{4,0},{8,12},{12,8},{16,20},{20,16},{24,28},{28,24},{32,36},... | collective-permute-start | bytes 1572872 | tf_op jit(solution)/shard_map/ppermute | solution.py:47
  11.5 38.5 %copy-start.8 = (bf16[1024,512]{1,0:T(8,128)(2,1)}, bf16[1024,512]{1,0:T(8,128)(2,1)S(1)}, u32[]{:S(2)}) copy-start(bf16[1024,512]{1,0:T(8,128)(2,1)S(1)} %pad_maximum_fusion.refs_4_) | copy-start | bytes 3145732
  11.5 38.5 %copy-start.2 = (bf16[256,1024]{1,0:T(8,128)(2,1)S(1)}, bf16[256,1024]{1,0:T(8,128)(2,1)}, u32[]{:S(2)}) copy-start(bf16[256,1024]{1,0:T(8,128)(2,1)} %v_ref.1) | copy-start | bytes 1572868
  11.5 23.8 %collective-permute-start.9 = (bf16[1024,512]{1,0:T(8,128)(2,1)S(1)}, bf16[1024,512]{1,0:T(8,128)(2,1)}, u32[]{:S(2)}, u32[]{:S(2)}) collective-permute-start(bf16[1024,512]{1,0:T(8,128)(2,1)S(1)} %pad_maximum_fusion.refs_4_), channel_id=1, source_target_pairs={{0,8},{4,60},{8,16},{12,4},{16,24},{20,12},{24,32},{28,20},{32,40}... | collective-permute-start | bytes 3145736 | tf_op jit(solution)/shard_map/ppermute | solution.py:47
  14.4 39.8 %collective-permute-start.7 = (bf16[272,1024]{1,0:T(8,128)(2,1)}, bf16[272,1024]{1,0:T(8,128)(2,1)}, u32[]{:S(2)}, u32[]{:S(2)}) collective-permute-start(bf16[272,1024]{1,0:T(8,128)(2,1)} %fusion.1.refs_0_), channel_id=1, source_target_pairs={{192,0},{196,4},{200,8},{204,12},{208,16},{212,20},{216,24},{220,2... | collective-permute-start | bytes 1671176 | tf_op jit(solution)/shard_map/ppermute | solution.py:47
  15.9 39.0 %collective-permute-start.6 = (bf16[272,1024]{1,0:T(8,128)(2,1)}, bf16[272,1024]{1,0:T(8,128)(2,1)}, u32[]{:S(2)}, u32[]{:S(2)}) collective-permute-start(bf16[272,1024]{1,0:T(8,128)(2,1)} %fusion.1.refs_0_), channel_id=1, source_target_pairs={{128,0},{132,4},{136,8},{140,12},{144,16},{148,20},{152,24},{156,2... | collective-permute-start | bytes 1671176 | tf_op jit(solution)/shard_map/ppermute | solution.py:47
  17.2 38.5 %collective-permute-start.5 = (bf16[272,1024]{1,0:T(8,128)(2,1)}, bf16[272,1024]{1,0:T(8,128)(2,1)}, u32[]{:S(2)}, u32[]{:S(2)}) collective-permute-start(bf16[272,1024]{1,0:T(8,128)(2,1)} %fusion.1.refs_0_), channel_id=1, source_target_pairs={{64,0},{68,4},{72,8},{76,12},{80,16},{84,20},{88,24},{92,28},{96,3... | collective-permute-start | bytes 1671176 | tf_op jit(solution)/shard_map/ppermute | solution.py:47
  35.3 38.8 %collective-permute-start.11 = (bf16[1024,512]{1,0:T(8,128)(2,1)}, bf16[1024,512]{1,0:T(8,128)(2,1)}, u32[]{:S(2)}, u32[]{:S(2)}) collective-permute-start(bf16[1024,512]{1,0:T(8,128)(2,1)} %collective-permute-done.9.refs_5_), channel_id=1, source_target_pairs={{0,8},{4,60},{8,16},{12,4},{16,24},{20,12},{24,32},{28,20},{32,40}... | collective-permute-start | bytes 3145736 | tf_op jit(solution)/shard_map/ppermute | solution.py:47
  35.4 0.8 collective-permute-start.2
  36.2 11.8 %collective-permute-start.1 = (f32[1,1024]{1,0:T(1,128)S(1)}, f32[1,1024]{1,0:T(1,128)S(1)}, u32[]{:S(2)}, u32[]{:S(2)}) collective-permute-start(f32[1,1024]{1,0:T(1,128)S(1)} %bitcast.26), channel_id=1, source_target_pairs={{0,128},{4,132},{8,136},{12,140},{16,144},{20,148},{24,152},{28,15... | collective-permute-start | bytes 12296 | tf_op jit(solution)/shard_map/ppermute | solution.py:47
  48.0 5.5 %collective-permute-start = (f32[1,1024]{1,0:T(1,128)S(1)}, f32[1,1024]{1,0:T(1,128)S(1)}, u32[]{:S(2)}, u32[]{:S(2)}) collective-permute-start(f32[1,1024]{1,0:T(1,128)S(1)} %bitcast.27), channel_id=1, source_target_pairs={{0,64},{4,68},{8,72},{12,76},{16,80},{20,84},{24,88},{28,92},{32,9... | collective-permute-start | bytes 12296 | tf_op jit(solution)/shard_map/ppermute | solution.py:47
  52.0 41.6 %copy-start.4 = (f32[256,512]{1,0:T(8,128)}, f32[256,512]{1,0:T(8,128)S(1)}, u32[]{:S(2)}) copy-start(f32[256,512]{1,0:T(8,128)S(1)} %get-tuple-element.35.own_ref) | copy-start | bytes 1572868
  52.0 41.6 %copy-start.6 = (f32[256,512]{1,0:T(8,128)}, f32[256,512]{1,0:T(8,128)S(1)}, u32[]{:S(2)}) copy-start(f32[256,512]{1,0:T(8,128)S(1)} %get-tuple-element.27.own_ref) | copy-start | bytes 1572868
  76.2 20.0 %collective-permute-start.13 = (bf16[512,512]{1,0:T(8,128)(2,1)S(1)}, bf16[512,512]{1,0:T(8,128)(2,1)}, u32[]{:S(2)}, u32[]{:S(2)}) collective-permute-start(bf16[512,512]{1,0:T(8,128)(2,1)S(1)} %get-tuple-element.45), channel_id=1, source_target_pairs={{0,8},{4,60},{8,16},{12,4},{16,24},{20,12},{24,32},{28,20},{32,40}... | collective-permute-start | bytes 1572872 | tf_op jit(solution)/shard_map/ppermute | solution.py:47
  83.2 17.9 %collective-permute-start.14 = (bf16[512,512]{1,0:T(8,128)(2,1)}, bf16[512,512]{1,0:T(8,128)(2,1)}, u32[]{:S(2)}, u32[]{:S(2)}) collective-permute-start(bf16[512,512]{1,0:T(8,128)(2,1)} %get-tuple-element.44), channel_id=1, source_target_pairs={{0,8},{4,60},{8,16},{12,4},{16,24},{20,12},{24,32},{28,20},{32,40}... | collective-permute-start | bytes 1572872 | tf_op jit(solution)/shard_map/ppermute | solution.py:47
  93.5 14.5 %collective-permute-start.10 = (bf16[1024,512]{1,0:T(8,128)(2,1)}, bf16[1024,512]{1,0:T(8,128)(2,1)}, u32[]{:S(2)}, u32[]{:S(2)}) collective-permute-start(bf16[1024,512]{1,0:T(8,128)(2,1)} %collective-permute-done.9.refs_5_), channel_id=1, source_target_pairs={{0,4},{4,0},{8,12},{12,8},{16,20},{20,16},{24,28},{28,24},{32,36},... | collective-permute-start | bytes 3145736 | tf_op jit(solution)/shard_map/ppermute | solution.py:47
  96.1 12.0 %collective-permute-start.12 = (bf16[1024,512]{1,0:T(8,128)(2,1)}, bf16[1024,512]{1,0:T(8,128)(2,1)S(1)}, u32[]{:S(2)}, u32[]{:S(2)}) collective-permute-start(bf16[1024,512]{1,0:T(8,128)(2,1)} %collective-permute-done.11.refs_7_), channel_id=1, source_target_pairs={{0,4},{4,0},{8,12},{12,8},{16,20},{20,16},{24,28},{28,24},{32,36},... | collective-permute-start | bytes 3145736 | tf_op jit(solution)/shard_map/ppermute | solution.py:47
  96.2 11.8 %collective-permute-start.17 = (bf16[512,512]{1,0:T(8,128)(2,1)}, bf16[512,512]{1,0:T(8,128)(2,1)}, u32[]{:S(2)}, u32[]{:S(2)}) collective-permute-start(bf16[512,512]{1,0:T(8,128)(2,1)} %collective-permute-done.13.refs_9_), channel_id=1, source_target_pairs={{0,8},{4,60},{8,16},{12,4},{16,24},{20,12},{24,32},{28,20},{32,40}... | collective-permute-start | bytes 1572872 | tf_op jit(solution)/shard_map/ppermute | solution.py:47
  96.2 24.5 %all-to-all-start.1 = ((bf16[4,256,640]{2,1,0:T(8,128)(2,1)}), bf16[4,256,640]{2,1,0:T(8,128)(2,1)S(1)}, u32[]{:S(2)}, u32[]{:S(2)}) async-start(bf16[4,256,640]{2,1,0:T(8,128)(2,1)} %chosen_attention.2), calls=%async_computation.1 | async-start | bytes 2621440 | tf_op jit(solution)/shard_map/all_to_all | solution.py:259
  101.0 7.0 %collective-permute-start.16 = (bf16[512,512]{1,0:T(8,128)(2,1)}, bf16[512,512]{1,0:T(8,128)(2,1)S(1)}, u32[]{:S(2)}, u32[]{:S(2)}) collective-permute-start(bf16[512,512]{1,0:T(8,128)(2,1)} %collective-permute-done.14.refs_10_), channel_id=1, source_target_pairs={{0,4},{4,0},{8,12},{12,8},{16,20},{20,16},{24,28},{28,24},{32,36},... | collective-permute-start | bytes 1572872 | tf_op jit(solution)/shard_map/ppermute | solution.py:47
  101.6 6.5 %collective-permute-start.15 = (bf16[512,512]{1,0:T(8,128)(2,1)}, bf16[512,512]{1,0:T(8,128)(2,1)S(1)}, u32[]{:S(2)}, u32[]{:S(2)}) collective-permute-start(bf16[512,512]{1,0:T(8,128)(2,1)} %collective-permute-done.13.refs_9_), channel_id=1, source_target_pairs={{0,4},{4,0},{8,12},{12,8},{16,20},{20,16},{24,28},{28,24},{32,36},... | collective-permute-start | bytes 1572872 | tf_op jit(solution)/shard_map/ppermute | solution.py:47
  108.1 2.3 %collective-permute-start.18 = (bf16[512,512]{1,0:T(8,128)(2,1)}, bf16[512,512]{1,0:T(8,128)(2,1)}, u32[]{:S(2)}, u32[]{:S(2)}) collective-permute-start(bf16[512,512]{1,0:T(8,128)(2,1)} %collective-permute-done.17.refs_13_), channel_id=1, source_target_pairs={{0,4},{4,0},{8,12},{12,8},{16,20},{20,16},{24,28},{28,24},{32,36},... | collective-permute-start | bytes 1572872 | tf_op jit(solution)/shard_map/ppermute | solution.py:47
  108.1 2.2 %copy-start.10 = (bf16[512,512]{1,0:T(8,128)(2,1)}, bf16[512,512]{1,0:T(8,128)(2,1)S(1)}, u32[]{:S(2)}) copy-start(bf16[512,512]{1,0:T(8,128)(2,1)S(1)} %collective-permute-done.16.refs_12_) | copy-start | bytes 1572868
  120.7 21.6 %all-to-all-start = ((bf16[4,256,640]{2,1,0:T(8,128)(2,1)}), bf16[4,256,640]{2,1,0:T(8,128)(2,1)S(1)}, u32[]{:S(2)}, u32[]{:S(2)}) async-start(bf16[4,256,640]{2,1,0:T(8,128)(2,1)} %chosen_attention.3), calls=%async_computation | async-start | bytes 2621440 | tf_op jit(solution)/shard_map/all_to_all | solution.py:259
  126.9 9.4 %copy-start.5 = (f32[256,512]{1,0:T(8,128)S(1)}, f32[256,512]{1,0:T(8,128)}, u32[]{:S(2)}) copy-start(f32[256,512]{1,0:T(8,128)} %copy-done.4) | copy-start | bytes 1572868
  128.1 5.1 %collective-permute-start.3 = (f32[256,64]{1,0:T(8,128)S(1)}, f32[256,64]{1,0:T(8,128)S(1)}, u32[]{:S(2)}, u32[]{:S(2)}) collective-permute-start(f32[256,64]{1,0:T(8,128)S(1)} %gate_share.1), channel_id=1, source_target_pairs={{0,1},{1,0},{2,3},{3,2},{4,5},{5,4},{6,7},{7,6},{8,9},{9,8},{10,11... | collective-permute-start | bytes 196616 | tf_op jit(solution)/shard_map/ppermute | solution.py:254
  133.2 6.6 %collective-permute-start.4 = (f32[256,64]{1,0:T(8,128)S(1)}, f32[256,64]{1,0:T(8,128)S(1)}, u32[]{:S(2)}, u32[]{:S(2)}) collective-permute-start(f32[256,64]{1,0:T(8,128)S(1)} %add.233), channel_id=1, source_target_pairs={{0,2},{1,3},{2,0},{3,1},{4,6},{5,7},{6,4},{7,5},{8,10},{9,11},{10,... | collective-permute-start | bytes 196616 | tf_op jit(solution)/shard_map/ppermute | solution.py:254
  136.3 6.0 %copy-start.7 = (f32[256,512]{1,0:T(8,128)S(1)}, f32[256,512]{1,0:T(8,128)}, u32[]{:S(2)}) copy-start(f32[256,512]{1,0:T(8,128)} %copy-done.6) | copy-start | bytes 1572868
  (4 other events, 4.7 us)
Sparse Core Ops, SparseCore 0:
  9.8 72.5 all-gather.4
  84.9 39.3 all-gather.6

commit v4 on v3

--- a/solution.py
+++ b/solution.py
@@ -267,11 +267,11 @@
     here = y.reshape(1).astype(jnp.int32)
     sign = 2 * c - 1
 
-    second = jnp.concatenate([keys[:, LANES:], values[:, LANES:]], axis=0)
+    first = jnp.concatenate([keys[:, :LANES], values[:, :LANES]], axis=0)
+    second = jnp.concatenate([after(keys[:, LANES:], first), values[:, LANES:]], axis=0)
     hops = [jnp.concatenate([second, swap(second)], axis=0)]
     hops += [ring(hops[0])]
     hops += [ring(hops[1])]
-    first = jnp.concatenate([keys[:, :LANES], values[:, :LANES]], axis=0)
     gathered = lax.all_gather(first, "seq", axis_index_groups=PLANES)
 
     choices = jnp.zeros((16, WIDTH), jnp.bfloat16).at[:TILES, :TOPK].set(gating.astype(jnp.bfloat16))

time: 154 us -> 154 us (level)
  no operation moved by 1% of the time
where the time goes in v4:
time: 154 us; the launch traced here: 152 us
  waiting for transfers between devices  58.6 us (38%)
  starting transfers between devices  37.6 us (24%)
  Pallas kernels  29.1 us (19%)
  between operations  14.7 us (10%)
  local copies, waits for them, and re-layouts  8.53 us (6%)
  other arithmetic  3.64 us (2%)
    ppermute x17, waiting for transfers between devices, send(): return lax.ppermute(x, 'seq', pairs)  45.8 us
    ppermute x17, starting transfers between devices, send(): return lax.ppermute(x, 'seq', pairs)  23.3 us
    pallas_call x2, Pallas kernels, chosen_attention(): call(functools.partial(chosen_kernel, half, blocks), 'chosen_attention',...  20.7 us
    all_to_all x2, starting transfers between devices, back(): lax.all_to_all(out, 'seq', split_axis=0, concat_axis=0, tiled=True, axis_...  9.65 us
    all_gather x1, waiting for transfers between devices, body(): gathered = lax.all_gather(first, 'seq', axis_index_groups=PLANES)  6.08 us
    pallas_call x2, Pallas kernels, combine(): call(functools.partial(combine_kernel, half), 'combine', jax.ShapeDtypeSt...  5.18 us
    ppermute x2, waiting for transfers between devices, over_heads(): lax.ppermute(share, 'head', [(i, i ^ bits) for i in range(4)])  4.82 us
    ppermute x2, starting transfers between devices, over_heads(): lax.ppermute(share, 'head', [(i, i ^ bits) for i in range(4)])  4.62 us
  transfers between devices with their start and end apart: 23, of which 11 were waited for; matrix products, arithmetic and copies ran while one was open for 5% of the time, Pallas kernels for 17%

profile of v4, /device:TPU:8, one launch (start us, length us, event | category | flops | bytes accessed | tf_op | source)
XLA Modules:
  0.0 152.1 jit_solution(5643751461185535511)
XLA Ops:
  7.2 1.1 fusion.23
  9.5 1.9 %collective-permute-done.8 = bf16[512,512]{1,0:T(8,128)(2,1)S(1)} collective-permute-done((bf16[512,512]{1,0:T(8,128)(2,1)S(1)}, bf16[512,512]{1,0:T(8,128)(2,1)S(1)}, u32[]{:S(2)}, u32[]{:S(2)}) %collective-permute-start.8) | collective-permute-done | bytes 524320 | tf_op jit(solution)/shard_map/ppermute | solution.py:47
  11.5 2.0 %collective-permute-start.9 = (bf16[1024,512]{1,0:T(8,128)(2,1)S(1)}, bf16[1024,512]{1,0:T(8,128)(2,1)}, u32[]{:S(2)}, u32[]{:S(2)}) collective-permute-start(bf16[1024,512]{1,0:T(8,128)(2,1)S(1)} %pad_maximum_fusion.refs_4_), channel_id=1, source_target_pairs={{0,8},{4,60},{8,16},{12,4},{16,24},{20,12},{24,32},{28,20},{32,40}... | collective-permute-start | bytes 3145736 | tf_op jit(solution)/shard_map/ppermute | solution.py:47
  13.6 0.9 fusion.1.refs_0_
  14.4 1.5 collective-permute-start.7
  15.9 1.3 collective-permute-start.6
  17.2 2.2 %collective-permute-start.5 = (bf16[272,1024]{1,0:T(8,128)(2,1)}, bf16[272,1024]{1,0:T(8,128)(2,1)}, u32[]{:S(2)}, u32[]{:S(2)}) collective-permute-start(bf16[272,1024]{1,0:T(8,128)(2,1)} %fusion.1.refs_0_), channel_id=1, source_target_pairs={{64,0},{68,4},{72,8},{76,12},{80,16},{84,20},{88,24},{92,28},{96,3... | collective-permute-start | bytes 1671176 | tf_op jit(solution)/shard_map/ppermute | solution.py:47
  19.4 15.9 %collective-permute-done.9.refs_5_ = bf16[1024,512]{1,0:T(8,128)(2,1)} collective-permute-done((bf16[1024,512]{1,0:T(8,128)(2,1)S(1)}, bf16[1024,512]{1,0:T(8,128)(2,1)}, u32[]{:S(2)}, u32[]{:S(2)}) %collective-permute-start.9) | collective-permute-done | bytes 1048608 | tf_op jit(solution)/shard_map/ppermute | solution.py:47
  36.2 10.5 %collective-permute-start.1 = (f32[1,1024]{1,0:T(1,128)S(1)}, f32[1,1024]{1,0:T(1,128)S(1)}, u32[]{:S(2)}, u32[]{:S(2)}) collective-permute-start(f32[1,1024]{1,0:T(1,128)S(1)} %bitcast.26), channel_id=1, source_target_pairs={{0,128},{4,132},{8,136},{12,140},{16,144},{20,148},{24,152},{28,15... | collective-permute-start | bytes 12296 | tf_op jit(solution)/shard_map/ppermute | solution.py:47
  46.8 1.2 collective-permute-done.1
  48.0 1.9 %collective-permute-start = (f32[1,1024]{1,0:T(1,128)S(1)}, f32[1,1024]{1,0:T(1,128)S(1)}, u32[]{:S(2)}, u32[]{:S(2)}) collective-permute-start(f32[1,1024]{1,0:T(1,128)S(1)} %bitcast.27), channel_id=1, source_target_pairs={{0,64},{4,68},{8,72},{12,76},{16,80},{20,84},{24,88},{28,92},{32,9... | collective-permute-start | bytes 12296 | tf_op jit(solution)/shard_map/ppermute | solution.py:47
  49.9 2.0 %own_attention.1 = (f32[256,512]{1,0:T(8,128)S(1)}, f32[256,512]{1,0:T(8,128)S(1)}, f32[256,128]{1,0:T(8,128)S(1)}) custom-call(bf16[256,1024]{1,0:T(8,128)(2,1)S(1)} %copy-done.1, bf16[256,1024]{1,0:T(8,128)(2,1)S(1)} %copy-done, bf16[256,1024]{1,0:T(8,128)(2,1)S(1)} %copy-done.2), custom_call_target="tpu_custom_call" | custom-call | flops 1 | bytes 1 | tf_op jit(solution)/shard_map/own_attention/pallas_call | solution.py:212
  52.3 1.2 collective-permute-done
  56.5 17.7 %collective-permute-done.11.refs_7_ = bf16[1024,512]{1,0:T(8,128)(2,1)} collective-permute-done((bf16[1024,512]{1,0:T(8,128)(2,1)}, bf16[1024,512]{1,0:T(8,128)(2,1)}, u32[]{:S(2)}, u32[]{:S(2)}) %collective-permute-start.11) | collective-permute-done | bytes 1048608 | tf_op jit(solution)/shard_map/ppermute | solution.py:47
  74.2 2.1 %fusion.21 = (bf16[512,512]{1,0:T(8,128)(2,1)}, bf16[512,512]{1,0:T(8,128)(2,1)S(1)}) fusion(bf16[1024,512]{1,0:T(8,128)(2,1)} %collective-permute-done.11.refs_7_), kind=kLoop, calls=%fused_computation.55 | loop fusion | bytes 2097152 | tf_op jit(solution)/shard_map/slice | solution.py:301
  76.4 6.1 %all-gather.5.cloned.1.call-done = bf16[8192,512]{1,0:T(8,128)(2,1)} async-done(((bf16[512,512]{1,0:T(8,128)(2,1)}), bf16[8192,512]{1,0:T(8,128)(2,1)}) %all-gather.5.cloned.1.call-update) | async-done | bytes 8388624 | tf_op jit(solution)/shard_map/all_gather | solution.py:275
  83.2 10.4 %chosen_attention.2 = bf16[4,256,640]{2,1,0:T(8,128)(2,1)} custom-call(s32[1]{0:T(128)} %bitcast.y_ref, s32[4,16]{1,0:T(4,128)} %get-tuple-element.55.idx_ref, bf16[272,1024]{1,0:T(8,128)(2,1)} %fusion.1.refs_0_, bf16[272,1024]{1,0:T(8,128)(2,1)} %collective-permute-done.5.refs_1_, bf16[272,1024]{1,0:T(8,128)(2,1)} %collective-permute-done.6.refs_2_, ...), custom_call_target="tpu_custom_call" | custom-call | flops 1 | bytes 1 | tf_op jit(solution)/shard_map/chosen_attention/pallas_call | solution.py:216
  93.6 2.5 %collective-permute-start.10 = (bf16[1024,512]{1,0:T(8,128)(2,1)}, bf16[1024,512]{1,0:T(8,128)(2,1)}, u32[]{:S(2)}, u32[]{:S(2)}) collective-permute-start(bf16[1024,512]{1,0:T(8,128)(2,1)} %collective-permute-done.9.refs_5_), channel_id=1, source_target_pairs={{0,4},{4,0},{8,12},{12,8},{16,20},{20,16},{24,28},{28,24},{32,36},... | collective-permute-start | bytes 3145736 | tf_op jit(solution)/shard_map/ppermute | solution.py:47
  96.2 4.8 %all-to-all-start.1 = ((bf16[4,256,640]{2,1,0:T(8,128)(2,1)}), bf16[4,256,640]{2,1,0:T(8,128)(2,1)S(1)}, u32[]{:S(2)}, u32[]{:S(2)}) async-start(bf16[4,256,640]{2,1,0:T(8,128)(2,1)} %chosen_attention.2), calls=%async_computation.1 | async-start | bytes 2621440 | tf_op jit(solution)/shard_map/all_to_all | solution.py:259
  101.6 6.5 %collective-permute-done.17.refs_13_ = bf16[512,512]{1,0:T(8,128)(2,1)} collective-permute-done((bf16[512,512]{1,0:T(8,128)(2,1)}, bf16[512,512]{1,0:T(8,128)(2,1)}, u32[]{:S(2)}, u32[]{:S(2)}) %collective-permute-start.17) | collective-permute-done | bytes 524320 | tf_op jit(solution)/shard_map/ppermute | solution.py:47
  108.9 1.4 collective-permute-done.18.refs_14_
  110.3 10.3 %chosen_attention.3 = bf16[4,256,640]{2,1,0:T(8,128)(2,1)} custom-call(s32[1]{0:T(128)} %bitcast.y_ref, s32[4,16]{1,0:T(4,128)} %get-tuple-element.30.idx_ref, bf16[272,1024]{1,0:T(8,128)(2,1)} %fusion.1.refs_0_, bf16[272,1024]{1,0:T(8,128)(2,1)} %collective-permute-done.5.refs_1_, bf16[272,1024]{1,0:T(8,128)(2,1)} %collective-permute-done.6.refs_2_, ...), custom_call_target="tpu_custom_call" | custom-call | flops 1 | bytes 1 | tf_op jit(solution)/shard_map/chosen_attention/pallas_call | solution.py:216
  120.7 4.8 %all-to-all-start = ((bf16[4,256,640]{2,1,0:T(8,128)(2,1)}), bf16[4,256,640]{2,1,0:T(8,128)(2,1)S(1)}, u32[]{:S(2)}, u32[]{:S(2)}) async-start(bf16[4,256,640]{2,1,0:T(8,128)(2,1)} %chosen_attention.3), calls=%async_computation | async-start | bytes 2621440 | tf_op jit(solution)/shard_map/all_to_all | solution.py:259
  125.7 1.2 copy-done.3
  126.9 1.2 gate_share.1
  128.1 1.6 %collective-permute-start.3 = (f32[256,64]{1,0:T(8,128)S(1)}, f32[256,64]{1,0:T(8,128)S(1)}, u32[]{:S(2)}, u32[]{:S(2)}) collective-permute-start(f32[256,64]{1,0:T(8,128)S(1)} %gate_share.1), channel_id=1, source_target_pairs={{0,1},{1,0},{2,3},{3,2},{4,5},{5,4},{6,7},{7,6},{8,9},{9,8},{10,11... | collective-permute-start | bytes 196616 | tf_op jit(solution)/shard_map/ppermute | solution.py:254
  129.7 3.5 %collective-permute-done.3 = f32[256,64]{1,0:T(8,128)S(1)} collective-permute-done((f32[256,64]{1,0:T(8,128)S(1)}, f32[256,64]{1,0:T(8,128)S(1)}, u32[]{:S(2)}, u32[]{:S(2)}) %collective-permute-start.3) | collective-permute-done | bytes 65568 | tf_op jit(solution)/shard_map/ppermute | solution.py:254
  133.2 3.1 %collective-permute-start.4 = (f32[256,64]{1,0:T(8,128)S(1)}, f32[256,64]{1,0:T(8,128)S(1)}, u32[]{:S(2)}, u32[]{:S(2)}) collective-permute-start(f32[256,64]{1,0:T(8,128)S(1)} %add.233), channel_id=1, source_target_pairs={{0,2},{1,3},{2,0},{3,1},{4,6},{5,7},{6,4},{7,5},{8,10},{9,11},{10,... | collective-permute-start | bytes 196616 | tf_op jit(solution)/shard_map/ppermute | solution.py:254
  136.3 2.2 %combine.2.refs_0_ = bf16[256,512]{1,0:T(8,128)(2,1)S(1)} custom-call(s32[1]{0:T(128)} %bitcast.y_ref, f32[256,512]{1,0:T(8,128)S(1)} %copy-done.5, f32[256,128]{1,0:T(8,128)S(1)} %get-tuple-element.29.lse_ref, bf16[4,256,640]{2,1,0:T(8,128)(2,1)S(1)} %all-to-all-done.1.pieces_ref), custom_call_target="tpu_custom_call" | custom-call | flops 1 | bytes 1 | tf_op jit(solution)/shard_map/combine/pallas_call | solution.py:234
  138.5 1.3 collective-permute-done.4
  140.5 1.8 %all-to-all-done.pieces_ref = bf16[4,256,640]{2,1,0:T(8,128)(2,1)S(1)} async-done(((bf16[4,256,640]{2,1,0:T(8,128)(2,1)}), bf16[4,256,640]{2,1,0:T(8,128)(2,1)S(1)}, u32[]{:S(2)}, u32[]{:S(2)}) %all-to-all-start) | async-done | bytes 1310752 | tf_op jit(solution)/shard_map/all_to_all | solution.py:259
  142.3 3.0 %combine.3 = bf16[256,1024]{1,0:T(8,128)(2,1)} custom-call(s32[1]{0:T(128)} %bitcast.y_ref, f32[256,512]{1,0:T(8,128)S(1)} %copy-done.7, f32[256,128]{1,0:T(8,128)S(1)} %get-tuple-element.29.lse_ref, bf16[4,256,640]{2,1,0:T(8,128)(2,1)S(1)} %all-to-all-done.pieces_ref, bf16[256,512]{1,0:T(8,128)(2,1)S(1)} %combine.2.refs_0_), custom_call_target="tpu_custom_call" | custom-call | flops 1 | bytes 1 | tf_op jit(solution)/shard_map/combine/pallas_call | solution.py:234
  (82 shorter events, 8.4 us)
Async XLA Ops:
  7.2 75.3 %all-gather.5.cloned.1.call-start = ((), (), s32[]{:S(2)}) async-start(), calls=%async_computation.2 | async-start | bytes 8912896 | tf_op jit(solution)/shard_map/all_gather | solution.py:275
  9.3 116.4 %all-gather.7.cloned.1.call-start = ((), (), s32[]{:S(2)}) async-start(), calls=%async_computation.3 | async-start | bytes 1114112 | tf_op jit(solution)/shard_map/all_gather | solution.py:303
  9.3 4.2 %copy-start.12 = (s32[8,3]{0,1:T(4,128)S(1)}, s32[8,3]{0,1:T(4,128)}, u32[]{:S(2)}) copy-start(s32[8,3]{0,1:T(4,128)} %param.9) | copy-start | bytes 292
  9.4 4.2 %copy-start.1 = (bf16[256,1024]{1,0:T(8,128)(2,1)S(1)}, bf16[256,1024]{1,0:T(8,128)(2,1)}, u32[]{:S(2)}) copy-start(bf16[256,1024]{1,0:T(8,128)(2,1)} %q_ref.3) | copy-start | bytes 1572868
  9.4 2.0 %collective-permute-start.8 = (bf16[512,512]{1,0:T(8,128)(2,1)S(1)}, bf16[512,512]{1,0:T(8,128)(2,1)S(1)}, u32[]{:S(2)}, u32[]{:S(2)}) collective-permute-start(bf16[512,512]{1,0:T(8,128)(2,1)S(1)} %pad_maximum_fusion.2), channel_id=1, source_target_pairs={{0,4},{4,0},{8,12},{12,8},{16,20},{20,16},{24,28},{28,24},{32,36},... | collective-permute-start | bytes 1572872 | tf_op jit(solution)/shard_map/ppermute | solution.py:47
  11.5 38.5 %copy-start.8 = (bf16[1024,512]{1,0:T(8,128)(2,1)}, bf16[1024,512]{1,0:T(8,128)(2,1)S(1)}, u32[]{:S(2)}) copy-start(bf16[1024,512]{1,0:T(8,128)(2,1)S(1)} %pad_maximum_fusion.refs_4_) | copy-start | bytes 3145732
  11.5 38.5 %copy-start.2 = (bf16[256,1024]{1,0:T(8,128)(2,1)S(1)}, bf16[256,1024]{1,0:T(8,128)(2,1)}, u32[]{:S(2)}) copy-start(bf16[256,1024]{1,0:T(8,128)(2,1)} %v_ref.1) | copy-start | bytes 1572868
  11.5 23.8 %collective-permute-start.9 = (bf16[1024,512]{1,0:T(8,128)(2,1)S(1)}, bf16[1024,512]{1,0:T(8,128)(2,1)}, u32[]{:S(2)}, u32[]{:S(2)}) collective-permute-start(bf16[1024,512]{1,0:T(8,128)(2,1)S(1)} %pad_maximum_fusion.refs_4_), channel_id=1, source_target_pairs={{0,8},{4,60},{8,16},{12,4},{16,24},{20,12},{24,32},{28,20},{32,40}... | collective-permute-start | bytes 3145736 | tf_op jit(solution)/shard_map/ppermute | solution.py:47
  14.4 39.8 %collective-permute-start.7 = (bf16[272,1024]{1,0:T(8,128)(2,1)}, bf16[272,1024]{1,0:T(8,128)(2,1)}, u32[]{:S(2)}, u32[]{:S(2)}) collective-permute-start(bf16[272,1024]{1,0:T(8,128)(2,1)} %fusion.1.refs_0_), channel_id=1, source_target_pairs={{192,0},{196,4},{200,8},{204,12},{208,16},{212,20},{216,24},{220,2... | collective-permute-start | bytes 1671176 | tf_op jit(solution)/shard_map/ppermute | solution.py:47
  15.9 39.0 %collective-permute-start.6 = (bf16[272,1024]{1,0:T(8,128)(2,1)}, bf16[272,1024]{1,0:T(8,128)(2,1)}, u32[]{:S(2)}, u32[]{:S(2)}) collective-permute-start(bf16[272,1024]{1,0:T(8,128)(2,1)} %fusion.1.refs_0_), channel_id=1, source_target_pairs={{128,0},{132,4},{136,8},{140,12},{144,16},{148,20},{152,24},{156,2... | collective-permute-start | bytes 1671176 | tf_op jit(solution)/shard_map/ppermute | solution.py:47
  17.2 38.5 %collective-permute-start.5 = (bf16[272,1024]{1,0:T(8,128)(2,1)}, bf16[272,1024]{1,0:T(8,128)(2,1)}, u32[]{:S(2)}, u32[]{:S(2)}) collective-permute-start(bf16[272,1024]{1,0:T(8,128)(2,1)} %fusion.1.refs_0_), channel_id=1, source_target_pairs={{64,0},{68,4},{72,8},{76,12},{80,16},{84,20},{88,24},{92,28},{96,3... | collective-permute-start | bytes 1671176 | tf_op jit(solution)/shard_map/ppermute | solution.py:47
  35.3 38.8 %collective-permute-start.11 = (bf16[1024,512]{1,0:T(8,128)(2,1)}, bf16[1024,512]{1,0:T(8,128)(2,1)}, u32[]{:S(2)}, u32[]{:S(2)}) collective-permute-start(bf16[1024,512]{1,0:T(8,128)(2,1)} %collective-permute-done.9.refs_5_), channel_id=1, source_target_pairs={{0,8},{4,60},{8,16},{12,4},{16,24},{20,12},{24,32},{28,20},{32,40}... | collective-permute-start | bytes 3145736 | tf_op jit(solution)/shard_map/ppermute | solution.py:47
  35.4 0.8 collective-permute-start.2
  36.2 11.8 %collective-permute-start.1 = (f32[1,1024]{1,0:T(1,128)S(1)}, f32[1,1024]{1,0:T(1,128)S(1)}, u32[]{:S(2)}, u32[]{:S(2)}) collective-permute-start(f32[1,1024]{1,0:T(1,128)S(1)} %bitcast.26), channel_id=1, source_target_pairs={{0,128},{4,132},{8,136},{12,140},{16,144},{20,148},{24,152},{28,15... | collective-permute-start | bytes 12296 | tf_op jit(solution)/shard_map/ppermute | solution.py:47
  48.0 5.5 %collective-permute-start = (f32[1,1024]{1,0:T(1,128)S(1)}, f32[1,1024]{1,0:T(1,128)S(1)}, u32[]{:S(2)}, u32[]{:S(2)}) collective-permute-start(f32[1,1024]{1,0:T(1,128)S(1)} %bitcast.27), channel_id=1, source_target_pairs={{0,64},{4,68},{8,72},{12,76},{16,80},{20,84},{24,88},{28,92},{32,9... | collective-permute-start | bytes 12296 | tf_op jit(solution)/shard_map/ppermute | solution.py:47
  52.0 41.6 %copy-start.4 = (f32[256,512]{1,0:T(8,128)}, f32[256,512]{1,0:T(8,128)S(1)}, u32[]{:S(2)}) copy-start(f32[256,512]{1,0:T(8,128)S(1)} %get-tuple-element.37.own_ref) | copy-start | bytes 1572868
  52.0 41.6 %copy-start.6 = (f32[256,512]{1,0:T(8,128)}, f32[256,512]{1,0:T(8,128)S(1)}, u32[]{:S(2)}) copy-start(f32[256,512]{1,0:T(8,128)S(1)} %get-tuple-element.28.own_ref) | copy-start | bytes 1572868
  76.2 20.0 %collective-permute-start.13 = (bf16[512,512]{1,0:T(8,128)(2,1)S(1)}, bf16[512,512]{1,0:T(8,128)(2,1)}, u32[]{:S(2)}, u32[]{:S(2)}) collective-permute-start(bf16[512,512]{1,0:T(8,128)(2,1)S(1)} %get-tuple-element.47), channel_id=1, source_target_pairs={{0,8},{4,60},{8,16},{12,4},{16,24},{20,12},{24,32},{28,20},{32,40}... | collective-permute-start | bytes 1572872 | tf_op jit(solution)/shard_map/ppermute | solution.py:47
  83.2 17.9 %collective-permute-start.14 = (bf16[512,512]{1,0:T(8,128)(2,1)}, bf16[512,512]{1,0:T(8,128)(2,1)}, u32[]{:S(2)}, u32[]{:S(2)}) collective-permute-start(bf16[512,512]{1,0:T(8,128)(2,1)} %get-tuple-element.46), channel_id=1, source_target_pairs={{0,8},{4,60},{8,16},{12,4},{16,24},{20,12},{24,32},{28,20},{32,40}... | collective-permute-start | bytes 1572872 | tf_op jit(solution)/shard_map/ppermute | solution.py:47
  93.6 14.5 %collective-permute-start.10 = (bf16[1024,512]{1,0:T(8,128)(2,1)}, bf16[1024,512]{1,0:T(8,128)(2,1)}, u32[]{:S(2)}, u32[]{:S(2)}) collective-permute-start(bf16[1024,512]{1,0:T(8,128)(2,1)} %collective-permute-done.9.refs_5_), channel_id=1, source_target_pairs={{0,4},{4,0},{8,12},{12,8},{16,20},{20,16},{24,28},{28,24},{32,36},... | collective-permute-start | bytes 3145736 | tf_op jit(solution)/shard_map/ppermute | solution.py:47
  96.1 12.0 %collective-permute-start.12 = (bf16[1024,512]{1,0:T(8,128)(2,1)}, bf16[1024,512]{1,0:T(8,128)(2,1)S(1)}, u32[]{:S(2)}, u32[]{:S(2)}) collective-permute-start(bf16[1024,512]{1,0:T(8,128)(2,1)} %collective-permute-done.11.refs_7_), channel_id=1, source_target_pairs={{0,4},{4,0},{8,12},{12,8},{16,20},{20,16},{24,28},{28,24},{32,36},... | collective-permute-start | bytes 3145736 | tf_op jit(solution)/shard_map/ppermute | solution.py:47
  96.2 11.8 %collective-permute-start.17 = (bf16[512,512]{1,0:T(8,128)(2,1)}, bf16[512,512]{1,0:T(8,128)(2,1)}, u32[]{:S(2)}, u32[]{:S(2)}) collective-permute-start(bf16[512,512]{1,0:T(8,128)(2,1)} %collective-permute-done.13.refs_9_), channel_id=1, source_target_pairs={{0,8},{4,60},{8,16},{12,4},{16,24},{20,12},{24,32},{28,20},{32,40}... | collective-permute-start | bytes 1572872 | tf_op jit(solution)/shard_map/ppermute | solution.py:47
  96.2 24.5 %all-to-all-start.1 = ((bf16[4,256,640]{2,1,0:T(8,128)(2,1)}), bf16[4,256,640]{2,1,0:T(8,128)(2,1)S(1)}, u32[]{:S(2)}, u32[]{:S(2)}) async-start(bf16[4,256,640]{2,1,0:T(8,128)(2,1)} %chosen_attention.2), calls=%async_computation.1 | async-start | bytes 2621440 | tf_op jit(solution)/shard_map/all_to_all | solution.py:259
  101.0 7.0 %collective-permute-start.16 = (bf16[512,512]{1,0:T(8,128)(2,1)}, bf16[512,512]{1,0:T(8,128)(2,1)S(1)}, u32[]{:S(2)}, u32[]{:S(2)}) collective-permute-start(bf16[512,512]{1,0:T(8,128)(2,1)} %collective-permute-done.14.refs_10_), channel_id=1, source_target_pairs={{0,4},{4,0},{8,12},{12,8},{16,20},{20,16},{24,28},{28,24},{32,36},... | collective-permute-start | bytes 1572872 | tf_op jit(solution)/shard_map/ppermute | solution.py:47
  101.6 6.5 %collective-permute-start.15 = (bf16[512,512]{1,0:T(8,128)(2,1)}, bf16[512,512]{1,0:T(8,128)(2,1)S(1)}, u32[]{:S(2)}, u32[]{:S(2)}) collective-permute-start(bf16[512,512]{1,0:T(8,128)(2,1)} %collective-permute-done.13.refs_9_), channel_id=1, source_target_pairs={{0,4},{4,0},{8,12},{12,8},{16,20},{20,16},{24,28},{28,24},{32,36},... | collective-permute-start | bytes 1572872 | tf_op jit(solution)/shard_map/ppermute | solution.py:47
  108.1 2.3 %collective-permute-start.18 = (bf16[512,512]{1,0:T(8,128)(2,1)}, bf16[512,512]{1,0:T(8,128)(2,1)}, u32[]{:S(2)}, u32[]{:S(2)}) collective-permute-start(bf16[512,512]{1,0:T(8,128)(2,1)} %collective-permute-done.17.refs_13_), channel_id=1, source_target_pairs={{0,4},{4,0},{8,12},{12,8},{16,20},{20,16},{24,28},{28,24},{32,36},... | collective-permute-start | bytes 1572872 | tf_op jit(solution)/shard_map/ppermute | solution.py:47
  108.1 2.2 %copy-start.10 = (bf16[512,512]{1,0:T(8,128)(2,1)}, bf16[512,512]{1,0:T(8,128)(2,1)S(1)}, u32[]{:S(2)}) copy-start(bf16[512,512]{1,0:T(8,128)(2,1)S(1)} %collective-permute-done.16.refs_12_) | copy-start | bytes 1572868
  120.7 21.6 %all-to-all-start = ((bf16[4,256,640]{2,1,0:T(8,128)(2,1)}), bf16[4,256,640]{2,1,0:T(8,128)(2,1)S(1)}, u32[]{:S(2)}, u32[]{:S(2)}) async-start(bf16[4,256,640]{2,1,0:T(8,128)(2,1)} %chosen_attention.3), calls=%async_computation | async-start | bytes 2621440 | tf_op jit(solution)/shard_map/all_to_all | solution.py:259
  126.9 9.4 %copy-start.5 = (f32[256,512]{1,0:T(8,128)S(1)}, f32[256,512]{1,0:T(8,128)}, u32[]{:S(2)}) copy-start(f32[256,512]{1,0:T(8,128)} %copy-done.4) | copy-start | bytes 1572868
  128.1 5.1 %collective-permute-start.3 = (f32[256,64]{1,0:T(8,128)S(1)}, f32[256,64]{1,0:T(8,128)S(1)}, u32[]{:S(2)}, u32[]{:S(2)}) collective-permute-start(f32[256,64]{1,0:T(8,128)S(1)} %gate_share.1), channel_id=1, source_target_pairs={{0,1},{1,0},{2,3},{3,2},{4,5},{5,4},{6,7},{7,6},{8,9},{9,8},{10,11... | collective-permute-start | bytes 196616 | tf_op jit(solution)/shard_map/ppermute | solution.py:254
  133.2 6.6 %collective-permute-start.4 = (f32[256,64]{1,0:T(8,128)S(1)}, f32[256,64]{1,0:T(8,128)S(1)}, u32[]{:S(2)}, u32[]{:S(2)}) collective-permute-start(f32[256,64]{1,0:T(8,128)S(1)} %add.233), channel_id=1, source_target_pairs={{0,2},{1,3},{2,0},{3,1},{4,6},{5,7},{6,4},{7,5},{8,10},{9,11},{10,... | collective-permute-start | bytes 196616 | tf_op jit(solution)/shard_map/ppermute | solution.py:254
  136.3 6.0 %copy-start.7 = (f32[256,512]{1,0:T(8,128)S(1)}, f32[256,512]{1,0:T(8,128)}, u32[]{:S(2)}) copy-start(f32[256,512]{1,0:T(8,128)} %copy-done.6) | copy-start | bytes 1572868
  (4 other events, 4.7 us)
Sparse Core Ops, SparseCore 0:
  9.8 72.5 all-gather.4
  84.9 39.3 all-gather.6

commit v5 on v4

--- a/solution.py
+++ b/solution.py
@@ -297,7 +297,7 @@
     mean = jnp.sum(keys, axis=0, dtype=jnp.float32).reshape(1, WIDTH) / ROWS
     means = jnp.concatenate([mean] + [climb(mean, d) for d in (1, 2, 3)], axis=0)
     means = jnp.concatenate(split(means) + [jnp.zeros((MEANS - 3 * NY, WIDTH), jnp.float32)], axis=0).astype(jnp.bfloat16)
-    ready = after(hops[2], own_lse, means, *sources)
+    ready = after(hops[2], own_lse, means, idx_first, *sources)
     same, cross = ring(ready[:2 * ROWS]), ring(ready[2 * ROWS:])
 
     means = lax.all_gather(after(means, gathered), "seq", axis_index_groups=PLANES)

time: 154 us -> 153 us (level)
  starting transfers between devices: 37.6 us -> 34.6 us
  waiting for transfers between devices: 58.6 us -> 61.3 us
    ppermute x17, starting transfers between devices: 23.3 us -> 20.3 us  [send(): return lax.ppermute(x, 'seq', pairs)]
    ppermute x17, waiting for transfers between devices: 45.8 us -> 48.5 us  [send(): return lax.ppermute(x, 'seq', pairs)]
  transfers between devices with their start and end apart: 23 -> 23, of which waited for: 11 -> 10; matrix products, arithmetic and copies ran while one was open for 5% -> 5% of each run, Pallas kernels for 17% -> 17%
where the time goes in v5:
time: 153 us; the launch traced here: 152 us
  waiting for transfers between devices  61.3 us (40%)
  starting transfers between devices  34.6 us (23%)
  Pallas kernels  29.1 us (19%)
  between operations  14.7 us (10%)
  local copies, waits for them, and re-layouts  8.53 us (6%)
  other arithmetic  3.64 us (2%)
    ppermute x17, waiting for transfers between devices, send(): return lax.ppermute(x, 'seq', pairs)  48.5 us
    pallas_call x2, Pallas kernels, chosen_attention(): call(functools.partial(chosen_kernel, half, blocks), 'chosen_attention',...  20.7 us
    ppermute x17, starting transfers between devices, send(): return lax.ppermute(x, 'seq', pairs)  20.3 us
    all_to_all x2, starting transfers between devices, back(): lax.all_to_all(out, 'seq', split_axis=0, concat_axis=0, tiled=True, axis_...  9.66 us
    all_gather x1, waiting for transfers between devices, body(): gathered = lax.all_gather(first, 'seq', axis_index_groups=PLANES)  6.22 us
    pallas_call x2, Pallas kernels, combine(): call(functools.partial(combine_kernel, half), 'combine', jax.ShapeDtypeSt...  5.18 us
    ppermute x2, waiting for transfers between devices, over_heads(): lax.ppermute(share, 'head', [(i, i ^ bits) for i in range(4)])  4.81 us
    ppermute x2, starting transfers between devices, over_heads(): lax.ppermute(share, 'head', [(i, i ^ bits) for i in range(4)])  4.62 us
  transfers between devices with their start and end apart: 23, of which 10 were waited for; matrix products, arithmetic and copies ran while one was open for 5% of the time, Pallas kernels for 17%

profile of v5, /device:TPU:8, one launch (start us, length us, event | category | flops | bytes accessed | tf_op | source)
XLA Modules:
  0.0 151.9 jit_solution(7736869337374424447)
XLA Ops:
  7.2 1.1 fusion.23
  8.4 0.8 pad_maximum_fusion.1
  9.5 1.9 %collective-permute-done.8 = bf16[512,512]{1,0:T(8,128)(2,1)S(1)} collective-permute-done((bf16[512,512]{1,0:T(8,128)(2,1)S(1)}, bf16[512,512]{1,0:T(8,128)(2,1)S(1)}, u32[]{:S(2)}, u32[]{:S(2)}) %collective-permute-start.8) | collective-permute-done | bytes 524320 | tf_op jit(solution)/shard_map/ppermute | solution.py:47
  11.5 2.0 %collective-permute-start.9 = (bf16[1024,512]{1,0:T(8,128)(2,1)S(1)}, bf16[1024,512]{1,0:T(8,128)(2,1)}, u32[]{:S(2)}, u32[]{:S(2)}) collective-permute-start(bf16[1024,512]{1,0:T(8,128)(2,1)S(1)} %pad_maximum_fusion.refs_4_), channel_id=1, source_target_pairs={{0,8},{4,60},{8,16},{12,4},{16,24},{20,12},{24,32},{28,20},{32,40}... | collective-permute-start | bytes 3145736 | tf_op jit(solution)/shard_map/ppermute | solution.py:47
  13.6 0.9 fusion.1.refs_0_
  14.4 1.5 collective-permute-start.7
  15.9 1.3 collective-permute-start.6
  17.2 2.2 %collective-permute-start.5 = (bf16[272,1024]{1,0:T(8,128)(2,1)}, bf16[272,1024]{1,0:T(8,128)(2,1)}, u32[]{:S(2)}, u32[]{:S(2)}) collective-permute-start(bf16[272,1024]{1,0:T(8,128)(2,1)} %fusion.1.refs_0_), channel_id=1, source_target_pairs={{64,0},{68,4},{72,8},{76,12},{80,16},{84,20},{88,24},{92,28},{96,3... | collective-permute-start | bytes 1671176 | tf_op jit(solution)/shard_map/ppermute | solution.py:47
  20.2 15.1 %collective-permute-done.9.refs_5_ = bf16[1024,512]{1,0:T(8,128)(2,1)} collective-permute-done((bf16[1024,512]{1,0:T(8,128)(2,1)S(1)}, bf16[1024,512]{1,0:T(8,128)(2,1)}, u32[]{:S(2)}, u32[]{:S(2)}) %collective-permute-start.9) | collective-permute-done | bytes 1048608 | tf_op jit(solution)/shard_map/ppermute | solution.py:47
  35.4 4.6 %collective-permute-start.1 = (f32[1,1024]{1,0:T(1,128)S(1)}, f32[1,1024]{1,0:T(1,128)S(1)}, u32[]{:S(2)}, u32[]{:S(2)}) collective-permute-start(f32[1,1024]{1,0:T(1,128)S(1)} %bitcast.26), channel_id=1, source_target_pairs={{0,128},{4,132},{8,136},{12,140},{16,144},{20,148},{24,152},{28,15... | collective-permute-start | bytes 12296 | tf_op jit(solution)/shard_map/ppermute | solution.py:47
  40.0 1.2 collective-permute-done.1
  41.2 4.8 %collective-permute-start = (f32[1,1024]{1,0:T(1,128)S(1)}, f32[1,1024]{1,0:T(1,128)S(1)}, u32[]{:S(2)}, u32[]{:S(2)}) collective-permute-start(f32[1,1024]{1,0:T(1,128)S(1)} %bitcast.27), channel_id=1, source_target_pairs={{0,64},{4,68},{8,72},{12,76},{16,80},{20,84},{24,88},{28,92},{32,9... | collective-permute-start | bytes 12296 | tf_op jit(solution)/shard_map/ppermute | solution.py:47
  46.0 2.0 %own_attention.1 = (f32[256,512]{1,0:T(8,128)S(1)}, f32[256,512]{1,0:T(8,128)S(1)}, f32[256,128]{1,0:T(8,128)S(1)}) custom-call(bf16[256,1024]{1,0:T(8,128)(2,1)S(1)} %copy-done.1, bf16[256,1024]{1,0:T(8,128)(2,1)S(1)} %copy-done, bf16[256,1024]{1,0:T(8,128)(2,1)S(1)} %copy-done.2), custom_call_target="tpu_custom_call" | custom-call | flops 1 | bytes 1 | tf_op jit(solution)/shard_map/own_attention/pallas_call | solution.py:212
  52.2 22.0 %collective-permute-done.11.refs_7_ = bf16[1024,512]{1,0:T(8,128)(2,1)} collective-permute-done((bf16[1024,512]{1,0:T(8,128)(2,1)}, bf16[1024,512]{1,0:T(8,128)(2,1)}, u32[]{:S(2)}, u32[]{:S(2)}) %collective-permute-start.11) | collective-permute-done | bytes 1048608 | tf_op jit(solution)/shard_map/ppermute | solution.py:47
  74.2 2.1 %fusion.21 = (bf16[512,512]{1,0:T(8,128)(2,1)}, bf16[512,512]{1,0:T(8,128)(2,1)S(1)}) fusion(bf16[1024,512]{1,0:T(8,128)(2,1)} %collective-permute-done.11.refs_7_), kind=kLoop, calls=%fused_computation.55 | loop fusion | bytes 2097152 | tf_op jit(solution)/shard_map/slice | solution.py:301
  76.2 6.2 %all-gather.5.cloned.1.call-done = bf16[8192,512]{1,0:T(8,128)(2,1)} async-done(((bf16[512,512]{1,0:T(8,128)(2,1)}), bf16[8192,512]{1,0:T(8,128)(2,1)}) %all-gather.5.cloned.1.call-update) | async-done | bytes 8388624 | tf_op jit(solution)/shard_map/all_gather | solution.py:275
  82.6 10.4 %chosen_attention.2 = bf16[4,256,640]{2,1,0:T(8,128)(2,1)} custom-call(s32[1]{0:T(128)} %bitcast.y_ref, s32[4,16]{1,0:T(4,128)} %get-tuple-element.55.idx_ref, bf16[272,1024]{1,0:T(8,128)(2,1)} %fusion.1.refs_0_, bf16[272,1024]{1,0:T(8,128)(2,1)} %collective-permute-done.5.refs_1_, bf16[272,1024]{1,0:T(8,128)(2,1)} %collective-permute-done.6.refs_2_, ...), custom_call_target="tpu_custom_call" | custom-call | flops 1 | bytes 1 | tf_op jit(solution)/shard_map/chosen_attention/pallas_call | solution.py:216
  93.0 2.5 %collective-permute-start.10 = (bf16[1024,512]{1,0:T(8,128)(2,1)}, bf16[1024,512]{1,0:T(8,128)(2,1)}, u32[]{:S(2)}, u32[]{:S(2)}) collective-permute-start(bf16[1024,512]{1,0:T(8,128)(2,1)} %collective-permute-done.9.refs_5_), channel_id=1, source_target_pairs={{0,4},{4,0},{8,12},{12,8},{16,20},{20,16},{24,28},{28,24},{32,36},... | collective-permute-start | bytes 3145736 | tf_op jit(solution)/shard_map/ppermute | solution.py:47
  95.6 4.8 %all-to-all-start.1 = ((bf16[4,256,640]{2,1,0:T(8,128)(2,1)}), bf16[4,256,640]{2,1,0:T(8,128)(2,1)S(1)}, u32[]{:S(2)}, u32[]{:S(2)}) async-start(bf16[4,256,640]{2,1,0:T(8,128)(2,1)} %chosen_attention.2), calls=%async_computation.1 | async-start | bytes 2621440 | tf_op jit(solution)/shard_map/all_to_all | solution.py:259
  101.0 6.9 %collective-permute-done.17.refs_13_ = bf16[512,512]{1,0:T(8,128)(2,1)} collective-permute-done((bf16[512,512]{1,0:T(8,128)(2,1)}, bf16[512,512]{1,0:T(8,128)(2,1)}, u32[]{:S(2)}, u32[]{:S(2)}) %collective-permute-start.17) | collective-permute-done | bytes 524320 | tf_op jit(solution)/shard_map/ppermute | solution.py:47
  108.7 1.4 collective-permute-done.18.refs_14_
  110.1 10.4 %chosen_attention.3 = bf16[4,256,640]{2,1,0:T(8,128)(2,1)} custom-call(s32[1]{0:T(128)} %bitcast.y_ref, s32[4,16]{1,0:T(4,128)} %get-tuple-element.30.idx_ref, bf16[272,1024]{1,0:T(8,128)(2,1)} %fusion.1.refs_0_, bf16[272,1024]{1,0:T(8,128)(2,1)} %collective-permute-done.5.refs_1_, bf16[272,1024]{1,0:T(8,128)(2,1)} %collective-permute-done.6.refs_2_, ...), custom_call_target="tpu_custom_call" | custom-call | flops 1 | bytes 1 | tf_op jit(solution)/shard_map/chosen_attention/pallas_call | solution.py:216
  120.5 4.8 %all-to-all-start = ((bf16[4,256,640]{2,1,0:T(8,128)(2,1)}), bf16[4,256,640]{2,1,0:T(8,128)(2,1)S(1)}, u32[]{:S(2)}, u32[]{:S(2)}) async-start(bf16[4,256,640]{2,1,0:T(8,128)(2,1)} %chosen_attention.3), calls=%async_computation | async-start | bytes 2621440 | tf_op jit(solution)/shard_map/all_to_all | solution.py:259
  125.5 1.2 copy-done.3
  126.7 1.2 gate_share.1
  127.9 1.6 %collective-permute-start.3 = (f32[256,64]{1,0:T(8,128)S(1)}, f32[256,64]{1,0:T(8,128)S(1)}, u32[]{:S(2)}, u32[]{:S(2)}) collective-permute-start(f32[256,64]{1,0:T(8,128)S(1)} %gate_share.1), channel_id=1, source_target_pairs={{0,1},{1,0},{2,3},{3,2},{4,5},{5,4},{6,7},{7,6},{8,9},{9,8},{10,11... | collective-permute-start | bytes 196616 | tf_op jit(solution)/shard_map/ppermute | solution.py:254
  129.5 3.5 %collective-permute-done.3 = f32[256,64]{1,0:T(8,128)S(1)} collective-permute-done((f32[256,64]{1,0:T(8,128)S(1)}, f32[256,64]{1,0:T(8,128)S(1)}, u32[]{:S(2)}, u32[]{:S(2)}) %collective-permute-start.3) | collective-permute-done | bytes 65568 | tf_op jit(solution)/shard_map/ppermute | solution.py:254
  133.0 3.1 %collective-permute-start.4 = (f32[256,64]{1,0:T(8,128)S(1)}, f32[256,64]{1,0:T(8,128)S(1)}, u32[]{:S(2)}, u32[]{:S(2)}) collective-permute-start(f32[256,64]{1,0:T(8,128)S(1)} %add.233), channel_id=1, source_target_pairs={{0,2},{1,3},{2,0},{3,1},{4,6},{5,7},{6,4},{7,5},{8,10},{9,11},{10,... | collective-permute-start | bytes 196616 | tf_op jit(solution)/shard_map/ppermute | solution.py:254
  136.1 2.2 %combine.2.refs_0_ = bf16[256,512]{1,0:T(8,128)(2,1)S(1)} custom-call(s32[1]{0:T(128)} %bitcast.y_ref, f32[256,512]{1,0:T(8,128)S(1)} %copy-done.5, f32[256,128]{1,0:T(8,128)S(1)} %get-tuple-element.29.lse_ref, bf16[4,256,640]{2,1,0:T(8,128)(2,1)S(1)} %all-to-all-done.1.pieces_ref), custom_call_target="tpu_custom_call" | custom-call | flops 1 | bytes 1 | tf_op jit(solution)/shard_map/combine/pallas_call | solution.py:234
  138.2 1.3 collective-permute-done.4
  140.3 1.8 %all-to-all-done.pieces_ref = bf16[4,256,640]{2,1,0:T(8,128)(2,1)S(1)} async-done(((bf16[4,256,640]{2,1,0:T(8,128)(2,1)}), bf16[4,256,640]{2,1,0:T(8,128)(2,1)S(1)}, u32[]{:S(2)}, u32[]{:S(2)}) %all-to-all-start) | async-done | bytes 1310752 | tf_op jit(solution)/shard_map/all_to_all | solution.py:259
  142.1 3.0 %combine.3 = bf16[256,1024]{1,0:T(8,128)(2,1)} custom-call(s32[1]{0:T(128)} %bitcast.y_ref, f32[256,512]{1,0:T(8,128)S(1)} %copy-done.7, f32[256,128]{1,0:T(8,128)S(1)} %get-tuple-element.29.lse_ref, bf16[4,256,640]{2,1,0:T(8,128)(2,1)S(1)} %all-to-all-done.pieces_ref, bf16[256,512]{1,0:T(8,128)(2,1)S(1)} %combine.2.refs_0_), custom_call_target="tpu_custom_call" | custom-call | flops 1 | bytes 1 | tf_op jit(solution)/shard_map/combine/pallas_call | solution.py:234
  (82 shorter events, 7.7 us)
Async XLA Ops:
  7.2 75.3 %all-gather.5.cloned.1.call-start = ((), (), s32[]{:S(2)}) async-start(), calls=%async_computation.2 | async-start | bytes 8912896 | tf_op jit(solution)/shard_map/all_gather | solution.py:275
  9.3 116.2 %all-gather.7.cloned.1.call-start = ((), (), s32[]{:S(2)}) async-start(), calls=%async_computation.3 | async-start | bytes 1114112 | tf_op jit(solution)/shard_map/all_gather | solution.py:303
  9.3 4.2 %copy-start.12 = (s32[8,3]{0,1:T(4,128)S(1)}, s32[8,3]{0,1:T(4,128)}, u32[]{:S(2)}) copy-start(s32[8,3]{0,1:T(4,128)} %param.9) | copy-start | bytes 292
  9.4 4.2 %copy-start.1 = (bf16[256,1024]{1,0:T(8,128)(2,1)S(1)}, bf16[256,1024]{1,0:T(8,128)(2,1)}, u32[]{:S(2)}) copy-start(bf16[256,1024]{1,0:T(8,128)(2,1)} %q_ref.3) | copy-start | bytes 1572868
  9.4 2.0 %collective-permute-start.8 = (bf16[512,512]{1,0:T(8,128)(2,1)S(1)}, bf16[512,512]{1,0:T(8,128)(2,1)S(1)}, u32[]{:S(2)}, u32[]{:S(2)}) collective-permute-start(bf16[512,512]{1,0:T(8,128)(2,1)S(1)} %pad_maximum_fusion.2), channel_id=1, source_target_pairs={{0,4},{4,0},{8,12},{12,8},{16,20},{20,16},{24,28},{28,24},{32,36},... | collective-permute-start | bytes 1572872 | tf_op jit(solution)/shard_map/ppermute | solution.py:47
  11.5 34.6 %copy-start.8 = (bf16[1024,512]{1,0:T(8,128)(2,1)}, bf16[1024,512]{1,0:T(8,128)(2,1)S(1)}, u32[]{:S(2)}) copy-start(bf16[1024,512]{1,0:T(8,128)(2,1)S(1)} %pad_maximum_fusion.refs_4_) | copy-start | bytes 3145732
  11.5 34.6 %copy-start.2 = (bf16[256,1024]{1,0:T(8,128)(2,1)S(1)}, bf16[256,1024]{1,0:T(8,128)(2,1)}, u32[]{:S(2)}) copy-start(bf16[256,1024]{1,0:T(8,128)(2,1)} %v_ref.1) | copy-start | bytes 1572868
  11.5 23.8 %collective-permute-start.9 = (bf16[1024,512]{1,0:T(8,128)(2,1)S(1)}, bf16[1024,512]{1,0:T(8,128)(2,1)}, u32[]{:S(2)}, u32[]{:S(2)}) collective-permute-start(bf16[1024,512]{1,0:T(8,128)(2,1)S(1)} %pad_maximum_fusion.refs_4_), channel_id=1, source_target_pairs={{0,8},{4,60},{8,16},{12,4},{16,24},{20,12},{24,32},{28,20},{32,40}... | collective-permute-start | bytes 3145736 | tf_op jit(solution)/shard_map/ppermute | solution.py:47
  14.4 34.7 %collective-permute-start.7 = (bf16[272,1024]{1,0:T(8,128)(2,1)}, bf16[272,1024]{1,0:T(8,128)(2,1)}, u32[]{:S(2)}, u32[]{:S(2)}) collective-permute-start(bf16[272,1024]{1,0:T(8,128)(2,1)} %fusion.1.refs_0_), channel_id=1, source_target_pairs={{192,0},{196,4},{200,8},{204,12},{208,16},{212,20},{216,24},{220,2... | collective-permute-start | bytes 1671176 | tf_op jit(solution)/shard_map/ppermute | solution.py:47
  15.9 34.0 %collective-permute-start.6 = (bf16[272,1024]{1,0:T(8,128)(2,1)}, bf16[272,1024]{1,0:T(8,128)(2,1)}, u32[]{:S(2)}, u32[]{:S(2)}) collective-permute-start(bf16[272,1024]{1,0:T(8,128)(2,1)} %fusion.1.refs_0_), channel_id=1, source_target_pairs={{128,0},{132,4},{136,8},{140,12},{144,16},{148,20},{152,24},{156,2... | collective-permute-start | bytes 1671176 | tf_op jit(solution)/shard_map/ppermute | solution.py:47
  17.2 33.4 %collective-permute-start.5 = (bf16[272,1024]{1,0:T(8,128)(2,1)}, bf16[272,1024]{1,0:T(8,128)(2,1)}, u32[]{:S(2)}, u32[]{:S(2)}) collective-permute-start(bf16[272,1024]{1,0:T(8,128)(2,1)} %fusion.1.refs_0_), channel_id=1, source_target_pairs={{64,0},{68,4},{72,8},{76,12},{80,16},{84,20},{88,24},{92,28},{96,3... | collective-permute-start | bytes 1671176 | tf_op jit(solution)/shard_map/ppermute | solution.py:47
  19.5 15.9 %collective-permute-start.2 = (f32[1,1024]{1,0:T(1,128)S(1)}, f32[1,1024]{1,0:T(1,128)S(1)}, u32[]{:S(2)}, u32[]{:S(2)}) collective-permute-start(f32[1,1024]{1,0:T(1,128)S(1)} %bitcast.25), channel_id=1, source_target_pairs={{0,192},{4,196},{8,200},{12,204},{16,208},{20,212},{24,216},{28,22... | collective-permute-start | bytes 12296 | tf_op jit(solution)/shard_map/ppermute | solution.py:47
  35.3 38.8 %collective-permute-start.11 = (bf16[1024,512]{1,0:T(8,128)(2,1)}, bf16[1024,512]{1,0:T(8,128)(2,1)}, u32[]{:S(2)}, u32[]{:S(2)}) collective-permute-start(bf16[1024,512]{1,0:T(8,128)(2,1)} %collective-permute-done.9.refs_5_), channel_id=1, source_target_pairs={{0,8},{4,60},{8,16},{12,4},{16,24},{20,12},{24,32},{28,20},{32,40}... | collective-permute-start | bytes 3145736 | tf_op jit(solution)/shard_map/ppermute | solution.py:47
  35.4 5.9 %collective-permute-start.1 = (f32[1,1024]{1,0:T(1,128)S(1)}, f32[1,1024]{1,0:T(1,128)S(1)}, u32[]{:S(2)}, u32[]{:S(2)}) collective-permute-start(f32[1,1024]{1,0:T(1,128)S(1)} %bitcast.26), channel_id=1, source_target_pairs={{0,128},{4,132},{8,136},{12,140},{16,144},{20,148},{24,152},{28,15... | collective-permute-start | bytes 12296 | tf_op jit(solution)/shard_map/ppermute | solution.py:47
  41.2 7.1 %collective-permute-start = (f32[1,1024]{1,0:T(1,128)S(1)}, f32[1,1024]{1,0:T(1,128)S(1)}, u32[]{:S(2)}, u32[]{:S(2)}) collective-permute-start(f32[1,1024]{1,0:T(1,128)S(1)} %bitcast.27), channel_id=1, source_target_pairs={{0,64},{4,68},{8,72},{12,76},{16,80},{20,84},{24,88},{28,92},{32,9... | collective-permute-start | bytes 12296 | tf_op jit(solution)/shard_map/ppermute | solution.py:47
  48.1 44.9 %copy-start.4 = (f32[256,512]{1,0:T(8,128)}, f32[256,512]{1,0:T(8,128)S(1)}, u32[]{:S(2)}) copy-start(f32[256,512]{1,0:T(8,128)S(1)} %get-tuple-element.37.own_ref) | copy-start | bytes 1572868
  48.1 44.9 %copy-start.6 = (f32[256,512]{1,0:T(8,128)}, f32[256,512]{1,0:T(8,128)S(1)}, u32[]{:S(2)}) copy-start(f32[256,512]{1,0:T(8,128)S(1)} %get-tuple-element.28.own_ref) | copy-start | bytes 1572868
  76.2 19.4 %collective-permute-start.13 = (bf16[512,512]{1,0:T(8,128)(2,1)S(1)}, bf16[512,512]{1,0:T(8,128)(2,1)}, u32[]{:S(2)}, u32[]{:S(2)}) collective-permute-start(bf16[512,512]{1,0:T(8,128)(2,1)S(1)} %get-tuple-element.47), channel_id=1, source_target_pairs={{0,8},{4,60},{8,16},{12,4},{16,24},{20,12},{24,32},{28,20},{32,40}... | collective-permute-start | bytes 1572872 | tf_op jit(solution)/shard_map/ppermute | solution.py:47
  82.5 17.9 %collective-permute-start.14 = (bf16[512,512]{1,0:T(8,128)(2,1)}, bf16[512,512]{1,0:T(8,128)(2,1)}, u32[]{:S(2)}, u32[]{:S(2)}) collective-permute-start(bf16[512,512]{1,0:T(8,128)(2,1)} %get-tuple-element.46), channel_id=1, source_target_pairs={{0,8},{4,60},{8,16},{12,4},{16,24},{20,12},{24,32},{28,20},{32,40}... | collective-permute-start | bytes 1572872 | tf_op jit(solution)/shard_map/ppermute | solution.py:47
  93.0 14.9 %collective-permute-start.10 = (bf16[1024,512]{1,0:T(8,128)(2,1)}, bf16[1024,512]{1,0:T(8,128)(2,1)}, u32[]{:S(2)}, u32[]{:S(2)}) collective-permute-start(bf16[1024,512]{1,0:T(8,128)(2,1)} %collective-permute-done.9.refs_5_), channel_id=1, source_target_pairs={{0,4},{4,0},{8,12},{12,8},{16,20},{20,16},{24,28},{28,24},{32,36},... | collective-permute-start | bytes 3145736 | tf_op jit(solution)/shard_map/ppermute | solution.py:47
  95.5 12.4 %collective-permute-start.12 = (bf16[1024,512]{1,0:T(8,128)(2,1)}, bf16[1024,512]{1,0:T(8,128)(2,1)S(1)}, u32[]{:S(2)}, u32[]{:S(2)}) collective-permute-start(bf16[1024,512]{1,0:T(8,128)(2,1)} %collective-permute-done.11.refs_7_), channel_id=1, source_target_pairs={{0,4},{4,0},{8,12},{12,8},{16,20},{20,16},{24,28},{28,24},{32,36},... | collective-permute-start | bytes 3145736 | tf_op jit(solution)/shard_map/ppermute | solution.py:47
  95.6 12.2 %collective-permute-start.17 = (bf16[512,512]{1,0:T(8,128)(2,1)}, bf16[512,512]{1,0:T(8,128)(2,1)}, u32[]{:S(2)}, u32[]{:S(2)}) collective-permute-start(bf16[512,512]{1,0:T(8,128)(2,1)} %collective-permute-done.13.refs_9_), channel_id=1, source_target_pairs={{0,8},{4,60},{8,16},{12,4},{16,24},{20,12},{24,32},{28,20},{32,40}... | collective-permute-start | bytes 1572872 | tf_op jit(solution)/shard_map/ppermute | solution.py:47
  95.6 24.9 %all-to-all-start.1 = ((bf16[4,256,640]{2,1,0:T(8,128)(2,1)}), bf16[4,256,640]{2,1,0:T(8,128)(2,1)S(1)}, u32[]{:S(2)}, u32[]{:S(2)}) async-start(bf16[4,256,640]{2,1,0:T(8,128)(2,1)} %chosen_attention.2), calls=%async_computation.1 | async-start | bytes 2621440 | tf_op jit(solution)/shard_map/all_to_all | solution.py:259
  100.4 7.4 %collective-permute-start.16 = (bf16[512,512]{1,0:T(8,128)(2,1)}, bf16[512,512]{1,0:T(8,128)(2,1)S(1)}, u32[]{:S(2)}, u32[]{:S(2)}) collective-permute-start(bf16[512,512]{1,0:T(8,128)(2,1)} %collective-permute-done.14.refs_10_), channel_id=1, source_target_pairs={{0,4},{4,0},{8,12},{12,8},{16,20},{20,16},{24,28},{28,24},{32,36},... | collective-permute-start | bytes 1572872 | tf_op jit(solution)/shard_map/ppermute | solution.py:47
  101.0 6.9 %collective-permute-start.15 = (bf16[512,512]{1,0:T(8,128)(2,1)}, bf16[512,512]{1,0:T(8,128)(2,1)S(1)}, u32[]{:S(2)}, u32[]{:S(2)}) collective-permute-start(bf16[512,512]{1,0:T(8,128)(2,1)} %collective-permute-done.13.refs_9_), channel_id=1, source_target_pairs={{0,4},{4,0},{8,12},{12,8},{16,20},{20,16},{24,28},{28,24},{32,36},... | collective-permute-start | bytes 1572872 | tf_op jit(solution)/shard_map/ppermute | solution.py:47
  107.8 2.3 %collective-permute-start.18 = (bf16[512,512]{1,0:T(8,128)(2,1)}, bf16[512,512]{1,0:T(8,128)(2,1)}, u32[]{:S(2)}, u32[]{:S(2)}) collective-permute-start(bf16[512,512]{1,0:T(8,128)(2,1)} %collective-permute-done.17.refs_13_), channel_id=1, source_target_pairs={{0,4},{4,0},{8,12},{12,8},{16,20},{20,16},{24,28},{28,24},{32,36},... | collective-permute-start | bytes 1572872 | tf_op jit(solution)/shard_map/ppermute | solution.py:47
  107.8 2.2 %copy-start.10 = (bf16[512,512]{1,0:T(8,128)(2,1)}, bf16[512,512]{1,0:T(8,128)(2,1)S(1)}, u32[]{:S(2)}) copy-start(bf16[512,512]{1,0:T(8,128)(2,1)S(1)} %collective-permute-done.16.refs_12_) | copy-start | bytes 1572868
  120.5 21.6 %all-to-all-start = ((bf16[4,256,640]{2,1,0:T(8,128)(2,1)}), bf16[4,256,640]{2,1,0:T(8,128)(2,1)S(1)}, u32[]{:S(2)}, u32[]{:S(2)}) async-start(bf16[4,256,640]{2,1,0:T(8,128)(2,1)} %chosen_attention.3), calls=%async_computation | async-start | bytes 2621440 | tf_op jit(solution)/shard_map/all_to_all | solution.py:259
  126.7 9.3 %copy-start.5 = (f32[256,512]{1,0:T(8,128)S(1)}, f32[256,512]{1,0:T(8,128)}, u32[]{:S(2)}) copy-start(f32[256,512]{1,0:T(8,128)} %copy-done.4) | copy-start | bytes 1572868
  127.9 5.1 %collective-permute-start.3 = (f32[256,64]{1,0:T(8,128)S(1)}, f32[256,64]{1,0:T(8,128)S(1)}, u32[]{:S(2)}, u32[]{:S(2)}) collective-permute-start(f32[256,64]{1,0:T(8,128)S(1)} %gate_share.1), channel_id=1, source_target_pairs={{0,1},{1,0},{2,3},{3,2},{4,5},{5,4},{6,7},{7,6},{8,9},{9,8},{10,11... | collective-permute-start | bytes 196616 | tf_op jit(solution)/shard_map/ppermute | solution.py:254
  133.0 6.6 %collective-permute-start.4 = (f32[256,64]{1,0:T(8,128)S(1)}, f32[256,64]{1,0:T(8,128)S(1)}, u32[]{:S(2)}, u32[]{:S(2)}) collective-permute-start(f32[256,64]{1,0:T(8,128)S(1)} %add.233), channel_id=1, source_target_pairs={{0,2},{1,3},{2,0},{3,1},{4,6},{5,7},{6,4},{7,5},{8,10},{9,11},{10,... | collective-permute-start | bytes 196616 | tf_op jit(solution)/shard_map/ppermute | solution.py:254
  136.1 6.0 %copy-start.7 = (f32[256,512]{1,0:T(8,128)S(1)}, f32[256,512]{1,0:T(8,128)}, u32[]{:S(2)}) copy-start(f32[256,512]{1,0:T(8,128)} %copy-done.6) | copy-start | bytes 1572868
  (4 other events, 4.7 us)
Sparse Core Ops, SparseCore 0:
  9.8 72.5 all-gather.4
  84.9 39.0 all-gather.6
